TPU v7x, 32 devices: a whole 2x2x4 slice. The times are simulated.
32 devices in a mesh: section: 2 (over y), rep: 4 (over z), shard: 4 (over x, core).
Axes of the slice: x: 2, y: 2, z: 4, core: 2. Of those that a mesh axis runs over, the one named last changes fastest.
Arguments:
- tokens: bfloat16 [3072, 2560], P(('rep', 'shard')), may hold values from -6 to 6
- segment_ids: int32 [32, 96], P(('rep', 'shard')), may hold values from 0 to 5, never falling along the last dimension, each value on 1 to 64 neighbouring positions
- input_gain: float32 [2, 2560], P('section'), may hold values from 0.25 to 1.75
- query_gain: float32 [2, 768], P('section'), may hold values from 0.25 to 1.75
- latent_gain: float32 [2, 256], P('section'), may hold values from 0.25 to 1.75
- post_gain: float32 [2, 2560], P('section'), may hold values from 0.25 to 1.75
- query_down: bfloat16 [2, 2560, 768], P('section', 'shard'), may hold values from -0.125 to 0.125
- query_up: bfloat16 [2, 768, 3840], P('section', 'shard'), may hold values from -0.21875 to 0.21875
- latent_down: bfloat16 [2, 2560, 288], P('section', 'shard'), may hold values from -0.125 to 0.125
- latent_up: bfloat16 [2, 256, 5120], P('section', 'shard'), may hold values from -0.375 to 0.375
- output_weight: bfloat16 [2, 2560, 2560], P('section', 'shard'), may hold values from -2 to 2
- gate_weight: bfloat16 [2, 2560, 6400], P('section', 'shard'), may hold values from -0.125 to 0.125
- up_weight: bfloat16 [2, 2560, 6400], P('section', 'shard'), may hold values from -0.125 to 0.125
- down_weight: bfloat16 [2, 6400, 2560], P('section', 'shard'), may hold values from -0.625 to 0.625
- cotangent: bfloat16 [3072, 2560], P(('rep', 'shard')), may hold values from -6 to 6
Outputs:
- boundary: bfloat16 [2, 3072, 2560], P('section', ('rep', 'shard'))
- input_grads: float32 [2, 3072, 2560], P('section', ('rep', 'shard'))
- grad_input_gain: float32 [2, 2560], P('section')
- grad_query_gain: float32 [2, 768], P('section')
- grad_latent_gain: float32 [2, 256], P('section')
- grad_post_gain: float32 [2, 2560], P('section')
- grad_query_down: float32 [2, 2560, 768], P('section', 'shard')
- grad_query_up: float32 [2, 768, 3840], P('section', 'shard')
- grad_latent_down: float32 [2, 2560, 288], P('section', 'shard')
- grad_latent_up: float32 [2, 256, 5120], P('section', 'shard')
- grad_output_weight: float32 [2, 2560, 2560], P('section', 'shard')
- grad_gate_weight: float32 [2, 2560, 6400], P('section', 'shard')
- grad_up_weight: float32 [2, 2560, 6400], P('section', 'shard')
- grad_down_weight: float32 [2, 6400, 2560], P('section', 'shard')
Inputs may be any that keep to these rules, and one draw needn't show every extreme that they name: `segment_ids`: each row holds the sequence numbers of the 96 packed positions of one slot; they never fall along a row, and each sequence spans 1 to 64 positions.
All inputs are finite; a program needn't handle non-finite values.
Results may differ from a plain program's by a relative error of at most 0.03.
Values may be sent and summed in bfloat16 or wider, within the bound.
A program may use at most 576 MiB of HBM per device.

v0:
```python
import math

import jax
import jax.numpy as jnp
from jax import lax
from jax.sharding import PartitionSpec as P

D = 2560
HEADS = 40
NOPE = 64
ROPE = 32
VDIM = 64
KVRANK = 256
SLOT = 96
MICRO = 2


epsilon = 1e-05
residual_scale = 1.4 / math.sqrt(62.0)
masked_score = -1e30


def passed_along(value, axis, steps):
    count = lax.axis_size(axis)
    leading, last = (max(0, -steps), min(count, count - steps))
    return lax.ppermute(value, axis, [(source, source + steps) for source in range(leading, last)])


def norm_scale(value):
    return lax.rsqrt(jnp.mean(value * value, axis=-1, keepdims=True) + epsilon)


def norm_back(value, scale, gain, grad):
    weighted = grad * gain
    inner = jnp.mean(value * weighted, axis=-1, keepdims=True)
    grad_value = scale * weighted - value * (scale * scale * scale) * inner
    return (grad_value, jnp.sum(grad * value * scale, axis=0))


def rotate(value, cosine, sine):
    half = value.shape[-1] // 2
    front = value[..., :half]
    back = value[..., half:]
    return jnp.concatenate([front * cosine - back * sine, back * cosine + front * sine], axis=-1)


def unrotate(grad, cosine, sine):
    half = grad.shape[-1] // 2
    front = grad[..., :half]
    back = grad[..., half:]
    return jnp.concatenate([front * cosine + back * sine, back * cosine - front * sine], axis=-1)


def slot_tables(segments):
    length = segments.shape[0]
    index = jnp.arange(length, dtype=jnp.int32)
    starts = jnp.concatenate(
        [jnp.ones((1,), dtype=jnp.bool_), segments[1:] != segments[:-1]], axis=0
    )
    first_index = lax.cummax(jnp.where(starts, index, 0), axis=0)
    position = (index - first_index).astype(jnp.float32)
    freq = jnp.exp(jnp.arange(ROPE // 2, dtype=jnp.float32) * (-2.0 * math.log(10000.0) / ROPE))
    angle = position[:, None] * freq
    allowed = (segments[:, None] == segments[None, :]) & (index[None, :] <= index[:, None])
    return (jnp.cos(angle), jnp.sin(angle), allowed)


def contract_rows(left, right):
    return lax.dot_general(
        left, right, (((0,), (0,)), ((), ())), preferred_element_type=jnp.float32
    )


def contract_cols(left, right):
    return lax.dot_general(
        left, right, (((1,), (1,)), ((), ())), preferred_element_type=jnp.float32
    )


def project(left, weight):
    return jnp.dot(left, weight, preferred_element_type=jnp.float32)


def layer_forward(hidden, tables, gains, weights):
    cosine, sine, allowed = tables
    input_gain, query_gain, latent_gain, post_gain = gains
    (
        query_down,
        query_up,
        latent_down,
        latent_up,
        output_weight,
        gate_weight,
        up_weight,
        down_weight,
    ) = weights
    count = hidden.shape[0]
    score_scale = 1.0 / math.sqrt(NOPE + ROPE)
    scale_in = norm_scale(hidden)
    normed = (hidden * scale_in * input_gain).astype(jnp.bfloat16)
    latent_q = project(normed, query_down)
    latent_kv = project(normed, latent_down)
    scale_q = norm_scale(latent_q)
    query_in = (latent_q * scale_q * query_gain).astype(jnp.bfloat16)
    latent = latent_kv[:, :KVRANK]
    scale_kv = norm_scale(latent)
    kv_in = (latent * scale_kv * latent_gain).astype(jnp.bfloat16)
    query = project(query_in, query_up).reshape(count, HEADS, NOPE + ROPE)
    keyval = project(kv_in, latent_up).reshape(count, HEADS, NOPE + VDIM)
    queries = jnp.concatenate(
        [query[..., :NOPE], rotate(query[..., NOPE:], cosine[:, None, :], sine[:, None, :])],
        axis=-1,
    ).astype(jnp.bfloat16)
    shared = rotate(latent_kv[:, KVRANK:], cosine, sine)
    keys = jnp.concatenate(
        [keyval[..., :NOPE], jnp.broadcast_to(shared[:, None, :], (count, HEADS, ROPE))], axis=-1
    ).astype(jnp.bfloat16)
    values = keyval[..., NOPE:].astype(jnp.bfloat16)
    raw_scores = jnp.einsum("shd,thd->hst", queries, keys, preferred_element_type=jnp.float32)
    scores = jnp.where(allowed, raw_scores * score_scale, masked_score)
    row_max = jnp.max(scores, axis=-1, keepdims=True)
    exp_terms = jnp.exp(scores - row_max)
    total = jnp.sum(exp_terms, axis=-1, keepdims=True)
    probs = exp_terms / total
    attended = jnp.einsum(
        "hst,thd->shd", probs.astype(jnp.bfloat16), values, preferred_element_type=jnp.float32
    )
    attended = attended.reshape(count, HEADS * VDIM).astype(jnp.bfloat16)
    mixed = hidden + residual_scale * project(attended, output_weight)
    scale_post = norm_scale(mixed)
    normed_two = (mixed * scale_post * post_gain).astype(jnp.bfloat16)
    gate = project(normed_two, gate_weight)
    up = project(normed_two, up_weight)
    activated = (jax.nn.silu(gate) * up).astype(jnp.bfloat16)
    output = mixed + residual_scale * project(activated, down_weight)
    kept = (
        hidden,
        scale_in,
        normed,
        latent_q,
        scale_q,
        query_in,
        latent_kv,
        scale_kv,
        kv_in,
        queries,
        keys,
        values,
        row_max + jnp.log(total),
        attended,
        mixed,
        scale_post,
        normed_two,
        gate,
        up,
        activated,
        cosine,
        sine,
        allowed,
    )
    return (output, kept)


def layer_backward(grad_out, kept, gains, weights):
    (
        hidden,
        scale_in,
        normed,
        latent_q,
        scale_q,
        query_in,
        latent_kv,
        scale_kv,
        kv_in,
        queries,
        keys,
        values,
        log_total,
        attended,
        mixed,
        scale_post,
        normed_two,
        gate,
        up,
        activated,
        cosine,
        sine,
        allowed,
    ) = kept
    input_gain, query_gain, latent_gain, post_gain = gains
    (
        query_down,
        query_up,
        latent_down,
        latent_up,
        output_weight,
        gate_weight,
        up_weight,
        down_weight,
    ) = weights
    count = hidden.shape[0]
    score_scale = 1.0 / math.sqrt(NOPE + ROPE)
    grad_down = (residual_scale * grad_out).astype(jnp.bfloat16)
    grad_act = contract_cols(grad_down, down_weight)
    sigmoid_gate = jax.nn.sigmoid(gate)
    grad_gate = (grad_act * up * sigmoid_gate * (1.0 + gate * (1.0 - sigmoid_gate))).astype(
        jnp.bfloat16
    )
    grad_up = (grad_act * gate * sigmoid_gate).astype(jnp.bfloat16)
    grad_normed_two = contract_cols(grad_gate, gate_weight) + contract_cols(grad_up, up_weight)
    grad_mixed_norm, dgain_post = norm_back(mixed, scale_post, post_gain, grad_normed_two)
    grad_mixed = grad_out + grad_mixed_norm
    grad_branch = (residual_scale * grad_mixed).astype(jnp.bfloat16)
    grad_attended = (
        contract_cols(grad_branch, output_weight).astype(jnp.bfloat16).reshape(count, HEADS, VDIM)
    )
    raw_scores = jnp.einsum("shd,thd->hst", queries, keys, preferred_element_type=jnp.float32)
    scores = jnp.where(allowed, raw_scores * score_scale, masked_score)
    probs = jnp.exp(scores - log_total)
    grad_values = jnp.einsum(
        "hst,shd->thd",
        probs.astype(jnp.bfloat16),
        grad_attended,
        preferred_element_type=jnp.float32,
    )
    grad_probs = jnp.einsum(
        "shd,thd->hst", grad_attended, values, preferred_element_type=jnp.float32
    )
    inner = jnp.sum(probs * grad_probs, axis=-1, keepdims=True)
    grad_scores = (probs * (grad_probs - inner) * score_scale).astype(jnp.bfloat16)
    grad_queries = jnp.einsum("hst,thd->shd", grad_scores, keys, preferred_element_type=jnp.float32)
    grad_keys = jnp.einsum("hst,shd->thd", grad_scores, queries, preferred_element_type=jnp.float32)
    grad_query = (
        jnp.concatenate(
            [
                grad_queries[..., :NOPE],
                unrotate(grad_queries[..., NOPE:], cosine[:, None, :], sine[:, None, :]),
            ],
            axis=-1,
        )
        .reshape(count, HEADS * (NOPE + ROPE))
        .astype(jnp.bfloat16)
    )
    grad_keyval = (
        jnp.concatenate([grad_keys[..., :NOPE], grad_values], axis=-1)
        .reshape(count, HEADS * (NOPE + VDIM))
        .astype(jnp.bfloat16)
    )
    grad_shared = unrotate(jnp.sum(grad_keys[..., NOPE:], axis=1), cosine, sine)
    grad_query_in = contract_cols(grad_query, query_up)
    grad_kv_in = contract_cols(grad_keyval, latent_up)
    grad_latent_q, dgain_query = norm_back(latent_q, scale_q, query_gain, grad_query_in)
    grad_latent, dgain_latent = norm_back(latent_kv[:, :KVRANK], scale_kv, latent_gain, grad_kv_in)
    grad_lq = grad_latent_q.astype(jnp.bfloat16)
    grad_lkv = jnp.concatenate([grad_latent, grad_shared], axis=-1).astype(jnp.bfloat16)
    grad_normed = contract_cols(grad_lq, query_down) + contract_cols(grad_lkv, latent_down)
    grad_hidden_norm, dgain_input = norm_back(hidden, scale_in, input_gain, grad_normed)
    grad_hidden = grad_mixed + grad_hidden_norm
    weight_pairs = (
        (normed, grad_lq),
        (query_in, grad_query),
        (normed, grad_lkv),
        (kv_in, grad_keyval),
        (attended, grad_branch),
        (normed_two, grad_gate),
        (normed_two, grad_up),
        (activated, grad_down),
    )
    gain_terms = (dgain_input, dgain_query, dgain_latent, dgain_post)
    return (grad_hidden, weight_pairs, gain_terms)


def body(
    tokens,
    segment_ids,
    input_gain,
    query_gain,
    latent_gain,
    post_gain,
    query_down,
    query_up,
    latent_down,
    latent_up,
    output_weight,
    gate_weight,
    up_weight,
    down_weight,
    cotangent,
):
    section = lax.axis_index("section")
    at_start = section == 0
    gains = (input_gain[0], query_gain[0], latent_gain[0], post_gain[0])
    own_weights = (
        query_down[0],
        query_up[0],
        latent_down[0],
        latent_up[0],
        output_weight[0],
        gate_weight[0],
        up_weight[0],
        down_weight[0],
    )
    weights = (
        lax.all_gather(own_weights[0], "shard", axis=0, tiled=True),
        lax.all_gather(own_weights[1], "shard", axis=0, tiled=True),
        lax.all_gather(own_weights[2], "shard", axis=0, tiled=True),
        lax.all_gather(own_weights[3], "shard", axis=0, tiled=True),
        lax.all_gather(own_weights[4], "shard", axis=0, tiled=True),
        lax.all_gather(own_weights[5], "shard", axis=0, tiled=True),
        lax.all_gather(own_weights[6], "shard", axis=0, tiled=True),
        lax.all_gather(own_weights[7], "shard", axis=0, tiled=True),
    )
    received = jnp.zeros((SLOT, D), jnp.bfloat16)
    kept_list = []
    leaving_list = []
    for tick in range(MICRO + 1):
        place = jnp.clip(tick - section, 0, MICRO - 1)
        own = lax.dynamic_slice_in_dim(tokens, place * SLOT, SLOT, 0)
        entering = jnp.where(at_start, own, received).astype(jnp.float32)
        tables = slot_tables(lax.dynamic_index_in_dim(segment_ids, place, 0, keepdims=False))
        leaving, kept = layer_forward(entering, tables, gains, weights)
        leaving = leaving.astype(jnp.bfloat16)
        kept_list.append(kept)
        leaving_list.append(leaving)
        if tick < MICRO:
            received = passed_along(leaving, "section", 1)
    returned = jnp.zeros((SLOT, D), jnp.bfloat16)
    grad_list = []
    pair_list = []
    gain_sums = ()
    for tick in range(MICRO + 1):
        micro = tick - 1 + section
        valid = (micro >= 0) & (micro < MICRO)
        place = jnp.clip(micro, 0, MICRO - 1)
        own = lax.dynamic_slice_in_dim(cotangent, place * SLOT, SLOT, 0).astype(jnp.float32)
        incoming = jnp.where(at_start, returned.astype(jnp.float32), jnp.where(valid, own, 0.0))
        kept = jax.tree.map(
            lambda early, late: jnp.where(at_start, early, late),
            kept_list[max(tick - 1, 0)],
            kept_list[min(tick + 1, MICRO)],
        )
        grad_hidden, weight_pairs, gain_terms = layer_backward(incoming, kept, gains, weights)
        if tick == 0:
            gain_sums = gain_terms
        else:
            gain_sums = jax.tree.map(lambda total, term: total + term, gain_sums, gain_terms)
        pair_list.append(weight_pairs)
        grad_list.append(grad_hidden)
        if tick < MICRO:
            returned = passed_along(grad_hidden.astype(jnp.bfloat16), "section", -1)
    chosen = [
        jax.tree.map(
            lambda early, late: jnp.where(at_start, early, late),
            pair_list[index + 1],
            pair_list[index],
        )
        for index in range(MICRO)
    ]
    owned = []
    for weight_index in range(8):
        left_all = jnp.concatenate(
            [chosen[index][weight_index][0] for index in range(MICRO)], axis=0
        )
        grad_all = jnp.concatenate(
            [chosen[index][weight_index][1] for index in range(MICRO)], axis=0
        )
        owned.append(
            lax.psum_scatter(
                contract_rows(left_all, grad_all).astype(jnp.bfloat16),
                "shard",
                scatter_dimension=0,
                tiled=True,
            ).astype(jnp.float32)
        )
    weight_totals = (
        lax.psum(owned[0].astype(jnp.bfloat16), "rep").astype(jnp.float32),
        lax.psum(owned[1].astype(jnp.bfloat16), "rep").astype(jnp.float32),
        lax.psum(owned[2].astype(jnp.bfloat16), "rep").astype(jnp.float32),
        lax.psum(owned[3].astype(jnp.bfloat16), "rep").astype(jnp.float32),
        lax.psum(owned[4].astype(jnp.bfloat16), "rep").astype(jnp.float32),
        lax.psum(owned[5].astype(jnp.bfloat16), "rep").astype(jnp.float32),
        lax.psum(owned[6].astype(jnp.bfloat16), "rep").astype(jnp.float32),
        lax.psum(owned[7].astype(jnp.bfloat16), "rep").astype(jnp.float32),
    )
    gain_totals = lax.psum(
        (gain_sums[0], gain_sums[1], gain_sums[2], gain_sums[3]), ("rep", "shard")
    )
    boundary = jnp.concatenate(
        [
            jnp.where(at_start, leaving_list[index], leaving_list[index + 1])
            for index in range(MICRO)
        ],
        axis=0,
    )
    input_grads = jnp.concatenate(
        [jnp.where(at_start, grad_list[index + 1], grad_list[index]) for index in range(MICRO)],
        axis=0,
    )
    return (
        boundary[None],
        input_grads[None],
        gain_totals[0][None],
        gain_totals[1][None],
        gain_totals[2][None],
        gain_totals[3][None],
        weight_totals[0][None],
        weight_totals[1][None],
        weight_totals[2][None],
        weight_totals[3][None],
        weight_totals[4][None],
        weight_totals[5][None],
        weight_totals[6][None],
        weight_totals[7][None],
    )


def solution(mesh):
    placed = (
        P(("rep", "shard"), None),
        P(("rep", "shard"), None),
        P("section", None),
        P("section", None),
        P("section", None),
        P("section", None),
        P("section", "shard", None),
        P("section", "shard", None),
        P("section", "shard", None),
        P("section", "shard", None),
        P("section", "shard", None),
        P("section", "shard", None),
        P("section", "shard", None),
        P("section", "shard", None),
        P(("rep", "shard"), None),
    )
    return jax.shard_map(
        body,
        mesh=mesh,
        in_specs=placed,
        out_specs=(
            P("section", ("rep", "shard"), None),
            P("section", ("rep", "shard"), None),
            P("section", None),
            P("section", None),
            P("section", None),
            P("section", None),
            P("section", "shard", None),
            P("section", "shard", None),
            P("section", "shard", None),
            P("section", "shard", None),
            P("section", "shard", None),
            P("section", "shard", None),
            P("section", "shard", None),
            P("section", "shard", None),
        ),
        check_vma=False,
    )
```

profile of v0, /device:TPU:1, one launch (start us, length us, event | category | flops | bytes accessed | tf_op | source)
XLA Modules:
  0.0 3423.7 jit_solution(43395609753984907)
XLA Ops:
  34.5 23.8 all-gather.19.cloned.1.call-done
  63.6 29.4 all-gather.21.cloned.1.call-done
  96.0 42.5 %all-gather.23.cloned.1.call-done = bf16[1,768,3840]{2,1,0:T(8,128)(2,1)} async-done(((bf16[1,192,3840]{2,1,0:T(8,128)(2,1)}), bf16[1,768,3840]{2,1,0:T(8,128)(2,1)}) %all-gather.23.cloned.1.call-update) | async-done | bytes 5898256 | tf_op jit(solution)/shard_map/all_gather | solution.py:305
  153.3 71.8 %all-gather.25.cloned.1.call-done = bf16[1,2560,2560]{2,1,0:T(8,128)(2,1)} async-done(((bf16[1,640,2560]{2,1,0:T(8,128)(2,1)}), bf16[1,2560,2560]{2,1,0:T(8,128)(2,1)}) %all-gather.25.cloned.1.call-update) | async-done | bytes 13107216 | tf_op jit(solution)/shard_map/all_gather | solution.py:308
  232.3 191.4 %all-gather.27.cloned.1.call-done = bf16[1,2560,6400]{2,1,0:T(8,128)(2,1)} async-done(((bf16[1,640,6400]{2,1,0:T(8,128)(2,1)}), bf16[1,2560,6400]{2,1,0:T(8,128)(2,1)}) %all-gather.27.cloned.1.call-update) | async-done | bytes 32768016 | tf_op jit(solution)/shard_map/all_gather | solution.py:309
  423.6 18.1 fusion.37
  441.8 180.5 %all-gather.29.cloned.1.call-done = bf16[1,2560,6400]{2,1,0:T(8,128)(2,1)} async-done(((bf16[1,640,6400]{2,1,0:T(8,128)(2,1)}), bf16[1,2560,6400]{2,1,0:T(8,128)(2,1)}) %all-gather.29.cloned.1.call-update) | async-done | bytes 32768016 | tf_op jit(solution)/shard_map/all_gather | solution.py:310
  622.3 21.7 multiply_convert_fusion.8
  643.9 177.0 %all-gather.31.cloned.1.call-done = bf16[1,6400,2560]{2,1,0:T(8,128)(2,1)} async-done(((bf16[1,1600,2560]{2,1,0:T(8,128)(2,1)}), bf16[1,6400,2560]{2,1,0:T(8,128)(2,1)}) %all-gather.31.cloned.1.call-update) | async-done | bytes 32768016 | tf_op jit(solution)/shard_map/all_gather | solution.py:311
  888.8 17.5 fusion.35
  921.1 19.0 multiply_convert_fusion.5
  956.6 17.8 multiply_reduce_fusion.5
  1134.8 18.6 broadcast_select_fusion.6
  1169.9 17.5 multiply_reduce_fusion.4
  1254.7 21.0 broadcast_select_fusion.5
  1292.1 17.2 multiply_reduce_fusion.3
  1449.1 16.6 reduce-scatter.17.cloned.1.call-done
  1465.7 59.0 %reduce-scatter.19.cloned.1.call-done = bf16[192,3840]{1,0:T(8,128)(2,1)} async-done(((bf16[768,3840]{1,0:T(8,128)(2,1)}), bf16[192,3840]{1,0:T(8,128)(2,1)}) %reduce-scatter.19.cloned.1.call-update) | async-done | bytes 1474576 | tf_op jit(solution)/shard_map/reduce_scatter | solution.py:368
  1524.7 105.7 %reduce-scatter.23.cloned.1.call-done = bf16[640,2560]{1,0:T(8,128)(2,1)} async-done(((bf16[2560,2560]{1,0:T(8,128)(2,1)}), bf16[640,2560]{1,0:T(8,128)(2,1)}) %reduce-scatter.23.cloned.1.call-update) | async-done | bytes 3276816 | tf_op jit(solution)/shard_map/reduce_scatter | solution.py:368
  1630.4 232.6 %reduce-scatter.31.cloned.1.call-done = bf16[1600,2560]{1,0:T(8,128)(2,1)} async-done(((bf16[6400,2560]{1,0:T(8,128)(2,1)}), bf16[1600,2560]{1,0:T(8,128)(2,1)}) %reduce-scatter.31.cloned.1.call-update) | async-done | bytes 8192016
  1863.0 232.8 %reduce-scatter.29.cloned.1.call-done = bf16[640,6400]{1,0:T(8,128)(2,1)} async-done(((bf16[2560,6400]{1,0:T(8,128)(2,1)}), bf16[640,6400]{1,0:T(8,128)(2,1)}) %reduce-scatter.29.cloned.1.call-update) | async-done | bytes 8192016
  2095.8 232.6 %reduce-scatter.27.cloned.1.call-done = bf16[640,6400]{1,0:T(8,128)(2,1)} async-done(((bf16[2560,6400]{1,0:T(8,128)(2,1)}), bf16[640,6400]{1,0:T(8,128)(2,1)}) %reduce-scatter.27.cloned.1.call-update) | async-done | bytes 8192016
  2335.3 66.2 %all-reduce.3 = (f32[1,2560]{1,0:T(1,128)}, f32[1,768]{1,0:T(1,128)}, f32[1,256]{1,0:T(1,128)}, f32[1,2560]{1,0:T(1,128)}) all-reduce(f32[1,2560]{1,0:T(1,128)S(1)} %broadcast_in_dim.198, f32[1,768]{1,0:T(1,128)S(1)} %broadcast_in_dim.199, ...), channel_id=1, replica_groups=mesh['section'=2,'rep'=4,'shard'=4] {'rep','shard'}, use_global_device_ids=true, to_apply=%region_42.43 | all-reduce | flops 6144 | bytes 49152 | tf_op jit(solution)/shard_map/psum | solution.py:385
  2419.7 956.4 %all-reduce.7.cloned.1.call-done = (bf16[1,640,768]{2,1,0:T(8,128)(2,1)}, bf16[1,192,3840]{2,1,0:T(8,128)(2,1)}, bf16[1,640,288]{1,2,0:T(8,128)(2,1)}, bf16[1,64...) async-done(((bf16[1,640,768]{2,1,0:T(8,128)(2,1)}, ...) | async-done | bytes 31334416 | tf_op jit(solution)/shard_map/psum | solution.py:376
  (908 shorter events, 619.4 us)
Async XLA Ops:
  7.2 24.0 all-gather.17.cloned.1.call-start
  7.9 50.4 %all-gather.19.cloned.1.call-start = ((), (), s32[]{:S(2)}) async-start(), calls=%async_computation.13 | async-start | bytes 3276800 | tf_op jit(solution)/shard_map/all_gather | solution.py:307
  8.7 84.3 %all-gather.21.cloned.1.call-start = ((), (), s32[]{:S(2)}) async-start(), calls=%async_computation.14 | async-start | bytes 4915200 | tf_op jit(solution)/shard_map/all_gather | solution.py:304
  9.4 129.2 %all-gather.23.cloned.1.call-start = ((), (), s32[]{:S(2)}) async-start(), calls=%async_computation.15 | async-start | bytes 7372800 | tf_op jit(solution)/shard_map/all_gather | solution.py:305
  10.0 215.1 %all-gather.25.cloned.1.call-start = ((), (), s32[]{:S(2)}) async-start(), calls=%async_computation.16 | async-start | bytes 16384000 | tf_op jit(solution)/shard_map/all_gather | solution.py:308
  10.6 413.1 %all-gather.27.cloned.1.call-start = ((), (), s32[]{:S(2)}) async-start(), calls=%async_computation.17 | async-start | bytes 40960000 | tf_op jit(solution)/shard_map/all_gather | solution.py:309
  11.1 611.1 %all-gather.29.cloned.1.call-start = ((), (), s32[]{:S(2)}) async-start(), calls=%async_computation.18 | async-start | bytes 40960000 | tf_op jit(solution)/shard_map/all_gather | solution.py:310
  11.9 809.0 %all-gather.31.cloned.1.call-start = ((), (), s32[]{:S(2)}) async-start(), calls=%async_computation.19 | async-start | bytes 40960000 | tf_op jit(solution)/shard_map/all_gather | solution.py:311
  12.7 1434.5 %reduce-scatter.25.cloned.1.call-start = ((), (), s32[]{:S(2)}) async-start(), calls=%async_computation.20 | async-start | bytes 2457600
  12.8 1230.2 %copy-start.147 = (f32[2560]{0:T(1024)}, f32[2560]{0:T(1024)S(1)}, u32[]{:S(2)}) copy-start(f32[2560]{0:T(1024)S(1)} %reduce) | copy-start | bytes 30724
  14.2 852.4 %copy-start.222 = (f32[96]{0:T(128)}, f32[96]{0:T(128)S(1)}, u32[]{:S(2)}) copy-start(f32[96]{0:T(128)S(1)} %subtract_convert_fusion.16) | copy-start | bytes 1156
  96.0 756.8 %copy-start.262 = (f32[96]{0:T(128)}, f32[96]{0:T(128)S(1)}, u32[]{:S(2)}) copy-start(f32[96]{0:T(128)S(1)} %get-tuple-element.224) | copy-start | bytes 1156
  835.0 13.8 collective-permute-start
  1044.2 12.8 collective-permute-start.1
  1098.4 35.2 %collective-permute-start.2 = (bf16[96,2560]{1,0:T(8,128)(2,1)}, bf16[96,2560]{1,0:T(8,128)(2,1)S(1)}, u32[]{:S(2)}, u32[]{:S(2)}) collective-permute-start(bf16[96,2560]{1,0:T(8,128)(2,1)} %get-tuple-element.100), channel_id=1, source_target_pairs={{16,0},{17,1},{18,2},{19,3},{20,4},{21,5},{22,6},{23,7},{24,8},{25... | collective-permute-start | bytes 1474568 | tf_op jit(solution)/shard_map/ppermute | solution.py:26
  1241.2 13.4 collective-permute-start.3
  1349.8 99.4 %reduce-scatter.21.cloned.1.call-start = ((), (), s32[]{:S(2)}) async-start(), calls=%async_computation.10 | async-start | bytes 3276800 | tf_op jit(solution)/shard_map/reduce_scatter | solution.py:368
  1356.1 109.6 %reduce-scatter.17.cloned.1.call-start = ((), (), s32[]{:S(2)}) async-start(), calls=%async_computation.8 | async-start | bytes 4915200 | tf_op jit(solution)/shard_map/reduce_scatter | solution.py:368
  1377.3 147.4 %reduce-scatter.19.cloned.1.call-start = ((), (), s32[]{:S(2)}) async-start(), calls=%async_computation.9 | async-start | bytes 7372800 | tf_op jit(solution)/shard_map/reduce_scatter | solution.py:368
  1385.5 244.9 %reduce-scatter.23.cloned.1.call-start = ((), (), s32[]{:S(2)}) async-start(), calls=%async_computation.11 | async-start | bytes 16384000 | tf_op jit(solution)/shard_map/reduce_scatter | solution.py:368
  1396.3 466.7 %reduce-scatter.31.cloned.1.call-start = ((), (), s32[]{:S(2)}) async-start(), calls=%async_computation.23 | async-start | bytes 40960000
  1413.8 682.0 %reduce-scatter.29.cloned.1.call-start = ((), (), s32[]{:S(2)}) async-start(), calls=%async_computation.22 | async-start | bytes 40960000
  1431.5 897.0 %reduce-scatter.27.cloned.1.call-start = ((), (), s32[]{:S(2)}) async-start(), calls=%async_computation.21 | async-start | bytes 40960000
  1447.1 1929.0 %all-reduce.7.cloned.1.call-start = ((), (), s32[]{:S(2)}) async-start(), calls=%async_computation.24 | async-start | bytes 62668800 | tf_op jit(solution)/shard_map/psum | solution.py:376
  (296 other events, 5397.9 us)
Sparse Core Ops, SparseCore 0:
  9.6 21.5 all-gather.16
  32.7 25.5 all-gather.18
  59.9 32.9 all-gather.20
  94.4 44.1 all-gather.22
  140.0 85.0 all-gather.24
  226.5 197.0 all-gather.26
  425.2 197.0 all-gather.28
  623.9 197.0 all-gather.30
  1349.9 31.9 reduce-scatter.24
  1385.0 34.6 reduce-scatter.20
  1422.8 42.8 reduce-scatter.16
  1468.9 55.7 reduce-scatter.18
  1527.8 102.5 reduce-scatter.22
  1632.9 230.0 reduce-scatter.30
  1865.7 230.1 reduce-scatter.28
  2098.3 230.1 reduce-scatter.26
  2332.8 1043.2 all-reduce.6
where the time goes:
time: 3430 us; the launch traced here: 3420 us
  waiting for transfers between devices  2590 us (76%)
  matrix products  536 us (16%)
  other arithmetic  107 us (3%)
  local copies, waits for them, and re-layouts  92.1 us (3%)
  blocking collectives  66.2 us (2%)
    psum x1, waiting for transfers between devices, body(): lax.psum(owned[0].astype(jnp.bfloat16), 'rep').astype(jnp.float32)  956 us
    unnamed x21, waiting for transfers between devices  703 us
    dot_general x24, matrix products, contract_cols(): lax.dot_general(left, right, (((1,), (1,)), ((), ())), preferred_element_...  220 us
    all_gather x1, waiting for transfers between devices, body(): lax.all_gather(own_weights[5], 'shard', axis=0, tiled=True)  191 us
    dot_general x24, matrix products, project(): return jnp.dot(left, weight, preferred_element_type=jnp.float32)  182 us
    reduce_scatter x4, waiting for transfers between devices, body(): lax.psum_scatter(contract_rows(left_all, grad_all).astype(jnp.bfloat16),...  181 us
    all_gather x1, waiting for transfers between devices, body(): lax.all_gather(own_weights[6], 'shard', axis=0, tiled=True)  181 us
    all_gather x1, waiting for transfers between devices, body(): lax.all_gather(own_weights[7], 'shard', axis=0, tiled=True)  177 us
  transfers between devices with their start and end apart: 21, of which 18 were waited for; matrix products, arithmetic and copies ran while one was open for 7% of the time, Pallas kernels for 0%

commit v1 on v0

v1 whole, which is shorter than its diff:
```python
import functools
import math

import jax
import jax.numpy as jnp
from jax import lax
from jax.experimental import pallas as pl
from jax.experimental.pallas import tpu as pltpu
from jax.sharding import PartitionSpec as P

D = 2560
HEADS = 40
NOPE = 64
ROPE = 32
VDIM = 64
QRANK = 768
KVRANK = 256
SLOT = 96
LANES = 128

epsilon = 1e-05
residual_scale = 1.4 / math.sqrt(62.0)
masked_score = -1e30
score_scale = 1.0 / math.sqrt(NOPE + ROPE)
bf16 = jnp.bfloat16
f32 = jnp.float32


def norm_scale(value):
    return lax.rsqrt(jnp.mean(value * value, axis=-1, keepdims=True) + epsilon)


def norm_back(value, scale, gain, grad):
    weighted = grad * gain
    inner = jnp.mean(value * weighted, axis=-1, keepdims=True)
    grad_value = scale * weighted - value * (scale * scale * scale) * inner
    return (grad_value, jnp.sum(grad * value * scale, axis=0))


def rotate(value, cosine, sine):
    half = value.shape[-1] // 2
    front = value[..., :half]
    back = value[..., half:]
    return jnp.concatenate([front * cosine - back * sine, back * cosine + front * sine], axis=-1)


def slot_tables(segments):
    index = jnp.arange(SLOT, dtype=jnp.int32)
    first = jnp.ones(segments.shape[:1] + (1,), dtype=jnp.bool_)
    starts = jnp.concatenate([first, segments[:, 1:] != segments[:, :-1]], axis=1)
    first_index = lax.cummax(jnp.where(starts, index, 0), axis=1)
    position = (index - first_index).astype(f32)
    freq = jnp.exp(jnp.arange(ROPE // 2, dtype=f32) * (-2.0 * math.log(10000.0) / ROPE))
    angle = position[..., None] * freq
    return (jnp.cos(angle), jnp.sin(angle))


def head_tables(segments):
    cosine, sine = slot_tables(segments)
    slots = segments.shape[0]
    ones = jnp.ones((slots, SLOT, NOPE), f32)
    tail = jnp.zeros((slots, SLOT, LANES - NOPE - ROPE), f32)
    half = jnp.zeros_like(sine)
    keep = jnp.concatenate([ones, cosine, cosine, tail], axis=-1)
    left = jnp.concatenate([0.0 * ones, -sine, half, tail], axis=-1)
    right = jnp.concatenate([0.0 * ones, half, sine, tail], axis=-1)
    index = jnp.arange(SLOT, dtype=jnp.int32)
    allowed = (segments[:, :, None] == segments[:, None, :]) & (index[None, :] <= index[:, None])
    mask = jnp.where(allowed, 0.0, masked_score).astype(f32)
    flat = lambda table: table.reshape(slots * SLOT, LANES)
    return (flat(keep), flat(left), flat(right), mask)


def contract_rows(left, right):
    return lax.dot_general(left, right, (((0,), (0,)), ((), ())), preferred_element_type=f32)


def contract_cols(left, right):
    return lax.dot_general(left, right, (((1,), (1,)), ((), ())), preferred_element_type=f32)


def project(left, weight):
    return jnp.dot(left, weight, preferred_element_type=f32)


def low_lanes():
    return lax.broadcasted_iota(jnp.int32, (SLOT, LANES), 1) < NOPE


def attend_kernel(heads, q_ref, kv_ref, sh_ref, keep_ref, left_ref, right_ref, mask_ref,
                  att_ref, qo_ref, kvo_ref):
    low = low_lanes()
    shared = sh_ref[...].astype(f32)
    keep, left, right = keep_ref[...], left_ref[...], right_ref[...]
    mask = mask_ref[0]
    held = None
    for head in range(heads):
        lanes = slice(head * LANES, (head + 1) * LANES)
        q = q_ref[:, lanes]
        q = q * keep + pltpu.roll(q, LANES - 16, 1) * left + pltpu.roll(q, 16, 1) * right
        q = q.astype(bf16)
        qo_ref[:, lanes] = q
        kv = kv_ref[:, lanes]
        kvb = kv.astype(bf16)
        kvo_ref[:, lanes] = kvb
        k = jnp.where(low, kv, shared).astype(bf16)
        scores = contract_cols(q, k) * score_scale + mask
        top = jnp.max(scores, axis=-1, keepdims=True)
        terms = jnp.exp(scores - top)
        probs = terms / jnp.sum(terms, axis=-1, keepdims=True)
        out = project(probs.astype(bf16), kvb)
        if head % 2 == 0:
            held = pltpu.roll(out, NOPE, 1)
            if head == heads - 1:
                att_ref[:, head * VDIM:(head + 1) * VDIM] = held[:, :VDIM].astype(bf16)
        else:
            att_ref[:, (head - 1) * VDIM:(head + 1) * VDIM] = jnp.where(low, held, out).astype(bf16)


def attend(query, keyval, shared, tables):
    tokens = query.shape[0]
    heads = query.shape[1] // LANES
    wide = pl.BlockSpec((SLOT, heads * LANES), lambda s: (s, 0))
    one = pl.BlockSpec((SLOT, LANES), lambda s: (s, 0))
    return pl.pallas_call(
        functools.partial(attend_kernel, heads),
        grid=(tokens // SLOT,),
        in_specs=[wide, wide, one, one, one, one, pl.BlockSpec((1, SLOT, SLOT), lambda s: (s, 0, 0))],
        out_specs=[pl.BlockSpec((SLOT, heads * VDIM), lambda s: (s, 0)), wide, wide],
        out_shape=[
            jax.ShapeDtypeStruct((tokens, heads * VDIM), bf16),
            jax.ShapeDtypeStruct(query.shape, bf16),
            jax.ShapeDtypeStruct(keyval.shape, bf16),
        ],
        name="attend",
    )(query, keyval, shared, *tables)


def attend_back_kernel(heads, q_ref, kv_ref, sh_ref, keep_ref, left_ref, right_ref, mask_ref,
                       ga_ref, gq_ref, gkv_ref, gsh_ref):
    low = low_lanes()
    shared = sh_ref[...].astype(f32)
    keep, left, right = keep_ref[...], left_ref[...], right_ref[...]
    mask = mask_ref[0]
    total = jnp.zeros((SLOT, LANES), f32)
    for head in range(heads):
        lanes = slice(head * LANES, (head + 1) * LANES)
        q = q_ref[:, lanes]
        kvb = kv_ref[:, lanes]
        k = jnp.where(low, kvb.astype(f32), shared).astype(bf16)
        scores = contract_cols(q, k) * score_scale + mask
        top = jnp.max(scores, axis=-1, keepdims=True)
        terms = jnp.exp(scores - top)
        probs = terms / jnp.sum(terms, axis=-1, keepdims=True)
        if head % 2 == 0 and head == heads - 1:
            ga = ga_ref[:, head * VDIM:(head + 1) * VDIM].astype(f32)
            ga = jnp.concatenate([jnp.zeros_like(ga), ga], axis=1)
        else:
            start = (head // 2) * LANES
            ga = ga_ref[:, start:start + LANES].astype(f32)
            if head % 2 == 0:
                ga = pltpu.roll(ga, NOPE, 1)
            ga = jnp.where(low, 0.0, ga)
        ga = ga.astype(bf16)
        grad_values = contract_rows(probs.astype(bf16), ga)
        grad_probs = contract_cols(ga, kvb)
        inner = jnp.sum(probs * grad_probs, axis=-1, keepdims=True)
        grad_scores = (probs * (grad_probs - inner) * score_scale).astype(bf16)
        gq = project(grad_scores, k)
        gq = gq * keep - pltpu.roll(gq, LANES - 16, 1) * left - pltpu.roll(gq, 16, 1) * right
        gq_ref[:, lanes] = gq.astype(bf16)
        gk = contract_rows(grad_scores, q)
        total = total + gk
        gkv_ref[:, lanes] = jnp.where(low, gk, grad_values).astype(bf16)
    gsh_ref[...] = total


def attend_back(query, keyval, shared, tables, grad_attended):
    tokens = query.shape[0]
    heads = query.shape[1] // LANES
    wide = pl.BlockSpec((SLOT, heads * LANES), lambda s: (s, 0))
    one = pl.BlockSpec((SLOT, LANES), lambda s: (s, 0))
    return pl.pallas_call(
        functools.partial(attend_back_kernel, heads),
        grid=(tokens // SLOT,),
        in_specs=[wide, wide, one, one, one, one,
                  pl.BlockSpec((1, SLOT, SLOT), lambda s: (s, 0, 0)),
                  pl.BlockSpec((SLOT, heads * VDIM), lambda s: (s, 0))],
        out_specs=[wide, wide, one],
        out_shape=[
            jax.ShapeDtypeStruct(query.shape, bf16),
            jax.ShapeDtypeStruct(keyval.shape, bf16),
            jax.ShapeDtypeStruct((tokens, LANES), f32),
        ],
        name="attend_back",
    )(query, keyval, shared, *tables, grad_attended)


def gather(value):
    return lax.all_gather(value, "shard", axis=0, tiled=True)


def scatter(value):
    return lax.psum_scatter(value.astype(bf16), "shard", scatter_dimension=0, tiled=True).astype(f32)


def layer_forward(hidden, own_tables, tables, gains, weights):
    input_gain, query_gain, latent_gain, post_gain = gains
    down_both, query_up, latent_up, output_weight, gate_up, down_weight = weights
    scale_in = norm_scale(hidden)
    normed = (hidden * scale_in * input_gain).astype(bf16)
    latents = project(normed, down_both)
    latent_q = latents[:, :QRANK]
    latent = latents[:, QRANK:QRANK + KVRANK]
    scale_q = norm_scale(latent_q)
    scale_kv = norm_scale(latent)
    own_in = jnp.concatenate(
        [
            latent_q * scale_q * query_gain,
            latent * scale_kv * latent_gain,
            rotate(latents[:, QRANK + KVRANK:], *own_tables),
        ],
        axis=1,
    ).astype(bf16)
    all_in = gather(own_in)
    query_in = all_in[:, :QRANK]
    kv_in = all_in[:, QRANK:QRANK + KVRANK]
    shared = jnp.pad(all_in[:, QRANK + KVRANK:], ((0, 0), (NOPE, LANES - NOPE - ROPE)))
    attended, queries, keyval = attend(
        project(query_in, query_up), project(kv_in, latent_up), shared, tables
    )
    mixed = hidden + residual_scale * scatter(project(attended, output_weight))
    scale_post = norm_scale(mixed)
    own_two = (mixed * scale_post * post_gain).astype(bf16)
    normed_two = gather(own_two)
    both = project(normed_two, gate_up)
    width = both.shape[1] // 2
    gate, up = both[:, :width], both[:, width:]
    activated = (jax.nn.silu(gate) * up).astype(bf16)
    output = mixed + residual_scale * scatter(project(activated, down_weight))
    kept = (hidden, scale_in, normed, latent_q, scale_q, latent, scale_kv, query_in, kv_in,
            shared, queries, keyval, attended, mixed, scale_post, own_two, gate, up)
    return (output, kept)


def gate_backward(grad_act, gate, up):
    sigmoid = jax.nn.sigmoid(gate)
    grad_gate = (grad_act * up * sigmoid * (1.0 + gate * (1.0 - sigmoid))).astype(bf16)
    grad_up = (grad_act * gate * sigmoid).astype(bf16)
    return jnp.concatenate([grad_gate, grad_up], axis=1)


def layer_backward(grad_out, kept, own_tables, tables, gains, weights):
    (hidden, scale_in, normed, latent_q, scale_q, latent, scale_kv, query_in, kv_in,
     shared, queries, keyval, attended, mixed, scale_post, own_two, gate, up) = kept
    input_gain, query_gain, latent_gain, post_gain = gains
    down_both, query_up, latent_up, output_weight, gate_up, down_weight = weights
    cosine, sine = own_tables
    own_down = (residual_scale * grad_out).astype(bf16)
    grad_down = gather(own_down)
    grad_both = gate_backward(contract_cols(grad_down, down_weight), gate, up)
    grad_normed_two = scatter(contract_cols(grad_both, gate_up))
    grad_mixed_norm, dgain_post = norm_back(mixed, scale_post, post_gain, grad_normed_two)
    grad_mixed = grad_out + grad_mixed_norm
    grad_branch = gather((residual_scale * grad_mixed).astype(bf16))
    grad_attended = contract_cols(grad_branch, output_weight).astype(bf16)
    grad_query, grad_keyval, grad_shared = attend_back(queries, keyval, shared, tables, grad_attended)
    grad_in = scatter(
        jnp.concatenate(
            [
                contract_cols(grad_query, query_up),
                contract_cols(grad_keyval, latent_up),
                grad_shared[:, NOPE:NOPE + ROPE],
            ],
            axis=1,
        )
    )
    grad_latent_q, dgain_query = norm_back(latent_q, scale_q, query_gain, grad_in[:, :QRANK])
    grad_latent, dgain_latent = norm_back(
        latent, scale_kv, latent_gain, grad_in[:, QRANK:QRANK + KVRANK]
    )
    grad_lat = jnp.concatenate(
        [grad_latent_q, grad_latent, rotate(grad_in[:, QRANK + KVRANK:], cosine, -sine)], axis=1
    ).astype(bf16)
    grad_normed = contract_cols(grad_lat, down_both)
    grad_hidden_norm, dgain_input = norm_back(hidden, scale_in, input_gain, grad_normed)
    grad_hidden = grad_mixed + grad_hidden_norm
    found = (own_down, grad_branch, grad_query, grad_keyval, grad_lat)
    return (grad_hidden, found, (dgain_input, dgain_query, dgain_latent, dgain_post))


def spread(weight, count):
    rows, columns = weight.shape
    parts = weight.reshape(rows, count, columns // count).transpose(1, 0, 2)
    return lax.all_to_all(parts, "shard", 0, 0, tiled=True).reshape(rows * count, columns // count)


def collect(grad, count):
    rows, columns = grad.shape
    parts = lax.all_to_all(
        grad.reshape(count, rows // count, columns), "shard", 0, 0, tiled=True
    )
    return parts.transpose(1, 0, 2).reshape(rows // count, columns * count)


def pad_heads(weight):
    rows, columns = weight.shape
    heads = weight.reshape(rows, columns // (NOPE + ROPE), NOPE + ROPE)
    return jnp.pad(heads, ((0, 0), (0, 0), (0, LANES - NOPE - ROPE))).reshape(rows, -1)


def cut_heads(grad):
    rows, columns = grad.shape
    heads = grad.reshape(rows, columns // LANES, LANES)[:, :, :NOPE + ROPE]
    return heads.reshape(rows, -1)


def body(tokens, segment_ids, input_gain, query_gain, latent_gain, post_gain, query_down, query_up,
         latent_down, latent_up, output_weight, gate_weight, up_weight, down_weight, cotangent):
    at_start = lax.axis_index("section") == 0
    sections = lax.axis_size("section")
    count = lax.axis_size("shard")
    gains = (input_gain[0], query_gain[0], latent_gain[0], post_gain[0])
    down_both = gather(jnp.concatenate([query_down[0], latent_down[0]], axis=1))
    query_up_all = pad_heads(spread(query_up[0], count))
    latent_up_all = spread(latent_up[0], count)
    gate_up = jnp.concatenate([spread(gate_weight[0], count), spread(up_weight[0], count)], axis=1)
    weights = (down_both, query_up_all, latent_up_all, output_weight[0], gate_up, down_weight[0])
    own_tables = tuple(t.reshape(-1, ROPE // 2) for t in slot_tables(segment_ids))
    tables = head_tables(gather(segment_ids))

    start = tokens.astype(f32)
    onward = [(source, source + 1) for source in range(sections - 1)]
    back = [(source + 1, source) for source in range(sections - 1)]
    leaving, _ = layer_forward(start, own_tables, tables, gains, weights)
    received = lax.ppermute(leaving.astype(bf16), "section", onward)
    entering = jnp.where(at_start, start, received.astype(f32))
    leaving, kept = layer_forward(entering, own_tables, tables, gains, weights)
    boundary = leaving.astype(bf16)

    last = cotangent.astype(f32)
    grad, _, _ = layer_backward(last, kept, own_tables, tables, gains, weights)
    returned = lax.ppermute(grad.astype(bf16), "section", back)
    incoming = jnp.where(at_start, returned.astype(f32), last)
    grad, found, gain_terms = layer_backward(incoming, kept, own_tables, tables, gains, weights)

    (hidden, scale_in, normed, latent_q, scale_q, latent, scale_kv, query_in, kv_in,
     shared, queries, keyval, attended, mixed, scale_post, own_two, gate, up) = kept
    own_down, grad_branch, grad_query, grad_keyval, grad_lat = found

    two_all = lax.all_gather(own_two, ("rep", "shard"), axis=0, tiled=True)
    down_all = lax.all_gather(own_down, ("rep", "shard"), axis=0, tiled=True)
    both = project(two_all, gate_up)
    width = both.shape[1] // 2
    gate_all, up_all = both[:, :width], both[:, width:]
    activated_all = (jax.nn.silu(gate_all) * up_all).astype(bf16)
    grad_both = gate_backward(contract_cols(down_all, down_weight[0]), gate_all, up_all)
    total_gate = collect(contract_rows(two_all, grad_both[:, :width]).astype(bf16), count)
    total_up = collect(contract_rows(two_all, grad_both[:, width:]).astype(bf16), count)
    total_down = contract_rows(activated_all, down_all)

    normed_rows = lax.all_to_all(
        normed.reshape(normed.shape[0], count, -1).transpose(1, 0, 2), "shard", 0, 0, tiled=True
    ).reshape(normed.shape[0] * count, -1)
    part_down = contract_rows(normed_rows, gather(grad_lat)).astype(bf16)
    part_query = collect(cut_heads(contract_rows(query_in, grad_query).astype(bf16)), count)
    part_latent = collect(contract_rows(kv_in, grad_keyval).astype(bf16), count)
    part_output = contract_rows(attended, grad_branch).astype(bf16)
    total_down_both, total_query, total_latent, total_output = (
        part.astype(f32) for part in lax.psum((part_down, part_query, part_latent, part_output), "rep")
    )
    gain_totals = lax.psum(gain_terms, ("rep", "shard"))
    return (
        boundary[None],
        grad[None],
        gain_totals[0][None],
        gain_totals[1][None],
        gain_totals[2][None],
        gain_totals[3][None],
        total_down_both[None, :, :QRANK],
        total_query[None],
        total_down_both[None, :, QRANK:],
        total_latent[None],
        total_output[None],
        total_gate.astype(f32)[None],
        total_up.astype(f32)[None],
        total_down[None],
    )


def solution(mesh):
    tokens = P(("rep", "shard"), None)
    gain = P("section", None)
    weight = P("section", "shard", None)
    out = P("section", ("rep", "shard"), None)
    return jax.shard_map(
        body,
        mesh=mesh,
        in_specs=(tokens, tokens) + (gain,) * 4 + (weight,) * 8 + (tokens,),
        out_specs=(out, out) + (gain,) * 4 + (weight,) * 8,
        check_vma=False,
    )
```

time: 3430 us -> 1990 us (0.58)
  waiting for transfers between devices: 2590 us -> 884 us
  Pallas kernels: 0 us -> 134 us
  blocking collectives: 66.2 us -> 157 us
  matrix products: 536 us -> 460 us
  local copies, waits for them, and re-layouts: 92.1 us -> 168 us
  starting transfers between devices: 10.2 us -> 54.2 us
    psum x1, waiting for transfers between devices: 956 us -> 0.01 us  [body(): lax.psum((part_down, part_query, part_latent, part_output), 'rep')]
    unnamed x21, waiting for transfers between devices: 703 us -> 1.37 us
    all_gather x8 -> x12, waiting for transfers between devices: 732 us -> 342 us  [the longest x10 212 us: gather(): return lax.all_gather(value, 'shard', axis=0, tiled=True)]
    all_to_all x0 -> x9, waiting for transfers between devices: none -> 206 us  [the longest x4 158 us: spread(): lax.all_to_all(parts, 'shard', 0, 0, tiled=True)]
    pallas_call x0 -> x4, Pallas kernels: none -> 134 us  [the longest x2 74.8 us: attend_back(): pl.pallas_call(functools.partial(attend_back_kernel, heads), grid=(tokens...]
    reduce_scatter x4 -> x8, waiting for transfers between devices: 181 us -> 293 us  [scatter(): lax.psum_scatter(value.astype(bf16), 'shard', scatter_dimension=0, tiled=...]
    dot_general x24 -> x13, matrix products: 220 us -> 144 us  [contract_cols(): lax.dot_general(left, right, (((1,), (1,)), ((), ())), preferred_element_...]
    dot_general x45 -> x13, matrix products: 253 us -> 180 us  [project(): return jnp.dot(left, weight, preferred_element_type=f32)]
  transfers between devices with their start and end apart: 21 -> 32, of which waited for: 18 -> 23; matrix products, arithmetic and copies ran while one was open for 7% -> 24% of each run, Pallas kernels for 0% -> 0%
where the time goes in v1:
time: 1990 us; the launch traced here: 1970 us
  waiting for transfers between devices  884 us (44%)
  matrix products  460 us (23%)
  local copies, waits for them, and re-layouts  168 us (8%)
  blocking collectives  157 us (8%)
  Pallas kernels  134 us (7%)
  other arithmetic  94.9 us (5%)
  starting transfers between devices  54.2 us (3%)
    reduce_scatter x8, waiting for transfers between devices, scatter(): lax.psum_scatter(value.astype(bf16), 'shard', scatter_dimension=0, tiled=...  293 us
    all_gather x10, waiting for transfers between devices, gather(): return lax.all_gather(value, 'shard', axis=0, tiled=True)  212 us
    dot_general x13, matrix products, project(): return jnp.dot(left, weight, preferred_element_type=f32)  180 us
    all_to_all x4, waiting for transfers between devices, spread(): lax.all_to_all(parts, 'shard', 0, 0, tiled=True)  158 us
    dot_general x13, matrix products, contract_cols(): lax.dot_general(left, right, (((1,), (1,)), ((), ())), preferred_element_...  144 us
    dot_general x7, matrix products, contract_rows(): lax.dot_general(left, right, (((0,), (0,)), ((), ())), preferred_element_...  137 us
    psum x1, blocking collectives, body(): gain_totals = lax.psum(gain_terms, ('rep', 'shard'))  132 us
    all_gather x1, waiting for transfers between devices, body(): two_all = lax.all_gather(own_two, ('rep', 'shard'), axis=0, tiled=True)  89.4 us
  transfers between devices with their start and end apart: 32, of which 23 were waited for; matrix products, arithmetic and copies ran while one was open for 24% of the time, Pallas kernels for 0%

profile of v1, /device:TPU:1, one launch (start us, length us, event | category | flops | bytes accessed | tf_op | source)
XLA Modules:
  0.0 1968.7 jit_solution(5901017557491961818)
XLA Ops:
  14.4 44.4 %all-gather.14.cloned.1.call-done = bf16[2560,1056]{1,0:T(8,128)(2,1)} async-done(((bf16[640,1056]{1,0:T(8,128)(2,1)}), bf16[2560,1056]{1,0:T(8,128)(2,1)}) %all-gather.14.cloned.1.call-update) | async-done | bytes 5406736 | tf_op jit(solution)/shard_map/all_gather | solution.py:200
  209.9 35.1 %reduce-scatter.9.cloned.1.call-done = bf16[192,2560]{1,0:T(8,128)(2,1)} async-done(((bf16[768,2560]{1,0:T(8,128)(2,1)}), bf16[192,2560]{1,0:T(8,128)(2,1)}) %reduce-scatter.9.cloned.1.call-update) | async-done | bytes 983056 | tf_op jit(solution)/shard_map/reduce_scatter | solution.py:204
  247.0 62.3 %all-to-all-done.2 = bf16[4,640,1600]{1,2,0:T(8,128)(2,1)} async-done(((bf16[4,640,1600]{1,2,0:T(8,128)(2,1)}), bf16[4,640,1600]{1,2,0:T(8,128)(2,1)}, u32[]{:S(2)}, u32[]{:S(2)}) %all-to-all-start.2) | async-done | bytes 8192032 | tf_op jit(solution)/shard_map/all_to_all | solution.py:295
  331.0 96.0 %all-to-all-done.3 = bf16[4,640,1600]{1,2,0:T(8,128)(2,1)} async-done(((bf16[4,640,1600]{1,2,0:T(8,128)(2,1)}), bf16[4,640,1600]{1,2,0:T(8,128)(2,1)}, u32[]{:S(2)}, u32[]{:S(2)}) %all-to-all-start.3) | async-done | bytes 8192032 | tf_op jit(solution)/shard_map/all_to_all | solution.py:295
  474.8 43.2 %reduce-scatter.11.cloned.1.call-done = bf16[192,2560]{1,0:T(8,128)(2,1)} async-done(((bf16[768,2560]{1,0:T(8,128)(2,1)}), bf16[192,2560]{1,0:T(8,128)(2,1)}) %reduce-scatter.11.cloned.1.call-update) | async-done | bytes 983056 | tf_op jit(solution)/shard_map/reduce_scatter | solution.py:204
  589.6 29.8 %attend.3 = (bf16[768,640]{1,0:T(8,128)(2,1)}, bf16[768,1280]{1,0:T(8,128)(2,1)}, bf16[768,1280]{1,0:T(8,128)(2,1)}) custom-call(f32[768,1280]{1,0:T(8,128)} %fusion.52.q_ref, f32[768,1280]{1,0:T(8,128)} %fusion.62.kv_ref, bf16[768,128]{1,0:T(8,128)(2,1)} %pad.15.sh_ref, f32[768,128]{1,0:T(8,128)} %get-tuple-element.164.keep_ref, ...), custom_call_target="tpu_custom_call" | custom-call | tf_op jit(solution)/shard_map/attend/pallas_call | solution.py:125
  625.4 42.6 %reduce-scatter.13.cloned.1.call-done = bf16[192,2560]{1,0:T(8,128)(2,1)} async-done(((bf16[768,2560]{1,0:T(8,128)(2,1)}), bf16[192,2560]{1,0:T(8,128)(2,1)}) %reduce-scatter.13.cloned.1.call-update) | async-done | bytes 983056 | tf_op jit(solution)/shard_map/reduce_scatter | solution.py:204
  675.5 31.0 %all-gather.22.cloned.1.call-done = bf16[768,2560]{1,0:T(8,128)(2,1)} async-done(((bf16[192,2560]{1,0:T(8,128)(2,1)}), bf16[768,2560]{1,0:T(8,128)(2,1)}) %all-gather.22.cloned.1.call-update) | async-done | bytes 3932176 | tf_op jit(solution)/shard_map/all_gather | solution.py:200
  779.0 42.6 %reduce-scatter.17.cloned.1.call-done = bf16[192,2560]{1,0:T(8,128)(2,1)} async-done(((bf16[768,2560]{1,0:T(8,128)(2,1)}), bf16[192,2560]{1,0:T(8,128)(2,1)}) %reduce-scatter.17.cloned.1.call-update) | async-done | bytes 983056 | tf_op jit(solution)/shard_map/reduce_scatter | solution.py:204
  827.3 33.5 %all-gather.26.cloned.1.call-done = bf16[768,2560]{1,0:T(8,128)(2,1)} async-done(((bf16[192,2560]{1,0:T(8,128)(2,1)}), bf16[768,2560]{1,0:T(8,128)(2,1)}) %all-gather.26.cloned.1.call-update) | async-done | bytes 3932176 | tf_op jit(solution)/shard_map/all_gather | solution.py:200
  867.1 37.6 %attend_back.2 = (bf16[768,1280]{1,0:T(8,128)(2,1)}, bf16[768,1280]{1,0:T(8,128)(2,1)}, f32[768,128]{1,0:T(8,128)}) custom-call(bf16[768,1280]{1,0:T(8,128)(2,1)} %get-tuple-element.26.q_ref, bf16[768,1280]{1,0:T(8,128)(2,1)} %get-tuple-element.27.kv_ref, bf16[768,128]{1,0:T(8,128)(2,1)} %pad.15.sh_ref, f32[768,128]{1,0:T(8,128)} %get-tuple-element.164.keep_ref, ...), custom_call_target="tpu_custom_call" | custom-call | tf_op jit(solution)/shard_map/attend_back/pallas_call | solution.py:183
  983.0 33.5 %all-gather.28.cloned.1.call-done = bf16[768,2560]{1,0:T(8,128)(2,1)} async-done(((bf16[192,2560]{1,0:T(8,128)(2,1)}), bf16[768,2560]{1,0:T(8,128)(2,1)}) %all-gather.28.cloned.1.call-update) | async-done | bytes 3932176 | tf_op jit(solution)/shard_map/all_gather | solution.py:200
  1098.6 42.9 %reduce-scatter.15.cloned.1.call-done = bf16[192,2560]{1,0:T(8,128)(2,1)} async-done(((bf16[768,2560]{1,0:T(8,128)(2,1)}), bf16[192,2560]{1,0:T(8,128)(2,1)}) %reduce-scatter.15.cloned.1.call-update) | async-done | bytes 983056 | tf_op jit(solution)/shard_map/reduce_scatter | solution.py:204
  1147.1 33.5 %all-gather.30.cloned.1.call-done = bf16[768,2560]{1,0:T(8,128)(2,1)} async-done(((bf16[192,2560]{1,0:T(8,128)(2,1)}), bf16[768,2560]{1,0:T(8,128)(2,1)}) %all-gather.30.cloned.1.call-update) | async-done | bytes 3932176 | tf_op jit(solution)/shard_map/all_gather | solution.py:200
  1186.9 37.2 %attend_back.3 = (bf16[768,1280]{1,0:T(8,128)(2,1)}, bf16[768,1280]{1,0:T(8,128)(2,1)}, f32[768,128]{1,0:T(8,128)}) custom-call(bf16[768,1280]{1,0:T(8,128)(2,1)} %get-tuple-element.26.q_ref, bf16[768,1280]{1,0:T(8,128)(2,1)} %get-tuple-element.27.kv_ref, bf16[768,128]{1,0:T(8,128)(2,1)} %pad.15.sh_ref, f32[768,128]{1,0:T(8,128)} %get-tuple-element.164.keep_ref, ...), custom_call_target="tpu_custom_call" | custom-call | tf_op jit(solution)/shard_map/attend_back/pallas_call | solution.py:183
  1294.4 89.4 %all-gather.34.cloned.1.call-done = bf16[3072,2560]{1,0:T(8,128)(2,1)} async-done(((bf16[192,2560]{1,0:T(8,128)(2,1)}), bf16[3072,2560]{1,0:T(8,128)(2,1)}) %all-gather.34.cloned.1.call-update) | async-done | bytes 15728656 | tf_op jit(solution)/shard_map/all_gather | solution.py:351
  1383.7 70.4 %fusion.105 = f32[3072,3200]{0,1:T(8,128)} fusion(bf16[3072,2560]{1,0:T(8,128)(2,1)} %all-gather.34.cloned.1.call-done, bf16[2560,1600]{1,0:T(8,128)(2,1)} %bitcast.153, bf16[2560,1600]{1,0:T(8,128)(2,1)} %bitcast.148), kind=kOutput, calls=%fused_computation.220 | convolution fusion | flops 50364416000 | bytes 71434240 | tf_op jit(solution)/shard_map/dot_general | solution.py:83
  1496.9 40.3 %all-gather.36.cloned.1.call-done = bf16[3072,2560]{1,0:T(8,128)(2,1)} async-done(((bf16[192,2560]{1,0:T(8,128)(2,1)}), bf16[3072,2560]{1,0:T(8,128)(2,1)}) %all-gather.36.cloned.1.call-update) | async-done | bytes 15728656 | tf_op jit(solution)/shard_map/all_gather | solution.py:352
  1537.3 33.2 %fusion = f32[3072,1600]{0,1:T(8,128)} fusion(bf16[3072,2560]{1,0:T(8,128)(2,1)} %all-gather.36.cloned.1.call-done, bf16[1,1600,2560]{2,1,0:T(8,128)(2,1)} %param.28), kind=kOutput, calls=%fused_computation.10 | convolution fusion | flops 25165824000 | bytes 43581440 | tf_op jit(solution)/shard_map/dot_general | solution.py:79
  1570.5 36.2 %convolution_convert_fusion = bf16[2560,1600]{0,1:T(8,128)(2,1)} fusion(bf16[3072,2560]{1,0:T(8,128)(2,1)} %all-gather.34.cloned.1.call-done, f32[3072,1600]{0,1:T(8,128)} %fusion, f32[3072,3200]{0,1:T(8,128)} %fusion.105), kind=kOutput, calls=%fused_computation.6 | convolution fusion | flops 25199411200 | bytes 63242240 | tf_op jit(solution)/shard_map/dot_general | solution.py:75
  1620.0 44.2 %convolution_convert_fusion.1 = bf16[2560,1600]{0,1:T(8,128)(2,1)} fusion(bf16[3072,2560]{1,0:T(8,128)(2,1)} %all-gather.34.cloned.1.call-done, f32[3072,1600]{0,1:T(8,128)} %fusion, f32[3072,3200]{0,1:T(8,128)} %fusion.105), kind=kOutput, calls=%fused_computation.7 | convolution fusion | flops 25219072000 | bytes 82903040 | tf_op jit(solution)/shard_map/dot_general | solution.py:75
  1672.4 37.8 %all-to-all-done.8 = bf16[4,640,1600]{1,2,0:T(8,128)(2,1)} async-done(((bf16[4,640,1600]{1,2,0:T(8,128)(2,1)}), bf16[4,640,1600]{1,2,0:T(8,128)(2,1)}, u32[]{:S(2)}, u32[]{:S(2)}) %all-to-all-start.8) | async-done | bytes 8192032 | tf_op jit(solution)/shard_map/all_to_all | solution.py:300
  1720.9 132.2 %all-reduce.5 = (f32[1,2560]{1,0:T(1,128)}, f32[1,768]{1,0:T(1,128)}, f32[1,256]{1,0:T(1,128)}, f32[1,2560]{1,0:T(1,128)}) all-reduce(f32[1,2560]{1,0:T(1,128)S(1)} %broadcast_in_dim.118, f32[1,768]{1,0:T(1,128)S(1)} %broadcast_in_dim.119, ...), channel_id=1, replica_groups=mesh['section'=2,'rep'=4,'shard'=4] {'rep','shard'}, use_global_device_ids=true, to_apply=%region_27.28 | all-reduce | flops 6144 | bytes 49152 | tf_op jit(solution)/shard_map/psum | solution.py:372
  1853.2 36.0 %convolution_bitcast_fusion = f32[1,1600,2560]{2,1,0:T(8,128)} fusion(bf16[3072,2560]{1,0:T(8,128)(2,1)} %all-gather.36.cloned.1.call-done, f32[3072,3200]{0,1:T(8,128)} %fusion.105), kind=kOutput, calls=%fused_computation.5 | convolution fusion | flops 25195315200 | bytes 71434240 | tf_op jit(solution)/shard_map/dot_general | solution.py:75
  (327 shorter events, 788.2 us)
Async XLA Ops:
  12.0 121.1 %all-gather.16.cloned.1.call-start = ((), (), s32[]{:S(2)}) async-start(), calls=%async_computation.18 | async-start | bytes 2211840 | tf_op jit(solution)/shard_map/all_gather | solution.py:200
  120.6 124.4 %reduce-scatter.9.cloned.1.call-start = ((), (), s32[]{:S(2)}) async-start(), calls=%async_computation.19 | async-start | bytes 4915200 | tf_op jit(solution)/shard_map/reduce_scatter | solution.py:204
  192.1 117.2 %all-to-all-start.2 = ((bf16[4,640,1600]{1,2,0:T(8,128)(2,1)}), bf16[4,640,1600]{1,2,0:T(8,128)(2,1)}, u32[]{:S(2)}, u32[]{:S(2)}) async-start(bf16[4,640,1600]{1,2,0:T(8,128)(2,1)} %bitcast.142), calls=%async_computation.3 | async-start | bytes 16384000 | tf_op jit(solution)/shard_map/all_to_all | solution.py:295
  309.3 117.7 %all-to-all-start.3 = ((bf16[4,640,1600]{1,2,0:T(8,128)(2,1)}), bf16[4,640,1600]{1,2,0:T(8,128)(2,1)}, u32[]{:S(2)}, u32[]{:S(2)}) async-start(bf16[4,640,1600]{1,2,0:T(8,128)(2,1)} %bitcast.141), calls=%async_computation.4 | async-start | bytes 16384000 | tf_op jit(solution)/shard_map/all_to_all | solution.py:295
  315.7 123.3 %all-gather.18.cloned.1.call-start = ((), (), s32[]{:S(2)}) async-start(), calls=%async_computation.20 | async-start | bytes 4915200 | tf_op jit(solution)/shard_map/all_gather | solution.py:200
  318.6 199.5 %reduce-scatter.11.cloned.1.call-start = ((), (), s32[]{:S(2)}) async-start(), calls=%async_computation.21 | async-start | bytes 4915200 | tf_op jit(solution)/shard_map/reduce_scatter | solution.py:204
  474.8 105.5 %all-gather.20.cloned.1.call-start = ((), (), s32[]{:S(2)}) async-start(), calls=%async_computation.22 | async-start | bytes 2211840 | tf_op jit(solution)/shard_map/all_gather | solution.py:200
  557.1 110.9 %reduce-scatter.13.cloned.1.call-start = ((), (), s32[]{:S(2)}) async-start(), calls=%async_computation.23 | async-start | bytes 4915200 | tf_op jit(solution)/shard_map/reduce_scatter | solution.py:204
  625.4 81.1 %all-gather.22.cloned.1.call-start = ((), (), s32[]{:S(2)}) async-start(), calls=%async_computation.24 | async-start | bytes 4915200 | tf_op jit(solution)/shard_map/all_gather | solution.py:200
  675.3 146.3 %reduce-scatter.17.cloned.1.call-start = ((), (), s32[]{:S(2)}) async-start(), calls=%async_computation.27 | async-start | bytes 4915200 | tf_op jit(solution)/shard_map/reduce_scatter | solution.py:204
  778.9 81.9 %all-gather.26.cloned.1.call-start = ((), (), s32[]{:S(2)}) async-start(), calls=%async_computation.28 | async-start | bytes 4915200 | tf_op jit(solution)/shard_map/all_gather | solution.py:200
  827.3 113.9 %reduce-scatter.19.cloned.1.call-start = ((), (), s32[]{:S(2)}) async-start(), calls=%async_computation.29 | async-start | bytes 2211840 | tf_op jit(solution)/shard_map/reduce_scatter | solution.py:204
  912.0 104.4 %all-gather.28.cloned.1.call-start = ((), (), s32[]{:S(2)}) async-start(), calls=%async_computation.30 | async-start | bytes 4915200 | tf_op jit(solution)/shard_map/all_gather | solution.py:200
  982.9 113.3 %reduce-scatter.21.cloned.1.call-start = ((), (), s32[]{:S(2)}) async-start(), calls=%async_computation.31 | async-start | bytes 4915200 | tf_op jit(solution)/shard_map/reduce_scatter | solution.py:204
  1053.6 87.9 %reduce-scatter.15.cloned.1.call-start = ((), (), s32[]{:S(2)}) async-start(), calls=%async_computation.25 | async-start | bytes 4915200 | tf_op jit(solution)/shard_map/reduce_scatter | solution.py:204
  1067.6 113.0 %all-gather.30.cloned.1.call-start = ((), (), s32[]{:S(2)}) async-start(), calls=%async_computation.32 | async-start | bytes 4915200 | tf_op jit(solution)/shard_map/all_gather | solution.py:200
  1147.0 113.6 %reduce-scatter.23.cloned.1.call-start = ((), (), s32[]{:S(2)}) async-start(), calls=%async_computation.33 | async-start | bytes 2211840 | tf_op jit(solution)/shard_map/reduce_scatter | solution.py:204
  1231.5 152.3 %all-gather.34.cloned.1.call-start = ((), (), s32[]{:S(2)}) async-start(), calls=%async_computation.35 | async-start | bytes 16711680 | tf_op jit(solution)/shard_map/all_gather | solution.py:351
  1232.0 260.5 %all-gather.32.cloned.1.call-start = ((), (), s32[]{:S(2)}) async-start(), calls=%async_computation.34 | async-start | bytes 2211840 | tf_op jit(solution)/shard_map/all_gather | solution.py:200
  1264.8 272.5 %all-gather.36.cloned.1.call-start = ((), (), s32[]{:S(2)}) async-start(), calls=%async_computation.36 | async-start | bytes 16711680 | tf_op jit(solution)/shard_map/all_gather | solution.py:352
  1290.0 174.3 %all-to-all-start.5 = ((bf16[4,192,960]{2,1,0:T(8,128)(2,1)}), bf16[4,192,960]{2,1,0:T(8,128)(2,1)S(1)}, u32[]{:S(2)}, u32[]{:S(2)}) async-start(bf16[4,192,960]{2,1,0:T(8,128)(2,1)} %copy.188), calls=%async_computation.13 | async-start | bytes 3145728 | tf_op jit(solution)/shard_map/all_to_all | solution.py:300
  1468.8 420.3 %all-reduce.9.cloned.1.call-start = ((), (), s32[]{:S(2)}) async-start(), calls=%async_computation.37 | async-start | bytes 13516800 | tf_op jit(solution)/shard_map/psum | solution.py:370
  1614.2 96.1 %all-to-all-start.8 = ((bf16[4,640,1600]{1,2,0:T(8,128)(2,1)}), bf16[4,640,1600]{1,2,0:T(8,128)(2,1)}, u32[]{:S(2)}, u32[]{:S(2)}) async-start(bf16[4,640,1600]{1,2,0:T(8,128)(2,1)} %bitcast.143), calls=%async_computation.16 | async-start | bytes 16384000 | tf_op jit(solution)/shard_map/all_to_all | solution.py:300
  1710.3 223.0 %all-to-all-start.7 = ((bf16[4,640,1600]{1,2,0:T(8,128)(2,1)}), bf16[4,640,1600]{1,2,0:T(8,128)(2,1)}, u32[]{:S(2)}, u32[]{:S(2)}) async-start(bf16[4,640,1600]{1,2,0:T(8,128)(2,1)} %bitcast.140), calls=%async_computation.15 | async-start | bytes 16384000 | tf_op jit(solution)/shard_map/all_to_all | solution.py:300
  (53 other events, 2641.2 us)
Sparse Core Ops, SparseCore 0:
  12.1 46.6 all-gather.13
  66.9 24.5 all-gather.15
  180.1 64.8 reduce-scatter.8
  318.7 55.4 all-gather.17
  474.9 43.1 reduce-scatter.10
  557.2 23.0 all-gather.19
  625.5 42.4 reduce-scatter.12
  673.0 33.3 all-gather.21
  708.7 32.9 all-gather.23
  779.0 42.4 reduce-scatter.16
  827.4 33.3 all-gather.25
  912.1 28.9 reduce-scatter.18
  983.0 33.3 all-gather.27
  1053.7 42.4 reduce-scatter.20
  1098.6 42.8 reduce-scatter.14
  1147.1 33.4 all-gather.29
  1231.6 28.9 reduce-scatter.22
  1262.7 120.9 all-gather.33
  1385.3 18.8 all-gather.31
  1406.4 130.8 all-gather.35
  1540.5 237.0 all-reduce.8

commit v2 on v1

v2 whole, which is shorter than its diff:
```python
import functools
import math

import jax
import jax.numpy as jnp
from jax import lax
from jax.experimental import pallas as pl
from jax.experimental.pallas import tpu as pltpu
from jax.sharding import PartitionSpec as P

D = 2560
HEADS = 40
NOPE = 64
ROPE = 32
VDIM = 64
QRANK = 768
KVRANK = 256
FF = 6400
SLOT = 96
LANES = 128

epsilon = 1e-05
residual_scale = 1.4 / math.sqrt(62.0)
masked_score = -1e30
score_scale = 1.0 / math.sqrt(NOPE + ROPE)
bf16 = jnp.bfloat16
f32 = jnp.float32


def norm_scale(value):
    return lax.rsqrt(jnp.mean(value * value, axis=-1, keepdims=True) + epsilon)


def norm_back(value, scale, gain, grad):
    weighted = grad * gain
    inner = jnp.mean(value * weighted, axis=-1, keepdims=True)
    grad_value = scale * weighted - value * (scale * scale * scale) * inner
    return (grad_value, jnp.sum(grad * value * scale, axis=0))


def rotate(value, cosine, sine):
    half = value.shape[-1] // 2
    front = value[..., :half]
    back = value[..., half:]
    return jnp.concatenate([front * cosine - back * sine, back * cosine + front * sine], axis=-1)


def slot_tables(segments):
    index = jnp.arange(SLOT, dtype=jnp.int32)
    first_index = jnp.sum((segments[:, None, :] < segments[:, :, None]).astype(jnp.int32), axis=-1)
    position = (index - first_index).astype(f32)
    freq = jnp.exp(jnp.arange(ROPE // 2, dtype=f32) * (-2.0 * math.log(10000.0) / ROPE))
    angle = position[..., None] * freq
    return (jnp.cos(angle), jnp.sin(angle))


def head_tables(segments):
    cosine, sine = slot_tables(segments)
    slots = segments.shape[0]
    ones = jnp.ones((slots, SLOT, NOPE), f32)
    tail = jnp.zeros((slots, SLOT, LANES - NOPE - ROPE), f32)
    half = jnp.zeros_like(sine)
    keep = jnp.concatenate([ones, cosine, cosine, tail], axis=-1)
    left = jnp.concatenate([0.0 * ones, -sine, half, tail], axis=-1)
    right = jnp.concatenate([0.0 * ones, half, sine, tail], axis=-1)
    index = jnp.arange(SLOT, dtype=jnp.int32)
    allowed = (segments[:, :, None] == segments[:, None, :]) & (index[None, :] <= index[:, None])
    mask = jnp.where(allowed, 0.0, masked_score).astype(f32)
    flat = lambda table: table.reshape(slots * SLOT, LANES)
    return (flat(keep), flat(left), flat(right), mask, mask.transpose(0, 2, 1))


def contract_rows(left, right):
    return lax.dot_general(left, right, (((0,), (0,)), ((), ())), preferred_element_type=f32)


def contract_cols(left, right):
    return lax.dot_general(left, right, (((1,), (1,)), ((), ())), preferred_element_type=f32)


def project(left, weight):
    return jnp.dot(left, weight, preferred_element_type=f32)


def low_lanes():
    return lax.broadcasted_iota(jnp.int32, (SLOT, LANES), 1) < NOPE


HEAD_GROUP = 5
HEAD_ROWS = 16


def attend_kernel(heads, q_ref, kv_ref, sh_ref, keep_ref, left_ref, right_ref, mask_ref,
                  att_ref, qo_ref, kvo_ref, log_ref):
    low = low_lanes()
    lane = lax.broadcasted_iota(jnp.int32, (SLOT, LANES), 1)
    shared = sh_ref[...].astype(f32)
    keep, left, right = keep_ref[...], left_ref[...], right_ref[...]
    mask = mask_ref[0]
    tallest = jnp.zeros((SLOT, LANES), f32)
    sums = jnp.ones((SLOT, LANES), f32)
    for first in range(0, heads, HEAD_GROUP):
        group = range(first, min(first + HEAD_GROUP, heads))
        scores, values = [], []
        for head in group:
            lanes = slice(head * LANES, (head + 1) * LANES)
            q = q_ref[:, lanes]
            q = q * keep + pltpu.roll(q, LANES - 16, 1) * left + pltpu.roll(q, 16, 1) * right
            q = q.astype(bf16)
            qo_ref[:, lanes] = q
            kv = kv_ref[:, lanes]
            kvo_ref[:, lanes] = kv.astype(bf16)
            k = jnp.where(low, kv, shared).astype(bf16)
            values.append(jnp.where(low, 1.0, kv).astype(bf16))
            scores.append(contract_cols(q, k) * score_scale + mask)
        tops = [jnp.max(score, axis=-1, keepdims=True) for score in scores]
        terms = [jnp.exp(score - top).astype(bf16) for score, top in zip(scores, tops)]
        outs = [project(term, value) for term, value in zip(terms, values)]
        for head, top, out in zip(group, tops, outs):
            turned = pltpu.roll(out, NOPE, 1)
            tallest = jnp.where(lane == head, top, tallest)
            sums = jnp.where(lane == head, out, sums)
            pair = (head // 2) * LANES
            if head % 2 == 0:
                att = turned / out
                att_ref[:, pair:pair + VDIM] = att[:, :VDIM].astype(bf16)
            else:
                att = out / turned
                att_ref[:, pair + VDIM:pair + LANES] = att[:, VDIM:].astype(bf16)
    log_ref[0] = (tallest + jnp.log(sums)).T[:HEAD_ROWS, :]


def attention_cost(tokens, heads, passes):
    return pl.CostEstimate(
        flops=passes * tokens * heads * SLOT * LANES * 20, bytes_accessed=tokens * heads * LANES * 12,
        transcendentals=tokens * heads * SLOT,
    )


def attend(query, keyval, shared, tables):
    tokens = query.shape[0]
    heads = query.shape[1] // LANES
    wide = pl.BlockSpec((SLOT, heads * LANES), lambda s: (s, 0))
    one = pl.BlockSpec((SLOT, LANES), lambda s: (s, 0))
    square = pl.BlockSpec((1, SLOT, SLOT), lambda s: (s, 0, 0))
    return pl.pallas_call(
        functools.partial(attend_kernel, heads),
        grid=(tokens // SLOT,),
        in_specs=[wide, wide, one, one, one, one, square],
        out_specs=[pl.BlockSpec((SLOT, heads * VDIM), lambda s: (s, 0)), wide, wide,
                   pl.BlockSpec((1, HEAD_ROWS, SLOT), lambda s: (s, 0, 0))],
        out_shape=[
            jax.ShapeDtypeStruct((tokens, heads * VDIM), bf16),
            jax.ShapeDtypeStruct(query.shape, bf16),
            jax.ShapeDtypeStruct(keyval.shape, bf16),
            jax.ShapeDtypeStruct((tokens // SLOT, HEAD_ROWS, SLOT), f32),
        ],
        cost_estimate=attention_cost(tokens, heads, 4),
        name="attend",
    )(query, keyval, shared, *tables[:4])


def attend_back_kernel(heads, q_ref, kv_ref, sh_ref, keep_ref, left_ref, right_ref, mask_ref,
                       ga_ref, att_ref, log_ref, gq_ref, gkv_ref, gsh_ref):
    low = low_lanes()
    shared = sh_ref[...].astype(f32)
    keep, left, right = keep_ref[...], left_ref[...], right_ref[...]
    mask = mask_ref[0]
    total = jnp.zeros((SLOT, LANES), f32)
    product = ga_ref[...].astype(f32) * att_ref[...].astype(f32)
    high = product.astype(bf16)
    rest = (product - high.astype(f32)).astype(bf16)
    shape = (HEAD_ROWS, product.shape[1])
    chosen = lax.broadcasted_iota(jnp.int32, shape, 1) // VDIM == lax.broadcasted_iota(jnp.int32, shape, 0)
    chosen = jnp.where(chosen, 1.0, 0.0).astype(bf16)
    inner = contract_cols(chosen, high) + contract_cols(chosen, rest)
    for first in range(0, heads, HEAD_GROUP):
        group = range(first, min(first + HEAD_GROUP, heads))
        queries, keys, grads, scores, grad_probs = [], [], [], [], []
        for head in group:
            lanes = slice(head * LANES, (head + 1) * LANES)
            q = q_ref[:, lanes]
            kvb = kv_ref[:, lanes]
            k = jnp.where(low, kvb.astype(f32), shared).astype(bf16)
            if head % 2 == 0 and head == heads - 1:
                ga = ga_ref[:, head * VDIM:(head + 1) * VDIM].astype(f32)
                ga = jnp.concatenate([jnp.zeros_like(ga), ga], axis=1)
            else:
                start = (head // 2) * LANES
                ga = ga_ref[:, start:start + LANES].astype(f32)
                if head % 2 == 0:
                    ga = pltpu.roll(ga, NOPE, 1)
                ga = jnp.where(low, 0.0, ga)
            ga = ga.astype(bf16)
            queries.append(q)
            keys.append(k)
            grads.append(ga)
            scores.append(contract_cols(k, q) * score_scale + mask)
            grad_probs.append(contract_cols(kvb, ga))
        probs = [jnp.exp(score - log_ref[0, head:head + 1, :]) for head, score in zip(group, scores)]
        changes = [
            (prob * (grad - inner[head:head + 1, :]) * score_scale).astype(bf16)
            for head, prob, grad in zip(group, probs, grad_probs)
        ]
        grad_values = [project(prob.astype(bf16), ga) for prob, ga in zip(probs, grads)]
        grad_keys = [project(change, q) for change, q in zip(changes, queries)]
        grad_queries = [contract_rows(change, k) for change, k in zip(changes, keys)]
        for head, gv, gk, gq in zip(group, grad_values, grad_keys, grad_queries):
            lanes = slice(head * LANES, (head + 1) * LANES)
            gq = gq * keep - pltpu.roll(gq, LANES - 16, 1) * left - pltpu.roll(gq, 16, 1) * right
            gq_ref[:, lanes] = gq.astype(bf16)
            total = total + gk
            gkv_ref[:, lanes] = jnp.where(low, gk, gv).astype(bf16)
    gsh_ref[...] = total


def attend_back(query, keyval, shared, tables, grad_attended, attended, logs):
    tokens = query.shape[0]
    heads = query.shape[1] // LANES
    wide = pl.BlockSpec((SLOT, heads * LANES), lambda s: (s, 0))
    one = pl.BlockSpec((SLOT, LANES), lambda s: (s, 0))
    half = pl.BlockSpec((SLOT, heads * VDIM), lambda s: (s, 0))
    return pl.pallas_call(
        functools.partial(attend_back_kernel, heads),
        grid=(tokens // SLOT,),
        in_specs=[wide, wide, one, one, one, one, pl.BlockSpec((1, SLOT, SLOT), lambda s: (s, 0, 0)),
                  half, half, pl.BlockSpec((1, HEAD_ROWS, SLOT), lambda s: (s, 0, 0))],
        out_specs=[wide, wide, one],
        out_shape=[
            jax.ShapeDtypeStruct(query.shape, bf16),
            jax.ShapeDtypeStruct(keyval.shape, bf16),
            jax.ShapeDtypeStruct((tokens, LANES), f32),
        ],
        cost_estimate=attention_cost(tokens, heads, 10),
        name="attend_back",
    )(query, keyval, shared, *tables[:3], tables[4], grad_attended, attended, logs)


MESH = pl.DeviceIdType.MESH
VMEM_LIMIT = 60 * 1024 * 1024


def partners():
    me = lax.axis_index("shard")
    core = me % 2
    return me, core, me + 1 - 2 * core, (me + 2) % 4


def greet(devices):
    barrier = pltpu.get_barrier_semaphore()
    for device in devices:
        pl.semaphore_signal(barrier, inc=1, device_id=device, device_id_type=MESH)
    pl.semaphore_wait(barrier, len(devices))


def columns(step, width):
    return pl.ds(pl.multiple_of(step * width, LANES), width)


def rows_at(start, rows):
    return pl.ds(pl.multiple_of(start * rows, 16), rows)


def remote(source, target, sems, step, device):
    return pltpu.make_async_remote_copy(
        src_ref=source, dst_ref=target, send_sem=sems.at[0, step], recv_sem=sems.at[1, step],
        device_id={"shard": device}, device_id_type=MESH,
    )


def exchange_scratch(rows, steps, width):
    part = pltpu.VMEM((steps, rows, width), bf16)
    return [part] * 6 + [
        pltpu.VMEM((steps, rows, width), f32),
        pltpu.VMEM((2 * rows, width), f32),
        pltpu.SemaphoreType.DMA((3, 2, steps)),
    ]


def each(steps, unrolled, do):
    if unrolled:
        for step in range(steps):
            do(step)
    else:
        def again(step, carry):
            do(step)
            return carry
        lax.fori_loop(0, steps, again, 0)


def sum_scatter(rows, steps, unrolled, partial, scratch, use):
    (to_sib, from_sib, to_far, from_far, own_sib, own_from, hold, stage, sems) = scratch
    me, core, sib, far = partners()
    mine = rows_at(core, rows)
    other = rows_at(1 - core, rows)

    def first(step):
        return remote(to_sib.at[step], from_sib.at[step], sems.at[0], step, sib)

    def across(step):
        return remote(to_far.at[step], from_far.at[step], sems.at[1], step, far)

    def beside(step):
        return remote(own_sib.at[step], own_from.at[step], sems.at[2], step, sib)

    def far_part(step):
        stage[...] = partial(rows_at(far // 2, 2 * rows), step)
        to_sib[step] = stage[other, :].astype(bf16)
        first(step).start()
        hold[step] = stage[mine, :]

    def far_send(step):
        first(step).wait_recv()
        to_far[step] = (hold[step] + from_sib[step].astype(f32)).astype(bf16)
        across(step).start()

    def far_step(step):
        far_part(step)
        if unrolled:
            if step > 0:
                far_send(step - 1)
        else:
            @pl.when(step > 0)
            def _():
                far_send(step - 1)

    each(steps, unrolled, far_step)
    far_send(steps - 1)

    def near_part(step):
        stage[...] = partial(rows_at(me // 2, 2 * rows), step)
        own_sib[step] = stage[other, :].astype(bf16)
        beside(step).start()
        hold[step] = stage[mine, :]

    each(steps, unrolled, near_part)

    def finish(step):
        beside(step).wait_recv()
        across(step).wait_recv()
        use(step, hold[step] + own_from[step].astype(f32) + from_far[step].astype(f32))

    each(steps, unrolled, finish)

    def settle(step):
        first(step).wait_send()
        across(step).wait_send()
        beside(step).wait_send()

    each(steps, unrolled, settle)


def spread_rows(rows, steps, width, place, all_ref, sems):
    me, core, sib, far = partners()

    def part(owner, step):
        return all_ref.at[rows_at(owner, rows), columns(step, width)]

    def across(step):
        return remote(part(me, step), part(me, step), sems.at[0], step, far)

    def beside(step):
        return remote(part(me, step), part(me, step), sems.at[1], step, sib)

    def onward(step):
        return remote(part(far, step), part(far, step), sems.at[2], step, sib)

    def send(step):
        place(step)
        across(step).start()
        beside(step).start()

    each(steps, False, send)

    def forward(step):
        across(step).wait_recv()
        onward(step).start()

    each(steps, False, forward)

    def settle(step):
        beside(step).wait_recv()
        onward(step).wait_recv()
        across(step).wait_send()
        beside(step).wait_send()
        onward(step).wait_send()

    each(steps, False, settle)


def vmem(count):
    return [pl.BlockSpec(memory_space=pltpu.VMEM)] * count


def comm_call(kernel, name, number, inputs, out_shape, scratch, flops=0):
    nbytes = sum(v.size * v.dtype.itemsize for v in (*inputs, *out_shape))
    return pl.pallas_call(
        kernel,
        in_specs=vmem(len(inputs)),
        out_specs=vmem(len(out_shape)),
        out_shape=out_shape,
        scratch_shapes=scratch,
        compiler_params=pltpu.CompilerParams(
            collective_id=number, has_side_effects=True, vmem_limit_bytes=VMEM_LIMIT
        ),
        cost_estimate=pl.CostEstimate(flops=flops, bytes_accessed=nbytes, transcendentals=0),
        name=name,
    )(*inputs)


def shape(rows, width, dtype):
    return jax.ShapeDtypeStruct((rows, width), dtype)


def gather_kernel(steps, width, own_ref, all_ref, sems):
    rows = own_ref.shape[0]
    me, core, sib, far = partners()
    greet([{"shard": sib}, {"shard": far}])

    def place(step):
        all_ref[rows_at(me, rows), columns(step, width)] = own_ref[:, columns(step, width)]

    spread_rows(rows, steps, width, place, all_ref, sems)


def gather(value, number, width):
    if lax.axis_size("shard") != 4:
        return lax.all_gather(value, "shard", axis=0, tiled=True)
    rows, total = value.shape
    steps = total // width
    (out,) = comm_call(
        functools.partial(gather_kernel, steps, width), "gather_rows", number, [value],
        [shape(4 * rows, total, bf16)], [pltpu.SemaphoreType.DMA((3, 2, steps))],
    )
    return out


def plain_gather(value):
    return lax.all_gather(value, "shard", axis=0, tiled=True)


def plain_scatter(value):
    return lax.psum_scatter(value.astype(bf16), "shard", scatter_dimension=0, tiled=True).astype(f32)


MODEL_STEP = 512


def output_kernel(att_ref, weight_ref, hidden_ref, gain_ref, mixed_ref, two_ref, *scratch):
    *parts, sems = scratch
    rows = hidden_ref.shape[0]
    width = MODEL_STEP
    steps = D // width
    me, core, sib, far = partners()
    greet([{"shard": sib}, {"shard": far}])

    def partial(where, step):
        return project(att_ref[where, :], weight_ref[:, columns(step, width)])

    def use(step, total):
        lanes = columns(step, width)
        mixed_ref[:, lanes] = hidden_ref[:, lanes] + residual_scale * total

    sum_scatter(rows, steps, False, partial, parts, use)
    mixed = mixed_ref[...]
    scale = norm_scale(mixed)

    def place(step):
        lanes = columns(step, width)
        two_ref[rows_at(me, rows), lanes] = (mixed_ref[:, lanes] * scale * gain_ref[:, lanes]).astype(bf16)

    spread_rows(rows, steps, width, place, two_ref, sems)


def output_norm(attended, weight, hidden, gain):
    if lax.axis_size("shard") != 4:
        mixed = hidden + residual_scale * plain_scatter(project(attended, weight))
        return mixed, plain_gather((mixed * norm_scale(mixed) * gain).astype(bf16))
    rows = hidden.shape[0]
    steps = D // MODEL_STEP
    return comm_call(
        output_kernel, "output_norm", 2, [attended, weight, hidden, gain[None]],
        [shape(rows, D, f32), shape(4 * rows, D, bf16)],
        exchange_scratch(rows, steps, MODEL_STEP) + [pltpu.SemaphoreType.DMA((3, 2, steps))],
        flops=2 * attended.size * D,
    )


def down_kernel(passing, act_ref, weight_ref, mixed_ref, out_ref, low_ref, *scratch):
    rows = mixed_ref.shape[0]
    width = MODEL_STEP
    steps = D // width
    me, core, sib, far = partners()
    devices = [{"shard": sib}, {"shard": far}]
    if passing:
        got_ref, *parts, sems = scratch
        section = lax.axis_index("section")
        devices.append({"section": 1 - section})
    else:
        parts = scratch
    greet(devices)

    def onward(step):
        lanes = columns(step, width)
        return pltpu.make_async_remote_copy(
            src_ref=low_ref.at[:, lanes], dst_ref=got_ref.at[:, lanes], send_sem=sems.at[0, step],
            recv_sem=sems.at[1, step], device_id={"section": 1 - section}, device_id_type=MESH,
        )

    def partial(where, step):
        return project(act_ref[where, :], weight_ref[:, columns(step, width)])

    def use(step, total):
        lanes = columns(step, width)
        out = mixed_ref[:, lanes] + residual_scale * total
        out_ref[:, lanes] = out
        low_ref[:, lanes] = out.astype(bf16)
        if passing:
            onward(step).start()

    sum_scatter(rows, steps, False, partial, parts, use)
    if passing:
        each(steps, False, lambda step: onward(step).wait())


def down_project(activated, weight, mixed, passing):
    if lax.axis_size("shard") != 4:
        output = mixed + residual_scale * plain_scatter(project(activated, weight))
        low = output.astype(bf16)
        return (output, low) + ((lax.ppermute(low, "section", [(0, 1)]),) if passing else ())
    rows = mixed.shape[0]
    steps = D // MODEL_STEP
    scratch = exchange_scratch(rows, steps, MODEL_STEP)
    return comm_call(
        functools.partial(down_kernel, passing), "down_project", 3 if passing else 4,
        [activated, weight, mixed],
        [shape(rows, D, f32)] + [shape(rows, D, bf16)] * (2 if passing else 1),
        scratch + ([pltpu.SemaphoreType.DMA((2, steps))] if passing else []),
        flops=2 * activated.size * D,
    )


def mlp_back_kernel(both_ref, weight_ref, mixed_ref, grad_ref, gain_ref, out_ref, dgain_ref, branch_ref,
                    *scratch):
    *parts, sems = scratch
    rows = mixed_ref.shape[0]
    width = MODEL_STEP
    steps = D // width
    me, core, sib, far = partners()
    greet([{"shard": sib}, {"shard": far}])

    def partial(where, step):
        return contract_cols(both_ref[where, :], weight_ref[columns(step, width), :])

    def use(step, total):
        out_ref[:, columns(step, width)] = total

    sum_scatter(rows, steps, False, partial, parts, use)
    mixed = mixed_ref[...]
    scale = norm_scale(mixed)
    inner = jnp.mean(mixed * out_ref[...] * gain_ref[...], axis=-1, keepdims=True)
    slope = scale * scale * scale * inner

    def place(step):
        lanes = columns(step, width)
        grad, value = out_ref[:, lanes], mixed_ref[:, lanes]
        dgain_ref[:, lanes] = jnp.sum(grad * value * scale, axis=0, keepdims=True)
        total = grad_ref[:, lanes] + scale * (grad * gain_ref[:, lanes]) - value * slope
        out_ref[:, lanes] = total
        branch_ref[rows_at(me, rows), lanes] = (residual_scale * total).astype(bf16)

    spread_rows(rows, steps, width, place, branch_ref, sems)


def mlp_back(grad_both, gate_up, mixed, grad_out, gain):
    if lax.axis_size("shard") != 4:
        grad = plain_scatter(contract_cols(grad_both, gate_up))
        back, dgain = norm_back(mixed, norm_scale(mixed), gain, grad)
        grad_mixed = grad_out + back
        return grad_mixed, dgain[None], plain_gather((residual_scale * grad_mixed).astype(bf16))
    rows = mixed.shape[0]
    steps = D // MODEL_STEP
    return comm_call(
        mlp_back_kernel, "mlp_back", 5, [grad_both, gate_up, mixed, grad_out, gain[None]],
        [shape(rows, D, f32), shape(1, D, f32), shape(4 * rows, D, bf16)],
        exchange_scratch(rows, steps, MODEL_STEP) + [pltpu.SemaphoreType.DMA((3, 2, steps))],
        flops=2 * grad_both.size * D,
    )


LATENT_STEP = 256


def latent_back_kernel(gq_ref, gkv_ref, gsh_ref, qup_ref, lup_ref, out_ref, *scratch):
    rows = out_ref.shape[0]
    width = LATENT_STEP
    me, core, sib, far = partners()
    greet([{"shard": sib}, {"shard": far}])

    def partial(where, step):
        if step < QRANK // width:
            return contract_cols(gq_ref[where, :], qup_ref[step * width:(step + 1) * width, :])
        if step == QRANK // width:
            return contract_cols(gkv_ref[where, :], lup_ref[...])
        shared = gsh_ref[where, :]
        return jnp.concatenate([shared, jnp.zeros_like(shared)], axis=1)

    def use(step, total):
        out_ref[:, step * width:(step + 1) * width] = total

    sum_scatter(rows, out_ref.shape[1] // width, True, partial, scratch, use)


def latent_back(grad_query, grad_keyval, grad_shared, query_up, latent_up):
    if lax.axis_size("shard") != 4:
        return plain_scatter(
            jnp.concatenate(
                [contract_cols(grad_query, query_up), contract_cols(grad_keyval, latent_up), grad_shared],
                axis=1,
            )
        )
    rows = grad_query.shape[0] // 4
    steps = QRANK // LATENT_STEP + 2
    (out,) = comm_call(
        latent_back_kernel, "latent_back", 6, [grad_query, grad_keyval, grad_shared, query_up, latent_up],
        [shape(rows, steps * LATENT_STEP, f32)], exchange_scratch(rows, steps, LATENT_STEP),
        flops=2 * grad_query.size * QRANK + 2 * grad_keyval.size * KVRANK,
    )
    return out


def any_space(count):
    return [pl.BlockSpec(memory_space=pl.ANY)] * count


def pair(value, index):
    return value.at[0, index], value.at[1, index]


def send_to(source, target, sems, index, device):
    send, receive = pair(sems, index)
    return pltpu.make_async_remote_copy(
        src_ref=source, dst_ref=target, send_sem=send, recv_sem=receive,
        device_id={"shard": device}, device_id_type=MESH,
    )


def move_kernel(whole, split, *refs):
    amount = whole + len(split)
    inputs, outputs, (sems, local) = refs[:amount], refs[amount:2 * amount], refs[2 * amount:]
    me, core, sib, far = partners()
    diagonal = far + 1 - 2 * core
    greet([{"shard": sib}, {"shard": far}, {"shard": diagonal}])
    waits, forwards, keeps = [], [], []
    number = 0
    for i, (source, target) in enumerate(zip(inputs, outputs)):
        if i < whole:
            to_far = send_to(source, target.at[me], sems, number, far)
            to_sib = send_to(source, target.at[me], sems, number + 1, sib)
            onward = send_to(target.at[far], target.at[far], sems, number + 2, sib)
            to_far.start()
            to_sib.start()
            forwards.append((to_far, onward))
            waits.append(to_sib)
            kept = source
        else:
            part = split[i - whole]
            for j, device in enumerate((far, diagonal, sib)):
                copy = send_to(part(source, device), target.at[me], sems, number + j, device)
                copy.start()
                waits.append(copy)
            kept = part(source, me)
        number += 3
        keep = pltpu.make_async_copy(kept, target.at[me], local.at[i])
        keep.start()
        keeps.append(keep)
    for to_far, onward in forwards:
        to_far.wait_recv()
        onward.start()
    for to_far, onward in forwards:
        to_far.wait_send()
        onward.wait()
    for copy in waits:
        copy.wait()
    for keep in keeps:
        keep.wait()


def move(name, number, wholes, splits):
    inputs = list(wholes) + [array for array, _, _ in splits]
    shapes = [w.shape for w in wholes] + [part for _, part, _ in splits]
    out_shape = [jax.ShapeDtypeStruct((4,) + tuple(sh), v.dtype) for sh, v in zip(shapes, inputs)]
    return pl.pallas_call(
        functools.partial(move_kernel, len(wholes), [f for _, _, f in splits]),
        in_specs=any_space(len(inputs)),
        out_specs=any_space(len(inputs)),
        out_shape=out_shape,
        scratch_shapes=[pltpu.SemaphoreType.DMA((2, 3 * len(inputs))), pltpu.SemaphoreType.DMA((len(inputs),))],
        compiler_params=pltpu.CompilerParams(collective_id=number, has_side_effects=True),
        cost_estimate=pl.CostEstimate(
            flops=0, bytes_accessed=sum(4 * v.size * v.dtype.itemsize for v in inputs), transcendentals=0
        ),
        name=name,
    )(*inputs)


QUERY_WINDOW = 1024


def query_window(ref, owner):
    return ref.at[:, pl.ds(pl.multiple_of(owner // 2 * 1920 + owner % 2 * 896, LANES), QUERY_WINDOW)]


def latent_window(ref, owner):
    return ref.at[:, pl.ds(pl.multiple_of(owner * 1280, LANES), 1280)]


def first_move(query_down, latent_down, query_up, latent_up, segments, count):
    if count != 4:
        return (
            plain_gather(query_down), plain_gather(latent_down), pad_heads(spread(query_up, count)),
            spread(latent_up, count), plain_gather(segments),
        )
    down_q, down_kv, groups, up_q, up_kv = move(
        "first_move", 7, [query_down, latent_down, segments],
        [(query_up, (query_up.shape[0], QUERY_WINDOW), query_window),
         (latent_up, (latent_up.shape[0], 1280), latent_window)],
    )
    merge = lambda value: value.reshape((-1,) + value.shape[2:])
    up_q = lax.dynamic_slice_in_dim(merge(up_q), lax.axis_index("shard") % 2 * 64, 960, 1)
    return merge(down_q), merge(down_kv), pad_heads(up_q), merge(up_kv), merge(groups)


def row_block(rows):
    return lambda ref, owner: ref.at[pl.ds(pl.multiple_of(owner * rows, 16), rows), :]


def last_move(grad_lat, gain_terms, query_part, latent_part, count):
    if count != 4:
        return (
            plain_gather(grad_lat), plain_gather(gain_terms), collect(cut_heads(query_part), count),
            collect(latent_part, count),
        )
    rows_q, rows_kv = query_part.shape[0] // 4, latent_part.shape[0] // 4
    lat, got_gains, got_q, got_kv = move(
        "last_move", 8, [grad_lat, gain_terms],
        [(query_part, (rows_q, query_part.shape[1]), row_block(rows_q)),
         (latent_part, (rows_kv, latent_part.shape[1]), row_block(rows_kv))],
    )
    side = lambda value: value.transpose(1, 0, 2).reshape(value.shape[1], -1)
    return lat.reshape(-1, lat.shape[2]), got_gains.reshape(4, -1), cut_heads(side(got_q)), side(got_kv)


def place_kernel(width, own, beside, gf, gf2, gd, gd2, uf, uf2, ud, ud2, gate_ref, up_ref):
    me, core, sib, far = partners()
    gate_ref[...] = jnp.zeros_like(gate_ref)
    up_ref[...] = jnp.zeros_like(up_ref)

    def lanes(owner):
        return pl.ds(pl.multiple_of(owner // 2 * 3200 + owner % 2 * 1536, LANES), width)

    for owner, part in ((me, own), (sib, beside)):
        gate_ref[:, lanes(owner)] += part[:, :width].astype(f32)
        up_ref[:, lanes(owner)] += part[:, width:].astype(f32)
    diagonal = far + 1 - 2 * core
    for owner, gate, gate2, up, up2 in ((far, gf, gf2, uf, uf2), (diagonal, gd, gd2, ud, ud2)):
        gate_ref[:, lanes(owner)] += gate[...].astype(f32) + gate2[...].astype(f32)
        up_ref[:, lanes(owner)] += up[...].astype(f32) + up2[...].astype(f32)


def head_lanes(value):
    return jnp.pad(value, ((0, 0), (NOPE, LANES - NOPE - ROPE)))


def layer_forward(hidden, own_tables, tables, gains, weights, passing, hidden_weights):
    input_gain, query_gain, latent_gain, post_gain = gains
    down_both, query_up, latent_up, output_weight = weights[:4]
    scale_in = norm_scale(hidden)
    normed = (hidden * scale_in * input_gain).astype(bf16)
    down_q, down_kv = down_both
    latent_q = project(normed, down_q)
    latent_kv = project(normed, down_kv)
    latent = latent_kv[:, :KVRANK]
    scale_q = norm_scale(latent_q)
    scale_kv = norm_scale(latent)
    own_in = jnp.concatenate(
        [
            latent_q * scale_q * query_gain,
            latent * scale_kv * latent_gain,
            head_lanes(rotate(latent_kv[:, KVRANK:], *own_tables)),
        ],
        axis=1,
    ).astype(bf16)
    all_in = gather(own_in, 0, 384)
    all_in, finish = hidden_weights(all_in)
    query_in = all_in[:, :QRANK]
    kv_in = all_in[:, QRANK:QRANK + KVRANK]
    shared = all_in[:, QRANK + KVRANK:]
    attended, queries, keyval, logs = attend(
        project(query_in, query_up), project(kv_in, latent_up), shared, tables
    )
    attended, gate_up = finish(attended)
    mixed, normed_two = output_norm(attended, output_weight, hidden, post_gain)
    both = project(normed_two, gate_up)
    width = both.shape[1] // 2
    gate, up = both[:, :width], both[:, width:]
    activated = (jax.nn.silu(gate) * up).astype(bf16)
    def outputs(order=lambda value: value):
        return down_project(order(activated), weights[4], mixed, passing)

    kept = (hidden, scale_in, normed, latent_q, scale_q, latent, scale_kv, query_in, kv_in,
            shared, queries, keyval, logs, attended, mixed, normed_two, gate, up)
    return (outputs, kept, gate_up)


def gate_backward(grad_act, gate, up):
    sigmoid = jax.nn.sigmoid(gate)
    grad_gate = (grad_act * up * sigmoid * (1.0 + gate * (1.0 - sigmoid))).astype(bf16)
    grad_up = (grad_act * gate * sigmoid).astype(bf16)
    return jnp.concatenate([grad_gate, grad_up], axis=1)


def mlp_backward(grad_out, kept, gains, weights):
    mixed, gate, up = kept[14], kept[16], kept[17]
    gate_up, down_weight = weights[4:]
    own_down = (residual_scale * grad_out).astype(bf16)
    grad_down = gather(own_down, 1, 512)
    grad_both = gate_backward(contract_cols(grad_down, down_weight), gate, up)
    grad_mixed, dgain_post, grad_branch = mlp_back(grad_both, gate_up, mixed, grad_out, gains[3])
    return own_down, grad_mixed, dgain_post[0], grad_branch


def attention_backward(grad_mixed, grad_branch, kept, own_tables, tables, gains, weights):
    (hidden, scale_in, normed, latent_q, scale_q, latent, scale_kv, query_in, kv_in,
     shared, queries, keyval, logs, attended, mixed, normed_two, gate, up) = kept
    input_gain, query_gain, latent_gain, post_gain = gains
    down_both, query_up, latent_up, output_weight, gate_up, down_weight = weights
    cosine, sine = own_tables
    grad_attended = contract_cols(grad_branch, output_weight).astype(bf16)
    grad_query, grad_keyval, grad_shared = attend_back(
        queries, keyval, shared, tables, grad_attended, attended, logs
    )
    grad_in = latent_back(grad_query, grad_keyval, grad_shared, query_up, latent_up)
    grad_latent_q, dgain_query = norm_back(latent_q, scale_q, query_gain, grad_in[:, :QRANK])
    grad_latent, dgain_latent = norm_back(
        latent, scale_kv, latent_gain, grad_in[:, QRANK:QRANK + KVRANK]
    )
    start = QRANK + KVRANK + NOPE
    grad_shared = rotate(grad_in[:, start:start + ROPE], cosine, -sine)
    grad_lat = jnp.concatenate(
        [grad_latent_q, grad_latent, jnp.pad(grad_shared, ((0, 0), (0, LANES - ROPE)))], axis=1
    ).astype(bf16)
    down_q, down_kv = down_both
    grad_normed = contract_cols(grad_lat[:, :QRANK], down_q) + contract_cols(
        grad_lat[:, QRANK:QRANK + KVRANK + ROPE], down_kv
    )
    grad_hidden_norm, dgain_input = norm_back(hidden, scale_in, input_gain, grad_normed)
    grad_hidden = grad_mixed + grad_hidden_norm
    found = (grad_branch, grad_query, grad_keyval, grad_lat)
    return (grad_hidden, found, (dgain_input, dgain_query, dgain_latent))


def spread(weight, count):
    rows, columns = weight.shape
    parts = weight.reshape(rows, count, columns // count).transpose(1, 0, 2)
    return lax.all_to_all(parts, "shard", 0, 0, tiled=True).reshape(rows * count, columns // count)


def collect(grad, count):
    rows, columns = grad.shape
    parts = lax.all_to_all(
        grad.reshape(count, rows // count, columns), "shard", 0, 0, tiled=True
    )
    return parts.transpose(1, 0, 2).reshape(rows // count, columns * count)


def pad_heads(weight):
    rows, columns = weight.shape
    heads = weight.reshape(rows, columns // (NOPE + ROPE), NOPE + ROPE)
    return jnp.pad(heads, ((0, 0), (0, 0), (0, LANES - NOPE - ROPE))).reshape(rows, -1)


def cut_heads(grad):
    rows, columns = grad.shape
    heads = grad.reshape(rows, columns // LANES, LANES)[:, :, :NOPE + ROPE]
    return heads.reshape(rows, -1)


def swap(value, step):
    count = lax.axis_size("shard")
    return lax.ppermute(value, "shard", [(source, source ^ step) for source in range(count)])


def hidden_window(count):
    size = FF // count
    width = -(-size // LANES) * LANES
    starts = [owner * size // LANES * LANES for owner in range(count)]
    starts = [min(start, FF - width) for start in starts]
    return size, width, starts, [owner * size - start for owner, start in enumerate(starts)]


def take_at(table, place):
    return jnp.asarray(table, jnp.int32)[place]


def shared_links(count):
    return count == 4 and lax.axis_size("rep") % 2 == 0


def relay_pairs(count):
    reps = lax.axis_size("rep")
    places = [(rep, own) for rep in range(reps) for own in range(count)]
    number = lambda rep, own: rep * count + own
    same = [(number(r, o), number(r, o ^ 2)) for r, o in places if o % 2 == r % 2]
    other = [(number(r, o), number(r, o ^ 3)) for r, o in places if o % 2 != r % 2]
    beside = [(number(r, o), number(r ^ 1, o)) for r, o in places if o % 2 == r % 2]
    return same, other, beside


def relay(value, count):
    *across, beside = relay_pairs(count)
    direct = [lax.ppermute(value, ("rep", "shard"), way) for way in across]
    return [(part, lax.ppermute(part, ("rep", "shard"), beside)) for part in direct]


def relay_owner(me):
    return (me // 2 * 2 + 2) % 4 + lax.axis_index("rep") % 2


def spread_hidden(gate, up, count):
    me = lax.axis_index("shard")
    size, width, starts, offsets = hidden_window(count)
    rows = gate.shape[0]
    whole = jnp.zeros((rows * count, 2 * width), bf16)
    for step in range(count):
        owner = me ^ step
        begin = take_at(starts, owner)
        part = jnp.concatenate(
            [lax.dynamic_slice(gate, (0, begin), (rows, width)), lax.dynamic_slice(up, (0, begin), (rows, width))],
            axis=1,
        )
        if step:
            part = swap(part, step)
        whole = lax.dynamic_update_slice(whole, part, (owner * rows, 0))
    return whole


def relay_hidden(gate, up, count):
    me = lax.axis_index("shard")
    size, width, starts, offsets = hidden_window(count)
    rows = gate.shape[0]
    pairs = relay_pairs(count)
    windows = lambda owner: [
        lax.dynamic_slice(weight, (0, take_at(starts, owner)), (rows, width)) for weight in (gate, up)
    ]
    direct = [
        [lax.ppermute(part, ("rep", "shard"), way) for way in pairs[:2]] for part in windows(relay_owner(me))
    ]
    own = windows(me)
    beside = [swap(part, 1) for part in windows(me ^ 1)]

    def finish(value):
        value, *flat = together(value, *direct[0], *direct[1], *beside)
        whole = jnp.zeros((rows * count, 2 * width), bf16)
        for which in range(2):
            far = [part + lax.ppermute(part, ("rep", "shard"), pairs[2]) for part in flat[2 * which:2 * which + 2]]
            for step, part in enumerate((own[which], flat[4 + which], *far)):
                whole = lax.dynamic_update_slice(whole, part, ((me ^ step) * rows, which * width))
        return value, whole

    return finish


def window_rows(down, count):
    size, width, starts, offsets = hidden_window(count)
    whole = jnp.zeros((width, down.shape[1]), bf16)
    return lax.dynamic_update_slice(whole, down, (take_at(offsets, lax.axis_index("shard")), 0))


def window_gradients(two_all, grad_both, count):
    me = lax.axis_index("shard")
    width = grad_both.shape[1] // 2
    rows = D // count

    def part(owner, grad):
        left = lax.dynamic_slice(two_all, (0, owner * rows), (two_all.shape[0], rows))
        return contract_rows(left, grad).astype(bf16)

    if shared_links(count):
        owner = relay_owner(me)
        return [part(owner, grad_both[:, :width]), part(owner, grad_both[:, width:]), part(me ^ 1, grad_both), part(me, grad_both)]
    return [part(me ^ step, grad_both) for step in reversed(range(count))]


def send_windows(parts, count):
    if shared_links(count):
        gate, up, beside, own = parts
        return [own, swap(beside, 1), *(relay(gate, count)), *(relay(up, count))]
    return [parts[-1]] + [swap(parts[count - 1 - step], step) for step in range(1, count)]


def place_windows(parts, count):
    size, width, starts, offsets = hidden_window(count)
    rows = parts[0].shape[0]
    if shared_links(count):
        own, beside, gate_far, gate_diagonal, up_far, up_diagonal = parts
        inputs = [own, beside, *gate_far, *gate_diagonal, *up_far, *up_diagonal]
        tile = 64
        return pl.pallas_call(
            functools.partial(place_kernel, width),
            grid=(rows // tile,),
            in_specs=[pl.BlockSpec((tile, v.shape[1]), lambda i: (i, 0)) for v in inputs],
            out_specs=[pl.BlockSpec((tile, FF), lambda i: (i, 0))] * 2,
            out_shape=[jax.ShapeDtypeStruct((rows, FF), f32)] * 2,
            compiler_params=pltpu.CompilerParams(vmem_limit_bytes=VMEM_LIMIT),
            name="place_windows",
        )(*inputs)
    me = lax.axis_index("shard")
    gathered = jnp.zeros((count, rows, 2 * width), bf16)
    for step, part in enumerate(parts):
        gathered = lax.dynamic_update_slice(gathered, part[None], (me ^ step, 0, 0))
    totals = []
    for which in range(2):
        pieces = []
        for owner in range(count):
            offset = which * width + offsets[owner]
            pieces.append(gathered[owner, :, offset:offset + size])
        totals.append(jnp.concatenate(pieces, axis=1).astype(f32))
    return totals


def together(*values):
    return lax.optimization_barrier(values)


def body(tokens, segment_ids, input_gain, query_gain, latent_gain, post_gain, query_down, query_up,
         latent_down, latent_up, output_weight, gate_weight, up_weight, down_weight, cotangent):
    at_start = lax.axis_index("section") == 0
    count = lax.axis_size("shard")
    size, width, starts, offsets = hidden_window(count)
    gains = (input_gain[0], query_gain[0], latent_gain[0], post_gain[0])
    down_q, down_kv, query_up_all, latent_up_all, groups = first_move(
        query_down[0], latent_down[0], query_up[0], latent_up[0], segment_ids, count
    )
    down_both = (down_q, down_kv)
    down_rows = window_rows(down_weight[0], count)
    weights = (down_both, query_up_all, latent_up_all, output_weight[0], down_rows)
    own_tables = tuple(t.reshape(-1, ROPE // 2) for t in slot_tables(segment_ids))
    tables = head_tables(groups)

    def first_weights(all_in):
        all_in, gate, up = together(all_in, gate_weight[0], up_weight[0])
        if shared_links(count):
            return all_in, relay_hidden(gate, up, count)
        whole = spread_hidden(gate, up, count)
        return all_in, lambda value: (value, whole)

    start = tokens.astype(f32)
    outputs, _, gate_up = layer_forward(start, own_tables, tables, gains, weights, True, first_weights)
    leaving, low, received = outputs()
    received, last = together(received, cotangent)
    last = last.astype(f32)
    entering = jnp.where(at_start, start, received.astype(f32))
    outputs, kept, _ = layer_forward(
        entering, own_tables, tables, gains, weights, False, lambda all_in: (all_in, lambda value: (value, gate_up))
    )
    weights = weights[:4] + (gate_up, down_rows)

    (hidden, scale_in, normed, latent_q, scale_q, latent, scale_kv, query_in, kv_in,
     shared, queries, keyval, logs, attended, mixed, normed_two, gate, up) = kept
    rows = hidden.shape[0]
    _, grad_mixed, _, grad_branch = mlp_backward(last, kept, gains, weights)
    own_two = lax.dynamic_slice_in_dim(normed_two, lax.axis_index("shard") * rows, rows, 0)
    grad_branch, own_two = together(grad_branch, own_two)
    two_all = lax.all_gather(own_two, ("rep", "shard"), axis=0, tiled=True)
    grad, _, _ = attention_backward(grad_mixed, grad_branch, kept, own_tables, tables, gains, weights)
    returned = lax.ppermute(grad.astype(bf16), "section", [(1, 0)])
    incoming = jnp.where(at_start, returned.astype(f32), last)

    own_down, grad_mixed, dgain_post, grad_branch = mlp_backward(incoming, kept, gains, weights)
    grad_branch, own_down, two_all = together(grad_branch, own_down, two_all)
    down_all = lax.all_gather(own_down, ("rep", "shard"), axis=0, tiled=True)
    part_output = contract_rows(attended, grad_branch).astype(bf16)
    grad_branch, part_output = together(grad_branch, part_output)
    total_output = lax.psum(part_output, "rep")

    grad, found, (dgain_input, dgain_query, dgain_latent) = attention_backward(
        grad_mixed, grad_branch, kept, own_tables, tables, gains, weights
    )
    grad_branch, grad_query, grad_keyval, grad_lat = found
    gain_terms = jnp.concatenate([dgain_input, dgain_query, dgain_latent, dgain_post])[None]
    normed_rows = lax.all_to_all(
        normed.reshape(normed.shape[0], count, -1).transpose(1, 0, 2), "shard", 0, 0, tiled=True
    ).reshape(normed.shape[0] * count, -1)
    part_query = contract_rows(query_in, grad_query).astype(bf16)
    part_latent = contract_rows(kv_in, grad_keyval).astype(bf16)
    lat_all, gains_all, part_query, part_latent = last_move(
        grad_lat, gain_terms, part_query, part_latent, count
    )
    part_down = contract_rows(normed_rows, lat_all[:, :QRANK + KVRANK + ROPE]).astype(bf16)
    part_gains = jnp.sum(gains_all, axis=0).astype(bf16)
    part_down, part_query, part_latent, down_all = together(part_down, part_query, part_latent, down_all)
    part_down, total_output = together(part_down, total_output)
    side = part_down.shape[1]
    gain_rows = -(-part_gains.shape[0] // side)
    part_gains = jnp.pad(part_gains, (0, gain_rows * side - part_gains.shape[0])).reshape(gain_rows, side)
    part_down = jnp.concatenate([part_down, part_gains], axis=0)
    total_down_both, total_query, total_latent = (
        part.astype(f32) for part in lax.psum((part_down, part_query, part_latent), "rep")
    )
    gain_totals = total_down_both[-gain_rows:].reshape(-1)
    total_down_both = total_down_both[:-gain_rows]

    both = project(two_all, gate_up)
    gate_all, up_all = both[:, :width], both[:, width:]
    activated_all = (jax.nn.silu(gate_all) * up_all).astype(bf16)
    grad_both = gate_backward(contract_cols(down_all, down_rows), gate_all, up_all)
    payloads = window_gradients(two_all, grad_both, count)
    activated_all, *payloads = together(activated_all, *payloads)
    hidden_parts = send_windows(payloads, count)
    total_down = contract_rows(activated_all, down_all)
    offset = take_at(offsets, lax.axis_index("shard"))
    total_down = lax.dynamic_slice_in_dim(total_down, offset, size, 0)
    leaving, boundary = outputs(lambda value: together(value, total_down)[0])
    total_gate, total_up = place_windows(hidden_parts, count)
    first, second, third = D, D + QRANK, D + QRANK + KVRANK
    gain_totals = (gain_totals[:first], gain_totals[first:second], gain_totals[second:third], gain_totals[third:third + D])
    return (
        boundary[None],
        grad[None],
        gain_totals[0][None],
        gain_totals[1][None],
        gain_totals[2][None],
        gain_totals[3][None],
        total_down_both[None, :, :QRANK],
        total_query[None],
        total_down_both[None, :, QRANK:],
        total_latent[None],
        total_output.astype(f32)[None],
        total_gate[None],
        total_up[None],
        total_down[None],
    )


def solution(mesh):
    tokens = P(("rep", "shard"), None)
    gain = P("section", None)
    weight = P("section", "shard", None)
    out = P("section", ("rep", "shard"), None)
    return jax.shard_map(
        body,
        mesh=mesh,
        in_specs=(tokens, tokens) + (gain,) * 4 + (weight,) * 8 + (tokens,),
        out_specs=(out, out) + (gain,) * 4 + (weight,) * 8,
        check_vma=False,
    )
```

time: 1990 us -> 1460 us (0.73)
  waiting for transfers between devices: 884 us -> 192 us
  Pallas kernels: 134 us -> 659 us
  blocking collectives: 157 us -> 0 us
  matrix products: 460 us -> 340 us
  local copies, waits for them, and re-layouts: 168 us -> 97.9 us
    pallas_call x0 -> x15, Pallas kernels: none -> 614 us  [the longest x12 462 us: comm_call(): pl.pallas_call(kernel, in_specs=vmem(len(inputs)), out_specs=vmem(len(out...]
    reduce_scatter x8 -> x0, waiting for transfers between devices: 293 us -> none  [scatter(): lax.psum_scatter(value.astype(bf16), 'shard', scatter_dimension=0, tiled=...]
    all_gather x10 -> x0, waiting for transfers between devices: 212 us -> none  [gather(): return lax.all_gather(value, 'shard', axis=0, tiled=True)]
    all_to_all x8 -> x0, waiting for transfers between devices: 196 us -> none  [the longest x4 158 us: spread(): lax.all_to_all(parts, 'shard', 0, 0, tiled=True)]
    psum x1 -> x0, blocking collectives: 132 us -> none  [body(): gain_totals = lax.psum(gain_terms, ('rep', 'shard'))]
    psum x1 -> x2, waiting for transfers between devices: 0.01 us -> 99.3 us  [the longest x1 99.3 us: body(): lax.psum((part_down, part_query, part_latent), 'rep')]
    all_gather x1, waiting for transfers between devices: 89.4 us -> 0.02 us  [body(): two_all = lax.all_gather(own_two, ('rep', 'shard'), axis=0, tiled=True)]
    unnamed x95 -> x114, local copies, waits for them, and re-layouts: 65.8 us -> 9.93 us
  transfers between devices with their start and end apart: 32 -> 25, of which waited for: 23 -> 5; matrix products, arithmetic and copies ran while one was open for 24% -> 28% of each run, Pallas kernels for 0% -> 23%
where the time goes in v2:
time: 1460 us; the launch traced here: 1450 us
  Pallas kernels  659 us (45%)
  matrix products  340 us (23%)
  waiting for transfers between devices  192 us (13%)
  local copies, waits for them, and re-layouts  97.9 us (7%)
  other arithmetic  76.6 us (5%)
  starting transfers between devices  59.3 us (4%)
  between operations  23.3 us (2%)
    pallas_call x12, Pallas kernels, comm_call(): pl.pallas_call(kernel, in_specs=vmem(len(inputs)), out_specs=vmem(len(out...  462 us
    pallas_call x2, Pallas kernels, move(): pl.pallas_call(functools.partial(move_kernel, len(wholes), [f for _, _, f...  129 us
    dot_general x11, matrix products, project(): return jnp.dot(left, weight, preferred_element_type=f32)  126 us
    dot_general x9, matrix products, contract_rows(): lax.dot_general(left, right, (((0,), (0,)), ((), ())), preferred_element_...  113 us
    dot_general x9, matrix products, contract_cols(): lax.dot_general(left, right, (((1,), (1,)), ((), ())), preferred_element_...  100 us
    psum x1, waiting for transfers between devices, body(): lax.psum((part_down, part_query, part_latent), 'rep')  99.3 us
    ppermute x4, waiting for transfers between devices, relay(): direct = [lax.ppermute(value, ('rep', 'shard'), way) for way in across]  37.7 us
  transfers between devices with their start and end apart: 25, of which 5 were waited for; matrix products, arithmetic and copies ran while one was open for 28% of the time, Pallas kernels for 23%

profile of v2, /device:TPU:1, one launch (start us, length us, event | category | flops | bytes accessed | tf_op | source)
XLA Modules:
  0.0 1448.5 jit_solution(723291546427774245)
XLA Ops:
  17.8 65.7 %first_move.1 = (bf16[4,640,768]{2,1,0:T(8,128)(2,1)}, bf16[4,640,288]{2,1,0:T(8,128)(2,1)}, s32[4,2,96]{2,1,0:T(2,128)}, bf16[4,192,1024]{2,1,0:T(8,128)(2,1)}, bf16[4,64,1280]{2,1,0:T(8,128)(2,1)}) custom-call(bf16[640,768]{1,0:T(8,128)(2,1)} %bitcast.124, bf16[640,288]{1,0:T(8,128)(2,1)} %bitcast.120, s32[2,96]{1,0:T(2,128)} %refs_2_.1, ...), custom_call_target="tpu_custom_call" | custom-call | bytes 13929472 | tf_op jit(solution)/shard_map/first_move/pallas_call | solution.py:693
  150.4 19.8 %collective-permute-start.5 = (bf16[640,1664]{1,0:T(8,128)(2,1)}, bf16[640,1664]{1,0:T(8,128)(2,1)}, u32[]{:S(2)}, u32[]{:S(2)}) collective-permute-start(bf16[640,1664]{1,0:T(8,128)(2,1)} %get-tuple-element.236), channel_id=1, source_target_pairs={{0,1},{1,0},{2,3},{3,2},{4,5},{5,4},{6,7},{7,6},{8,9},{9,8},{10,11... | collective-permute-start | bytes 6389768 | tf_op jit(solution)/shard_map/ppermute | solution.py:891
  192.4 23.2 %collective-permute-done.3 = bf16[640,1664]{1,0:T(8,128)(2,1)} collective-permute-done((bf16[640,1664]{1,0:T(8,128)(2,1)}, bf16[640,1664]{1,0:T(8,128)(2,1)}, u32[]{:S(2)}, u32[]{:S(2)}) %collective-permute-start.3) | collective-permute-done | bytes 2129952 | tf_op jit(solution)/shard_map/ppermute | solution.py:957
  236.7 63.6 %output_norm.2 = (f32[192,2560]{1,0:T(8,128)}, bf16[768,2560]{1,0:T(8,128)(2,1)}) custom-call(bf16[768,640]{1,0:T(8,128)(2,1)} %get-tuple-element.87.att_ref, bf16[640,2560]{1,0:T(8,128)(2,1)} %bitcast.141, f32[192,2560]{1,0:T(8,128)} %convert_element_type.133.hidden_ref, f32[1,2560]{1,0:T(1,128)} %gain_ref.7), custom_call_target="tpu_custom_call" | custom-call | flops 2516582400 | bytes 12134400 | tf_op jit(solution)/shard_map/output_norm/pallas_call | solution.py:397
  344.1 42.1 %down_project.2 = (f32[192,2560]{1,0:T(8,128)}, bf16[192,2560]{1,0:T(8,128)(2,1)}, bf16[192,2560]{1,0:T(8,128)(2,1)}) custom-call(bf16[768,1664]{1,0:T(8,128)(2,1)} %fusion.4.act_ref, bf16[1664,2560]{1,0:T(8,128)(2,1)} %bitcast_dynamic-update-slice_fusion.weight_ref, f32[192,2560]{1,0:T(8,128)} %get-tuple-element.95.mixed_ref), custom_call_target="tpu_custom_call" | custom-call | flops 6543114240 | bytes 16973824 | tf_op jit(solution)/shard_map/down_project/pallas_call | solution.py:397
  434.0 56.1 %output_norm.3 = (f32[192,2560]{1,0:T(8,128)}, bf16[768,2560]{1,0:T(8,128)(2,1)}) custom-call(bf16[768,640]{1,0:T(8,128)(2,1)} %get-tuple-element.98.att_ref, bf16[640,2560]{1,0:T(8,128)(2,1)} %bitcast.142, f32[192,2560]{1,0:T(8,128)} %copy-done, f32[1,2560]{1,0:T(1,128)} %gain_ref.7), custom_call_target="tpu_custom_call" | custom-call | flops 2516582400 | bytes 12134400 | tf_op jit(solution)/shard_map/output_norm/pallas_call | solution.py:397
  490.1 21.6 %fusion.92 = f32[768,3328]{1,0:T(8,128)} fusion(bf16[768,2560]{1,0:T(8,128)(2,1)} %get-tuple-element.99, bf16[2560,3328]{1,0:T(8,128)(2,1)} %add_dynamic-update-slice_fusion.weight_ref), kind=kOutput, calls=%fused_computation.204 | convolution fusion | flops 13086228480 | bytes 31195136 | tf_op jit(solution)/shard_map/dot_general | solution.py:82
  511.6 28.5 %gather_rows.6 = bf16[768,2560]{1,0:T(8,128)(2,1)} custom-call(bf16[192,2560]{1,0:T(8,128)(2,1)} %multiply_convert_fusion.9.own_ref), custom_call_target="tpu_custom_call" | custom-call | bytes 4915200 | tf_op jit(solution)/shard_map/gather_rows/pallas_call | solution.py:397
  559.6 63.0 %mlp_back.2 = (f32[192,2560]{1,0:T(8,128)}, f32[1,2560]{1,0:T(1,128)}, bf16[768,2560]{1,0:T(8,128)(2,1)}) custom-call(bf16[768,3328]{1,0:T(8,128)(2,1)} %pad_maximum_fusion.7.both_ref, bf16[2560,3328]{1,0:T(8,128)(2,1)} %add_dynamic-update-slice_fusion.weight_ref, f32[192,2560]{1,0:T(8,128)} %get-tuple-element.101.mixed_ref, ...), custom_call_target="tpu_custom_call" | custom-call | flops 13086228480 | bytes 32002048 | tf_op jit(solution)/shard_map/mlp_back/pallas_call | solution.py:397
  644.2 19.3 %latent_back.2 = f32[192,1280]{1,0:T(8,128)} custom-call(bf16[768,1280]{1,0:T(8,128)(2,1)} %get-tuple-element.108.gq_ref, bf16[768,1280]{1,0:T(8,128)(2,1)} %get-tuple-element.109.gkv_ref, f32[768,128]{1,0:T(8,128)} %get-tuple-element.110.gsh_ref, bf16[768,1280]{1,0:T(8,128)(2,1)} %copy.111.qup_ref, bf16[256,1280]{1,0:T(8,128)(2,1)} %bitcast.104), custom_call_target="tpu_custom_call" | custom-call | flops 2013265920 | bytes 7929856 | tf_op jit(solution)/shard_map/latent_back/pallas_call | solution.py:397
  676.0 23.0 %collective-permute-done.10 = bf16[192,2560]{1,0:T(8,128)(2,1)S(1)} collective-permute-done((bf16[192,2560]{1,0:T(8,128)(2,1)S(1)}, bf16[192,2560]{1,0:T(8,128)(2,1)S(1)}, u32[]{:S(2)}, u32[]{:S(2)}) %collective-permute-start.10) | collective-permute-done | bytes 983072 | tf_op jit(solution)/shard_map/ppermute | solution.py:1077
  701.0 38.5 %gather_rows.7 = bf16[768,2560]{1,0:T(8,128)(2,1)} custom-call(bf16[192,2560]{1,0:T(8,128)(2,1)} %get-tuple-element.123.own_ref), custom_call_target="tpu_custom_call" | custom-call | bytes 4915200 | tf_op jit(solution)/shard_map/gather_rows/pallas_call | solution.py:397
  760.6 62.5 %mlp_back.3 = (f32[192,2560]{1,0:T(8,128)}, f32[1,2560]{1,0:T(1,128)}, bf16[768,2560]{1,0:T(8,128)(2,1)}) custom-call(bf16[768,3328]{1,0:T(8,128)(2,1)} %pad_maximum_fusion.8.both_ref, bf16[2560,3328]{1,0:T(8,128)(2,1)} %add_dynamic-update-slice_fusion.weight_ref, f32[192,2560]{1,0:T(8,128)} %get-tuple-element.101.mixed_ref, ...), custom_call_target="tpu_custom_call" | custom-call | flops 13086228480 | bytes 32002048 | tf_op jit(solution)/shard_map/mlp_back/pallas_call | solution.py:397
  855.7 19.1 %latent_back.3 = f32[192,1280]{1,0:T(8,128)} custom-call(bf16[768,1280]{1,0:T(8,128)(2,1)} %get-tuple-element.116.gq_ref, bf16[768,1280]{1,0:T(8,128)(2,1)} %get-tuple-element.117.gkv_ref, f32[768,128]{1,0:T(8,128)} %get-tuple-element.118.gsh_ref, bf16[768,1280]{1,0:T(8,128)(2,1)} %copy.111.qup_ref, bf16[256,1280]{1,0:T(8,128)(2,1)} %bitcast.105), custom_call_target="tpu_custom_call" | custom-call | flops 2013265920 | bytes 7929856 | tf_op jit(solution)/shard_map/latent_back/pallas_call | solution.py:397
  893.1 63.2 %last_move.1 = (bf16[4,192,1152]{2,1,0:T(8,128)(2,1)}, f32[4,1,6144]{2,1,0:T(1,128)}, bf16[4,192,1280]{2,1,0:T(8,128)(2,1)}, bf16[4,64,1280]{2,1,0:T(8,128)(2,1)}) custom-call(bf16[192,1152]{1,0:T(8,128)(2,1)} %pad_maximum_fusion.10.refs_0_, f32[1,6144]{1,0:T(1,128)} %bitcast.127, bf16[768,1280]{1,0:T(8,128)(2,1)} %convolution_convert_fusion.1.refs_2_, ...), custom_call_target="tpu_custom_call" | custom-call | bytes 12353536 | tf_op jit(solution)/shard_map/last_move/pallas_call | solution.py:693
  975.7 63.1 %fusion.93 = f32[3072,3328]{1,0:T(8,128)} fusion(bf16[3072,2560]{1,0:T(8,128)(2,1)} %all-gather.3.cloned.1.call-done, bf16[2560,3328]{1,0:T(8,128)(2,1)} %add_dynamic-update-slice_fusion.weight_ref), kind=kOutput, calls=%fused_computation.205 | convolution fusion | flops 52344913920 | bytes 73662464 | tf_op jit(solution)/shard_map/dot_general | solution.py:82
  1042.9 45.9 %multiply_convert_fusion = (bf16[3072,1664]{1,0:T(8,128)(2,1)}, bf16[3072,1664]{1,0:T(8,128)(2,1)}, bf16[3072,1664]{1,0:T(8,128)(2,1)}) fusion(f32[3072,3328]{1,0:T(8,128)} %fusion.93, bf16[3072,2560]{1,0:T(8,128)(2,1)} %all-gather.5.cloned.1.call-done, bf16[1664,2560]{1,0:T(8,128)(2,1)} %bitcast_dynamic-update-slice_fusion.weight_ref), kind=kOutput, calls=%fused_computation.1 | convolution fusion | flops 26254245888 | bytes 95813632 | tf_op jit(solution)/shard_map/dot_general | solution.py:78
  1088.9 19.6 %fusion.2 = bf16[640,3328]{1,0:T(8,128)(2,1)} fusion(bf16[3072,1664]{1,0:T(8,128)(2,1)} %get-tuple-element.225, bf16[3072,1664]{1,0:T(8,128)(2,1)} %get-tuple-element.226, bf16[3072,2560]{1,0:T(8,128)(2,1)} %all-gather.3.cloned.1.call-done, s32[]{:T(128)S(6)} %select_n.124), kind=kOutput, calls=%fused_computation.8 | convolution fusion | flops 13129252864 | bytes 28639236 | tf_op jit(solution)/shard_map/dot_general | solution.py:74
  1108.5 20.0 %fusion.3.own = bf16[640,3328]{1,0:T(8,128)(2,1)} fusion(bf16[3072,1664]{1,0:T(8,128)(2,1)} %get-tuple-element.225, bf16[3072,1664]{1,0:T(8,128)(2,1)} %get-tuple-element.226, bf16[3072,2560]{1,0:T(8,128)(2,1)} %all-gather.3.cloned.1.call-done, s32[]{:T(128)S(6)} %select_n.123), kind=kOutput, calls=%fused_computation.9 | convolution fusion | flops 13129252864 | bytes 28639236 | tf_op jit(solution)/shard_map/dot_general | solution.py:74
  1161.9 34.6 %fusion.95 = f32[1664,2560]{1,0:T(8,128)} fusion(bf16[3072,1664]{1,0:T(8,128)(2,1)} %get-tuple-element.125, bf16[3072,2560]{1,0:T(8,128)(2,1)} %all-gather.5.cloned.1.call-done), kind=kOutput, calls=%fused_computation.207 | convolution fusion | flops 26172456960 | bytes 42991616 | tf_op jit(solution)/shard_map/dot_general | solution.py:74
  1207.3 37.7 %collective-permute-done.18.ud = bf16[640,1664]{1,0:T(8,128)(2,1)} collective-permute-done((bf16[640,1664]{1,0:T(8,128)(2,1)}, bf16[640,1664]{1,0:T(8,128)(2,1)}, u32[]{:S(2)}, u32[]{:S(2)}) %collective-permute-start.18) | collective-permute-done | bytes 2129952 | tf_op jit(solution)/shard_map/ppermute | solution.py:922
  1246.3 37.4 %down_project.3 = (f32[192,2560]{1,0:T(8,128)}, bf16[192,2560]{1,0:T(8,128)(2,1)}) custom-call(bf16[768,1664]{1,0:T(8,128)(2,1)} %get-tuple-element.126.act_ref, bf16[1664,2560]{1,0:T(8,128)(2,1)} %bitcast_dynamic-update-slice_fusion.weight_ref, f32[192,2560]{1,0:T(8,128)} %get-tuple-element.101.mixed_ref), custom_call_target="tpu_custom_call" | custom-call | flops 6543114240 | bytes 15990784 | tf_op jit(solution)/shard_map/down_project/pallas_call | solution.py:397
  1295.2 99.3 %all-reduce.12.cloned.1.call-done = (bf16[646,1056]{0,1:T(8,128)(2,1)}, bf16[1,192,3840]{2,1,0:T(8,128)(2,1)}, bf16[1,64,5120]{2,1,0:T(8,128)(2,1)}) async-done(((bf16[646,1056]{0,1:T(8,128)(2,1)}, bf16[1,192,3840]{2,1,0:T(8,128)(2,1)}, bf16[1,64,5120]{2,1,0:T(8,128)(2,1)}), (bf16[646,1056]{0,1:T(8,128)(2,1)}, bf16[1,192,3840]{2,1,0:T(8,128)(2,1)}, ...) | async-done | bytes 3494288 | tf_op jit(solution)/shard_map/psum | solution.py:1109
  1417.7 22.9 %place_windows.1 = (f32[640,6400]{1,0:T(8,128)}, f32[640,6400]{1,0:T(8,128)}) custom-call(bf16[640,3328]{1,0:T(8,128)(2,1)} %fusion.3.own, bf16[640,3328]{1,0:T(8,128)(2,1)} %collective-permute-done.11.beside, bf16[640,1664]{1,0:T(8,128)(2,1)} %collective-permute-done.12.gf, bf16[640,1664]{1,0:T(8,128)(2,1)} %collective-permute-done.13.gf2, ...), custom_call_target="tpu_custom_call" | custom-call | tf_op jit(solution)/shard_map/place_windows/pallas_call | solution.py:1009
  (322 shorter events, 435.6 us)
Async XLA Ops:
  7.2 816.0 %all-gather.3.cloned.1.call-start = ((), (), s32[]{:S(2)}) async-start(), calls=%async_computation.1 | async-start | bytes 16711680 | tf_op jit(solution)/shard_map/all_gather | solution.py:1075
  120.6 29.7 %collective-permute-start = (bf16[640,1664]{1,0:T(8,128)(2,1)}, bf16[640,1664]{1,0:T(8,128)(2,1)}, u32[]{:S(2)}, u32[]{:S(2)}) collective-permute-start(bf16[640,1664]{1,0:T(8,128)(2,1)} %get-tuple-element.235), channel_id=1, source_target_pairs={{0,2},{2,0},{5,7},{7,5},{8,10},{10,8},{13,15},{15,13},{16,18},{18,... | collective-permute-start | bytes 6389768 | tf_op jit(solution)/shard_map/ppermute | solution.py:957
  122.6 69.8 %collective-permute-start.1 = (bf16[640,1664]{1,0:T(8,128)(2,1)}, bf16[640,1664]{1,0:T(8,128)(2,1)}, u32[]{:S(2)}, u32[]{:S(2)}) collective-permute-start(bf16[640,1664]{1,0:T(8,128)(2,1)} %get-tuple-element.235), channel_id=1, source_target_pairs={{1,2},{3,0},{4,7},{6,5},{9,10},{11,8},{12,15},{14,13},{17,18},{19,... | collective-permute-start | bytes 6389768 | tf_op jit(solution)/shard_map/ppermute | solution.py:957
  132.2 60.2 %collective-permute-start.2 = (bf16[640,1664]{1,0:T(8,128)(2,1)}, bf16[640,1664]{1,0:T(8,128)(2,1)}, u32[]{:S(2)}, u32[]{:S(2)}) collective-permute-start(bf16[640,1664]{1,0:T(8,128)(2,1)} %get-tuple-element.237), channel_id=1, source_target_pairs={{0,2},{2,0},{5,7},{7,5},{8,10},{10,8},{13,15},{15,13},{16,18},{18,... | collective-permute-start | bytes 6389768 | tf_op jit(solution)/shard_map/ppermute | solution.py:957
  134.2 81.4 %collective-permute-start.3 = (bf16[640,1664]{1,0:T(8,128)(2,1)}, bf16[640,1664]{1,0:T(8,128)(2,1)}, u32[]{:S(2)}, u32[]{:S(2)}) collective-permute-start(bf16[640,1664]{1,0:T(8,128)(2,1)} %get-tuple-element.237), channel_id=1, source_target_pairs={{1,2},{3,0},{4,7},{6,5},{9,10},{11,8},{12,15},{14,13},{17,18},{19,... | collective-permute-start | bytes 6389768 | tf_op jit(solution)/shard_map/ppermute | solution.py:957
  136.8 78.8 %collective-permute-start.4 = (bf16[640,1664]{1,0:T(8,128)(2,1)}, bf16[640,1664]{1,0:T(8,128)(2,1)}, u32[]{:S(2)}, u32[]{:S(2)}) collective-permute-start(bf16[640,1664]{1,0:T(8,128)(2,1)} %get-tuple-element.234), channel_id=1, source_target_pairs={{0,1},{1,0},{2,3},{3,2},{4,5},{5,4},{6,7},{7,6},{8,9},{9,8},{10,11... | collective-permute-start | bytes 6389768 | tf_op jit(solution)/shard_map/ppermute | solution.py:891
  150.4 65.2 %collective-permute-start.5 = (bf16[640,1664]{1,0:T(8,128)(2,1)}, bf16[640,1664]{1,0:T(8,128)(2,1)}, u32[]{:S(2)}, u32[]{:S(2)}) collective-permute-start(bf16[640,1664]{1,0:T(8,128)(2,1)} %get-tuple-element.236), channel_id=1, source_target_pairs={{0,1},{1,0},{2,3},{3,2},{4,5},{5,4},{6,7},{7,6},{8,9},{9,8},{10,11... | collective-permute-start | bytes 6389768 | tf_op jit(solution)/shard_map/ppermute | solution.py:891
  215.6 84.8 %collective-permute-start.6 = (bf16[640,1664]{1,0:T(8,128)(2,1)}, bf16[640,1664]{1,0:T(8,128)(2,1)}, u32[]{:S(2)}, u32[]{:S(2)}) collective-permute-start(bf16[640,1664]{1,0:T(8,128)(2,1)} %collective-permute-done), channel_id=1, source_target_pairs={{0,4},{2,6},{5,1},{7,3},{8,12},{10,14},{13,9},{15,11},{16,20},{18,... | collective-permute-start | bytes 6389768 | tf_op jit(solution)/shard_map/ppermute | solution.py:966
  216.9 87.7 %collective-permute-start.7 = (bf16[640,1664]{1,0:T(8,128)(2,1)}, bf16[640,1664]{1,0:T(8,128)(2,1)}, u32[]{:S(2)}, u32[]{:S(2)}) collective-permute-start(bf16[640,1664]{1,0:T(8,128)(2,1)} %collective-permute-done.1), channel_id=1, source_target_pairs={{0,4},{2,6},{5,1},{7,3},{8,12},{10,14},{13,9},{15,11},{16,20},{18,... | collective-permute-start | bytes 6389768 | tf_op jit(solution)/shard_map/ppermute | solution.py:966
  231.0 83.9 %collective-permute-start.8 = (bf16[640,1664]{1,0:T(8,128)(2,1)}, bf16[640,1664]{1,0:T(8,128)(2,1)}, u32[]{:S(2)}, u32[]{:S(2)}) collective-permute-start(bf16[640,1664]{1,0:T(8,128)(2,1)} %collective-permute-done.2), channel_id=1, source_target_pairs={{0,4},{2,6},{5,1},{7,3},{8,12},{10,14},{13,9},{15,11},{16,20},{18,... | collective-permute-start | bytes 6389768 | tf_op jit(solution)/shard_map/ppermute | solution.py:966
  232.3 86.8 %collective-permute-start.9 = (bf16[640,1664]{1,0:T(8,128)(2,1)}, bf16[640,1664]{1,0:T(8,128)(2,1)}, u32[]{:S(2)}, u32[]{:S(2)}) collective-permute-start(bf16[640,1664]{1,0:T(8,128)(2,1)} %collective-permute-done.3), channel_id=1, source_target_pairs={{0,4},{2,6},{5,1},{7,3},{8,12},{10,14},{13,9},{15,11},{16,20},{18,... | collective-permute-start | bytes 6389768 | tf_op jit(solution)/shard_map/ppermute | solution.py:966
  622.6 420.3 %all-gather.5.cloned.1.call-start = ((), (), s32[]{:S(2)}) async-start(), calls=%async_computation.2 | async-start | bytes 16711680 | tf_op jit(solution)/shard_map/all_gather | solution.py:1082
  824.2 147.1 %all-to-all-start = ((bf16[4,192,640]{2,1,0:T(8,128)(2,1)}), bf16[4,192,640]{2,1,0:T(8,128)(2,1)}, u32[]{:S(2)}, u32[]{:S(2)}) async-start(bf16[4,192,640]{2,1,0:T(8,128)(2,1)} %bitcast.117), calls=%async_computation | async-start | bytes 1966080 | tf_op jit(solution)/shard_map/all_to_all | solution.py:1092
  828.6 367.9 %all-reduce.10.cloned.1.call-start = ((), (), s32[]{:S(2)}) async-start(), calls=%async_computation.3 | async-start | bytes 6553600 | tf_op jit(solution)/shard_map/psum | solution.py:1085
  1038.8 355.7 %all-reduce.12.cloned.1.call-start = ((), (), s32[]{:S(2)}) async-start(), calls=%async_computation.4 | async-start | bytes 7503872 | tf_op jit(solution)/shard_map/psum | solution.py:1109
  1150.2 53.3 %collective-permute-start.12 = (bf16[640,1664]{1,0:T(8,128)(2,1)}, bf16[640,1664]{1,0:T(8,128)(2,1)}, u32[]{:S(2)}, u32[]{:S(2)}) collective-permute-start(bf16[640,1664]{1,0:T(8,128)(2,1)} %fusion.12), channel_id=1, source_target_pairs={{0,2},{2,0},{5,7},{7,5},{8,10},{10,8},{13,15},{15,13},{16,18},{18,... | collective-permute-start | bytes 6389768 | tf_op jit(solution)/shard_map/ppermute | solution.py:922
  1152.3 52.4 %collective-permute-start.14 = (bf16[640,1664]{1,0:T(8,128)(2,1)}, bf16[640,1664]{1,0:T(8,128)(2,1)}, u32[]{:S(2)}, u32[]{:S(2)}) collective-permute-start(bf16[640,1664]{1,0:T(8,128)(2,1)} %fusion.12), channel_id=1, source_target_pairs={{1,2},{3,0},{4,7},{6,5},{9,10},{11,8},{12,15},{14,13},{17,18},{19,... | collective-permute-start | bytes 6389768 | tf_op jit(solution)/shard_map/ppermute | solution.py:922
  1157.4 48.7 %collective-permute-start.16 = (bf16[640,1664]{1,0:T(8,128)(2,1)}, bf16[640,1664]{1,0:T(8,128)(2,1)}, u32[]{:S(2)}, u32[]{:S(2)}) collective-permute-start(bf16[640,1664]{1,0:T(8,128)(2,1)} %fusion.15), channel_id=1, source_target_pairs={{0,2},{2,0},{5,7},{7,5},{8,10},{10,8},{13,15},{15,13},{16,18},{18,... | collective-permute-start | bytes 6389768 | tf_op jit(solution)/shard_map/ppermute | solution.py:922
  1159.3 85.7 %collective-permute-start.18 = (bf16[640,1664]{1,0:T(8,128)(2,1)}, bf16[640,1664]{1,0:T(8,128)(2,1)}, u32[]{:S(2)}, u32[]{:S(2)}) collective-permute-start(bf16[640,1664]{1,0:T(8,128)(2,1)} %fusion.15), channel_id=1, source_target_pairs={{1,2},{3,0},{4,7},{6,5},{9,10},{11,8},{12,15},{14,13},{17,18},{19,... | collective-permute-start | bytes 6389768 | tf_op jit(solution)/shard_map/ppermute | solution.py:922
  1196.5 212.1 %collective-permute-start.11 = (bf16[640,3328]{1,0:T(8,128)(2,1)}, bf16[640,3328]{1,0:T(8,128)(2,1)}, u32[]{:S(2)}, u32[]{:S(2)}) collective-permute-start(bf16[640,3328]{1,0:T(8,128)(2,1)} %fusion.2), channel_id=1, source_target_pairs={{0,1},{1,0},{2,3},{3,2},{4,5},{5,4},{6,7},{7,6},{8,9},{9,8},{10,11... | collective-permute-start | bytes 12779528 | tf_op jit(solution)/shard_map/ppermute | solution.py:891
  1203.4 205.1 %collective-permute-start.13 = (bf16[640,1664]{1,0:T(8,128)(2,1)}, bf16[640,1664]{1,0:T(8,128)(2,1)}, u32[]{:S(2)}, u32[]{:S(2)}) collective-permute-start(bf16[640,1664]{1,0:T(8,128)(2,1)} %collective-permute-done.12.gf), channel_id=1, source_target_pairs={{0,4},{2,6},{5,1},{7,3},{8,12},{10,14},{13,9},{15,11},{16,20},{18,... | collective-permute-start | bytes 6389768 | tf_op jit(solution)/shard_map/ppermute | solution.py:923
  1204.7 203.8 %collective-permute-start.15 = (bf16[640,1664]{1,0:T(8,128)(2,1)}, bf16[640,1664]{1,0:T(8,128)(2,1)}, u32[]{:S(2)}, u32[]{:S(2)}) collective-permute-start(bf16[640,1664]{1,0:T(8,128)(2,1)} %collective-permute-done.14.gd), channel_id=1, source_target_pairs={{0,4},{2,6},{5,1},{7,3},{8,12},{10,14},{13,9},{15,11},{16,20},{18,... | collective-permute-start | bytes 6389768 | tf_op jit(solution)/shard_map/ppermute | solution.py:923
  1206.0 202.5 %collective-permute-start.17 = (bf16[640,1664]{1,0:T(8,128)(2,1)}, bf16[640,1664]{1,0:T(8,128)(2,1)}, u32[]{:S(2)}, u32[]{:S(2)}) collective-permute-start(bf16[640,1664]{1,0:T(8,128)(2,1)} %collective-permute-done.16.uf), channel_id=1, source_target_pairs={{0,4},{2,6},{5,1},{7,3},{8,12},{10,14},{13,9},{15,11},{16,20},{18,... | collective-permute-start | bytes 6389768 | tf_op jit(solution)/shard_map/ppermute | solution.py:923
  1245.0 172.7 %collective-permute-start.19 = (bf16[640,1664]{1,0:T(8,128)(2,1)}, bf16[640,1664]{1,0:T(8,128)(2,1)}, u32[]{:S(2)}, u32[]{:S(2)}) collective-permute-start(bf16[640,1664]{1,0:T(8,128)(2,1)} %collective-permute-done.18.ud), channel_id=1, source_target_pairs={{0,4},{2,6},{5,1},{7,3},{8,12},{10,14},{13,9},{15,11},{16,20},{18,... | collective-permute-start | bytes 6389768 | tf_op jit(solution)/shard_map/ppermute | solution.py:923
  (56 other events, 4141.5 us)
Sparse Core Ops, SparseCore 0:
  622.7 127.0 all-gather.2
  823.3 142.0 all-gather.4
  1039.0 125.0 all-reduce.9
  1197.9 196.5 all-reduce.11

commit v3 on v2

--- a/solution.py
+++ b/solution.py
@@ -392,18 +392,19 @@
     return [pl.BlockSpec(memory_space=pltpu.VMEM)] * count
 
 
-def comm_call(kernel, name, number, inputs, out_shape, scratch, flops=0):
+def comm_call(kernel, name, number, inputs, out_shape, scratch, flops=0, aliased={}):
     nbytes = sum(v.size * v.dtype.itemsize for v in (*inputs, *out_shape))
     return pl.pallas_call(
         kernel,
-        in_specs=vmem(len(inputs)),
-        out_specs=vmem(len(out_shape)),
+        in_specs=vmem(len(inputs) - len(aliased)) + any_space(len(aliased)),
+        out_specs=vmem(len(out_shape) - len(aliased)) + any_space(len(aliased)),
         out_shape=out_shape,
         scratch_shapes=scratch,
+        input_output_aliases=aliased,
         compiler_params=pltpu.CompilerParams(
             collective_id=number, has_side_effects=True, vmem_limit_bytes=VMEM_LIMIT
         ),
-        cost_estimate=pl.CostEstimate(flops=flops, bytes_accessed=nbytes, transcendentals=0),
+        cost_estimate=pl.CostEstimate(flops=0, bytes_accessed=0 * nbytes, transcendentals=0),
         name=name,
     )(*inputs)
 
@@ -446,13 +447,26 @@
 MODEL_STEP = 512
 
 
-def output_kernel(att_ref, weight_ref, hidden_ref, gain_ref, mixed_ref, two_ref, *scratch):
+def output_kernel(relaying, att_ref, weight_ref, hidden_ref, gain_ref, *refs):
+    if relaying:
+        _, mixed_ref, two_ref, up_ref, *scratch, passed = refs
+    else:
+        mixed_ref, two_ref, *scratch = refs
     *parts, sems = scratch
     rows = hidden_ref.shape[0]
     width = MODEL_STEP
     steps = D // width
     me, core, sib, far = partners()
-    greet([{"shard": sib}, {"shard": far}])
+    devices = [{"shard": sib}, {"shard": far}]
+    if relaying:
+        partner, away = replica_pair()
+        devices.append({"rep": partner})
+    greet(devices)
+    if relaying:
+        @pl.when(away == 0)
+        def _():
+            for slot, owner in enumerate((far, far + 1 - 2 * core)):
+                pass_on(up_ref, passed, slot, owner).start()
 
     def partial(where, step):
         return project(att_ref[where, :], weight_ref[:, columns(step, width)])
@@ -470,30 +484,56 @@
         two_ref[rows_at(me, rows), lanes] = (mixed_ref[:, lanes] * scale * gain_ref[:, lanes]).astype(bf16)
 
     spread_rows(rows, steps, width, place, two_ref, sems)
-
-
-def output_norm(attended, weight, hidden, gain):
+    if relaying:
+        @pl.when(away == 0)
+        def _():
+            for slot, owner in enumerate((far, far + 1 - 2 * core)):
+                pass_on(up_ref, passed, slot, owner).wait_send()
+
+        @pl.when(away == 1)
+        def _():
+            for slot, owner in enumerate((far, far + 1 - 2 * core)):
+                pass_on(up_ref, passed, slot, owner).wait_recv()
+
+
+def output_norm(attended, weight, hidden, gain, up=None):
     if lax.axis_size("shard") != 4:
         mixed = hidden + residual_scale * plain_scatter(project(attended, weight))
         return mixed, plain_gather((mixed * norm_scale(mixed) * gain).astype(bf16))
     rows = hidden.shape[0]
     steps = D // MODEL_STEP
+    scratch = exchange_scratch(rows, steps, MODEL_STEP) + [pltpu.SemaphoreType.DMA((3, 2, steps))]
+    inputs = [attended, weight, hidden, gain[None]]
+    outputs = [shape(rows, D, f32), shape(4 * rows, D, bf16)]
+    flops = 2 * attended.size * D
+    if up is None:
+        return comm_call(functools.partial(output_kernel, False), "output_norm", 2, inputs, outputs, scratch, flops)
     return comm_call(
-        output_kernel, "output_norm", 2, [attended, weight, hidden, gain[None]],
-        [shape(rows, D, f32), shape(4 * rows, D, bf16)],
-        exchange_scratch(rows, steps, MODEL_STEP) + [pltpu.SemaphoreType.DMA((3, 2, steps))],
-        flops=2 * attended.size * D,
-    )
-
-
-def down_kernel(passing, act_ref, weight_ref, mixed_ref, out_ref, low_ref, *scratch):
+        functools.partial(output_kernel, True), "output_norm", 9, inputs + [up],
+        outputs + [jax.ShapeDtypeStruct(up.shape, bf16)], scratch + [pltpu.SemaphoreType.DMA((2, 2))], flops,
+        aliased={4: 2},
+    )
+
+
+def down_kernel(passing, act_ref, given_ref, mixed_ref, out_ref, low_ref, *scratch):
     rows = mixed_ref.shape[0]
     width = MODEL_STEP
     steps = D // width
     me, core, sib, far = partners()
     devices = [{"shard": sib}, {"shard": far}]
+    weight_ref = given_ref
     if passing:
-        got_ref, *parts, sems = scratch
+        got_ref, weight_ref, *parts, sems = scratch
+        size, more = given_ref.shape[0], weight_ref.shape[0] - given_ref.shape[0]
+        weight_ref[pl.ds(pl.multiple_of((1 - core) * size, 16), more), :] = jnp.zeros((more, D), bf16)
+        piece = 64
+
+        def fill(step):
+            source = pl.ds(pl.multiple_of(step * piece, 16), piece)
+            target = pl.ds(pl.multiple_of(step * piece + core * more, 16), piece)
+            weight_ref[target, :] = given_ref[source, :]
+
+        each(size // piece, False, fill)
         section = lax.axis_index("section")
         devices.append({"section": 1 - section})
     else:
@@ -524,23 +564,27 @@
 
 
 def down_project(activated, weight, mixed, passing):
-    if lax.axis_size("shard") != 4:
+    count = lax.axis_size("shard")
+    if count != 4:
+        if passing:
+            weight = window_rows(weight, count)
         output = mixed + residual_scale * plain_scatter(project(activated, weight))
         low = output.astype(bf16)
-        return (output, low) + ((lax.ppermute(low, "section", [(0, 1)]),) if passing else ())
+        return (output, low) + ((lax.ppermute(low, "section", [(0, 1)]), weight) if passing else ())
     rows = mixed.shape[0]
     steps = D // MODEL_STEP
     scratch = exchange_scratch(rows, steps, MODEL_STEP)
     return comm_call(
         functools.partial(down_kernel, passing), "down_project", 3 if passing else 4,
         [activated, weight, mixed],
-        [shape(rows, D, f32)] + [shape(rows, D, bf16)] * (2 if passing else 1),
+        [shape(rows, D, f32)] + [shape(rows, D, bf16)] * (2 if passing else 1)
+        + [shape(HIDDEN_WINDOW, D, bf16)] * passing,
         scratch + ([pltpu.SemaphoreType.DMA((2, steps))] if passing else []),
         flops=2 * activated.size * D,
     )
 
 
-def mlp_back_kernel(both_ref, weight_ref, mixed_ref, grad_ref, gain_ref, out_ref, dgain_ref, branch_ref,
+def mlp_back_kernel(gate_ref, up_ref, gate_weight_ref, up_weight_ref, mixed_ref, grad_ref, gain_ref, out_ref, dgain_ref, branch_ref,
                     *scratch):
     *parts, sems = scratch
     rows = mixed_ref.shape[0]
@@ -550,7 +594,10 @@
     greet([{"shard": sib}, {"shard": far}])
 
     def partial(where, step):
-        return contract_cols(both_ref[where, :], weight_ref[columns(step, width), :])
+        rows_of = columns(step, width)
+        return contract_cols(gate_ref[where, :], gate_weight_ref[rows_of, :]) + contract_cols(
+            up_ref[where, :], up_weight_ref[rows_of, :]
+        )
 
     def use(step, total):
         out_ref[:, columns(step, width)] = total
@@ -572,19 +619,20 @@
     spread_rows(rows, steps, width, place, branch_ref, sems)
 
 
-def mlp_back(grad_both, gate_up, mixed, grad_out, gain):
+def mlp_back(grad_gate, grad_up, gate_weight, up_weight, mixed, grad_out, gain):
     if lax.axis_size("shard") != 4:
-        grad = plain_scatter(contract_cols(grad_both, gate_up))
+        grad = plain_scatter(contract_cols(grad_gate, gate_weight) + contract_cols(grad_up, up_weight))
         back, dgain = norm_back(mixed, norm_scale(mixed), gain, grad)
         grad_mixed = grad_out + back
         return grad_mixed, dgain[None], plain_gather((residual_scale * grad_mixed).astype(bf16))
     rows = mixed.shape[0]
     steps = D // MODEL_STEP
     return comm_call(
-        mlp_back_kernel, "mlp_back", 5, [grad_both, gate_up, mixed, grad_out, gain[None]],
+        mlp_back_kernel, "mlp_back", 5,
+        [grad_gate, grad_up, gate_weight, up_weight, mixed, grad_out, gain[None]],
         [shape(rows, D, f32), shape(1, D, f32), shape(4 * rows, D, bf16)],
         exchange_scratch(rows, steps, MODEL_STEP) + [pltpu.SemaphoreType.DMA((3, 2, steps))],
-        flops=2 * grad_both.size * D,
+        flops=4 * grad_gate.size * D,
     )
 
 
@@ -645,13 +693,31 @@
     )
 
 
-def move_kernel(whole, split, *refs):
-    amount = whole + len(split)
-    inputs, outputs, (sems, local) = refs[:amount], refs[amount:2 * amount], refs[2 * amount:]
+def replica_pair():
+    replica = lax.axis_index("rep")
+    return replica + 1 - 2 * (replica % 2), (lax.axis_index("shard") + replica) % 2
+
+
+def pass_on(target, sems, step, owner):
+    partner, _ = replica_pair()
+    return pltpu.make_async_remote_copy(
+        src_ref=target.at[owner], dst_ref=target.at[owner], send_sem=sems.at[0, step], recv_sem=sems.at[1, step],
+        device_id={"rep": partner}, device_id_type=MESH,
+    )
+
+
+def move_kernel(whole, split, relayed, *refs):
+    amount = whole + len(split) + len(relayed)
+    inputs, outputs, held = refs[:amount], refs[amount:2 * amount], refs[2 * amount:3 * amount]
+    sems, local, *relays = refs[3 * amount:]
     me, core, sib, far = partners()
     diagonal = far + 1 - 2 * core
-    greet([{"shard": sib}, {"shard": far}, {"shard": diagonal}])
-    waits, forwards, keeps = [], [], []
+    devices = [{"shard": sib}, {"shard": far}, {"shard": diagonal}]
+    if relayed:
+        partner, away = replica_pair()
+        devices.append({"rep": partner})
+    greet(devices)
+    waits, forwards, keeps, bulk = [], [], [], []
     number = 0
     for i, (source, target) in enumerate(zip(inputs, outputs)):
         if i < whole:
@@ -663,17 +729,37 @@
             forwards.append((to_far, onward))
             waits.append(to_sib)
             kept = source
-        else:
+        elif i < whole + len(split):
             part = split[i - whole]
             for j, device in enumerate((far, diagonal, sib)):
                 copy = send_to(part(source, device), target.at[me], sems, number + j, device)
                 copy.start()
                 waits.append(copy)
             kept = part(source, me)
+        else:
+            begin, arrive, passed = relays
+            place = i - whole - len(split)
+            taker = far // 2 * 2 + lax.axis_index("rep") % 2
+
+            def across(owner, slot):
+                return pltpu.make_async_remote_copy(
+                    src_ref=hidden_columns(source, taker), dst_ref=target.at[owner], send_sem=begin.at[place],
+                    recv_sem=arrive.at[place, slot], device_id={"shard": taker}, device_id_type=MESH,
+                )
+
+            across(me, away).start()
+            beside = send_to(hidden_columns(source, sib), target.at[me], sems, number, sib)
+            beside.start()
+            waits.append(beside)
+            bulk.append((place, target, across))
+            kept = hidden_columns(source, me)
         number += 3
-        keep = pltpu.make_async_copy(kept, target.at[me], local.at[i])
+        keep = pltpu.make_async_copy(kept, held[i], local.at[0, i])
         keep.start()
-        keeps.append(keep)
+        keeps.append((keep, pltpu.make_async_copy(held[i], target.at[me], local.at[1, i])))
+    for keep, store in keeps:
+        keep.wait()
+        store.start()
     for to_far, onward in forwards:
         to_far.wait_recv()
         onward.start()
@@ -682,21 +768,56 @@
         onward.wait()
     for copy in waits:
         copy.wait()
-    for keep in keeps:
-        keep.wait()
-
-
-def move(name, number, wholes, splits):
-    inputs = list(wholes) + [array for array, _, _ in splits]
-    shapes = [w.shape for w in wholes] + [part for _, part, _ in splits]
+    for keep, store in keeps:
+        store.wait()
+    for place, target, across in bulk:
+        passing = relayed[place]
+        passed = relays[2]
+
+        @pl.when(away == 0)
+        def _():
+            for slot, owner in enumerate((far, diagonal)):
+                across(owner, slot).wait_recv()
+                if passing:
+                    pass_on(target, passed, 2 * place + slot, owner).start()
+
+    for place, target, across in bulk:
+        passing = relayed[place]
+        passed = relays[2]
+        across(me, away).wait_send()
+        if passing:
+            @pl.when(away == 0)
+            def _():
+                for slot, owner in enumerate((far, diagonal)):
+                    pass_on(target, passed, 2 * place + slot, owner).wait_send()
+
+            @pl.when(away == 1)
+            def _():
+                for slot, owner in enumerate((far, diagonal)):
+                    pass_on(target, passed, 2 * place + slot, owner).wait_recv()
+
+
+def move(name, number, wholes, splits, relayed=()):
+    inputs = list(wholes) + [array for array, _, _ in (*splits, *relayed)]
+    shapes = [w.shape for w in wholes] + [part for _, part, _ in (*splits, *relayed)]
     out_shape = [jax.ShapeDtypeStruct((4,) + tuple(sh), v.dtype) for sh, v in zip(shapes, inputs)]
+    scratch = [pltpu.VMEM(sh, v.dtype) for sh, v in zip(shapes, inputs)]
+    scratch += [pltpu.SemaphoreType.DMA((2, 3 * len(inputs))), pltpu.SemaphoreType.DMA((2, len(inputs)))]
+    if relayed:
+        amount = len(relayed)
+        scratch += [
+            pltpu.SemaphoreType.DMA((amount,)), pltpu.SemaphoreType.DMA((amount, 2)),
+            pltpu.SemaphoreType.DMA((2, 2 * amount)),
+        ]
     return pl.pallas_call(
-        functools.partial(move_kernel, len(wholes), [f for _, _, f in splits]),
+        functools.partial(move_kernel, len(wholes), [f for _, _, f in splits], [p for _, _, p in relayed]),
         in_specs=any_space(len(inputs)),
         out_specs=any_space(len(inputs)),
         out_shape=out_shape,
-        scratch_shapes=[pltpu.SemaphoreType.DMA((2, 3 * len(inputs))), pltpu.SemaphoreType.DMA((len(inputs),))],
-        compiler_params=pltpu.CompilerParams(collective_id=number, has_side_effects=True),
+        scratch_shapes=scratch,
+        compiler_params=pltpu.CompilerParams(
+            collective_id=number, has_side_effects=True, vmem_limit_bytes=VMEM_LIMIT
+        ),
         cost_estimate=pl.CostEstimate(
             flops=0, bytes_accessed=sum(4 * v.size * v.dtype.itemsize for v in inputs), transcendentals=0
         ),
@@ -704,6 +825,13 @@
     )(*inputs)
 
 
+HIDDEN_WINDOW = 1664
+
+
+def hidden_columns(ref, owner):
+    return ref.at[:, pl.ds(pl.multiple_of(owner // 2 * 3200 + owner % 2 * 1536, LANES), HIDDEN_WINDOW)]
+
+
 QUERY_WINDOW = 1024
 
 
@@ -715,66 +843,78 @@
     return ref.at[:, pl.ds(pl.multiple_of(owner * 1280, LANES), 1280)]
 
 
-def first_move(query_down, latent_down, query_up, latent_up, segments, count):
+def first_move(query_down, latent_down, query_up, latent_up, segments, gate, up, count):
     if count != 4:
+        gate, up = spread_hidden(gate, up, count)
         return (
             plain_gather(query_down), plain_gather(latent_down), pad_heads(spread(query_up, count)),
-            spread(latent_up, count), plain_gather(segments),
+            spread(latent_up, count), plain_gather(segments), gate, up,
         )
-    down_q, down_kv, groups, up_q, up_kv = move(
+    part = (gate.shape[0], HIDDEN_WINDOW)
+    relayed = [(gate, part, True), (up, part, False)] if shared_links(count) else []
+    down_q, down_kv, groups, up_q, up_kv, *hidden = move(
         "first_move", 7, [query_down, latent_down, segments],
         [(query_up, (query_up.shape[0], QUERY_WINDOW), query_window),
          (latent_up, (latent_up.shape[0], 1280), latent_window)],
+        relayed,
     )
     merge = lambda value: value.reshape((-1,) + value.shape[2:])
     up_q = lax.dynamic_slice_in_dim(merge(up_q), lax.axis_index("shard") % 2 * 64, 960, 1)
-    return merge(down_q), merge(down_kv), pad_heads(up_q), merge(up_kv), merge(groups)
-
-
-def row_block(rows):
-    return lambda ref, owner: ref.at[pl.ds(pl.multiple_of(owner * rows, 16), rows), :]
+    gate, up = hidden if relayed else spread_hidden(gate, up, count)
+    return merge(down_q), merge(down_kv), pad_heads(up_q), merge(up_kv), merge(groups), gate, up
+
+
+EXCHANGE_WIDTH = 1280
 
 
 def last_move(grad_lat, gain_terms, query_part, latent_part, count):
     if count != 4:
-        return (
+        parts = (
             plain_gather(grad_lat), plain_gather(gain_terms), collect(cut_heads(query_part), count),
             collect(latent_part, count),
         )
-    rows_q, rows_kv = query_part.shape[0] // 4, latent_part.shape[0] // 4
-    lat, got_gains, got_q, got_kv = move(
-        "last_move", 8, [grad_lat, gain_terms],
-        [(query_part, (rows_q, query_part.shape[1]), row_block(rows_q)),
-         (latent_part, (rows_kv, latent_part.shape[1]), row_block(rows_kv))],
-    )
+        return parts, lambda parts: parts
     side = lambda value: value.transpose(1, 0, 2).reshape(value.shape[1], -1)
-    return lat.reshape(-1, lat.shape[2]), got_gains.reshape(4, -1), cut_heads(side(got_q)), side(got_kv)
-
-
-def place_kernel(width, own, beside, gf, gf2, gd, gd2, uf, uf2, ud, ud2, gate_ref, up_ref):
+    same = lambda value: jnp.broadcast_to(value[None], (count,) + value.shape)
+    wide = lambda value: jnp.pad(value, ((0, 0), (0, EXCHANGE_WIDTH - value.shape[1])))
+    amount = gain_terms.shape[1]
+    gain_rows = -(-amount // EXCHANGE_WIDTH)
+    gain_rows += -gain_rows % 16
+    gains = jnp.pad(gain_terms[0].astype(bf16), (0, gain_rows * EXCHANGE_WIDTH - amount)).reshape(gain_rows, -1)
+    pieces = [
+        query_part.reshape(count, -1, EXCHANGE_WIDTH), latent_part.reshape(count, -1, EXCHANGE_WIDTH),
+        same(wide(grad_lat)), same(gains),
+    ]
+    got = lax.all_to_all(jnp.concatenate(pieces, axis=1), "shard", 0, 0, tiled=True)
+    ends = [0]
+    for piece in pieces:
+        ends.append(ends[-1] + piece.shape[1])
+    def finish(got):
+        got_q, got_kv, lat, gains = (got[:, start:end] for start, end in zip(ends, ends[1:]))
+        return (
+            lat.reshape(-1, EXCHANGE_WIDTH)[:, :grad_lat.shape[1]],
+            gains.reshape(count, -1)[:, :amount].astype(f32), cut_heads(side(got_q)), side(got_kv),
+        )
+
+    return got, finish
+
+
+def place_kernel(*refs):
     me, core, sib, far = partners()
-    gate_ref[...] = jnp.zeros_like(gate_ref)
-    up_ref[...] = jnp.zeros_like(up_ref)
-
-    def lanes(owner):
-        return pl.ds(pl.multiple_of(owner // 2 * 3200 + owner % 2 * 1536, LANES), width)
-
-    for owner, part in ((me, own), (sib, beside)):
-        gate_ref[:, lanes(owner)] += part[:, :width].astype(f32)
-        up_ref[:, lanes(owner)] += part[:, width:].astype(f32)
-    diagonal = far + 1 - 2 * core
-    for owner, gate, gate2, up, up2 in ((far, gf, gf2, uf, uf2), (diagonal, gd, gd2, ud, ud2)):
-        gate_ref[:, lanes(owner)] += gate[...].astype(f32) + gate2[...].astype(f32)
-        up_ref[:, lanes(owner)] += up[...].astype(f32) + up2[...].astype(f32)
+    *parts, out_ref = refs
+    out_ref[...] = jnp.zeros_like(out_ref)
+    for owner, part in zip((me, sib, far, far + 1 - 2 * core), parts):
+        lanes = pl.ds(pl.multiple_of(owner // 2 * 3200 + owner % 2 * 1536, LANES), HIDDEN_WINDOW)
+        out_ref[:, lanes] += part[...].astype(f32)
 
 
 def head_lanes(value):
     return jnp.pad(value, ((0, 0), (NOPE, LANES - NOPE - ROPE)))
 
 
-def layer_forward(hidden, own_tables, tables, gains, weights, passing, hidden_weights):
+def layer_forward(hidden, own_tables, tables, gains, weights, passing, lacking, early):
     input_gain, query_gain, latent_gain, post_gain = gains
-    down_both, query_up, latent_up, output_weight = weights[:4]
+    down_both, query_up, latent_up, output_weight, gate_weight, up_weight, down_weight = weights
     scale_in = norm_scale(hidden)
     normed = (hidden * scale_in * input_gain).astype(bf16)
     down_q, down_kv = down_both
@@ -792,55 +932,63 @@
         axis=1,
     ).astype(bf16)
     all_in = gather(own_in, 0, 384)
-    all_in, finish = hidden_weights(all_in)
+    all_in, early = together(all_in, early)
+    if lacking is not None:
+        early = plain_gather(early)
     query_in = all_in[:, :QRANK]
     kv_in = all_in[:, QRANK:QRANK + KVRANK]
     shared = all_in[:, QRANK + KVRANK:]
     attended, queries, keyval, logs = attend(
         project(query_in, query_up), project(kv_in, latent_up), shared, tables
     )
-    attended, gate_up = finish(attended)
-    mixed, normed_two = output_norm(attended, output_weight, hidden, post_gain)
-    both = project(normed_two, gate_up)
-    width = both.shape[1] // 2
-    gate, up = both[:, :width], both[:, width:]
+    attended, early = together(attended, early)
+    if lacking:
+        mixed, normed_two, up_weight = output_norm(attended, output_weight, hidden, post_gain, up_weight)
+    else:
+        mixed, normed_two = output_norm(attended, output_weight, hidden, post_gain)
+    merge = lambda value: value.reshape(D, -1)
+    gate = project(normed_two, merge(gate_weight))
+    up = project(normed_two, merge(up_weight))
     activated = (jax.nn.silu(gate) * up).astype(bf16)
-    def outputs(order=lambda value: value):
-        return down_project(order(activated), weights[4], mixed, passing)
+    def outputs(value):
+        return down_project(value, down_weight, mixed, passing)
 
     kept = (hidden, scale_in, normed, latent_q, scale_q, latent, scale_kv, query_in, kv_in,
             shared, queries, keyval, logs, attended, mixed, normed_two, gate, up)
-    return (outputs, kept, gate_up)
+    return (outputs, activated, kept, merge(gate_weight), merge(up_weight), early)
 
 
 def gate_backward(grad_act, gate, up):
     sigmoid = jax.nn.sigmoid(gate)
     grad_gate = (grad_act * up * sigmoid * (1.0 + gate * (1.0 - sigmoid))).astype(bf16)
     grad_up = (grad_act * gate * sigmoid).astype(bf16)
-    return jnp.concatenate([grad_gate, grad_up], axis=1)
-
-
-def mlp_backward(grad_out, kept, gains, weights):
+    return grad_gate, grad_up
+
+
+def mlp_backward(grad_out, kept, gains, weights, gather_down, wanted):
     mixed, gate, up = kept[14], kept[16], kept[17]
-    gate_up, down_weight = weights[4:]
+    gate_weight, up_weight, down_weight = weights[4:]
     own_down = (residual_scale * grad_out).astype(bf16)
-    grad_down = gather(own_down, 1, 512)
-    grad_both = gate_backward(contract_cols(grad_down, down_weight), gate, up)
-    grad_mixed, dgain_post, grad_branch = mlp_back(grad_both, gate_up, mixed, grad_out, gains[3])
-    return own_down, grad_mixed, dgain_post[0], grad_branch
-
-
-def attention_backward(grad_mixed, grad_branch, kept, own_tables, tables, gains, weights):
+    grad_down, own_down, wanted = together(gather_down(own_down), own_down, wanted)
+    grad_gate, grad_up = gate_backward(contract_cols(grad_down, down_weight), gate, up)
+    grad_mixed, dgain_post, grad_branch = mlp_back(
+        grad_gate, grad_up, gate_weight, up_weight, mixed, grad_out, gains[3]
+    )
+    return (grad_gate, grad_up), wanted, own_down, grad_mixed, dgain_post[0], grad_branch
+
+
+def attention_backward(grad_mixed, grad_branch, kept, own_tables, tables, gains, weights, wanted):
     (hidden, scale_in, normed, latent_q, scale_q, latent, scale_kv, query_in, kv_in,
      shared, queries, keyval, logs, attended, mixed, normed_two, gate, up) = kept
     input_gain, query_gain, latent_gain, post_gain = gains
-    down_both, query_up, latent_up, output_weight, gate_up, down_weight = weights
+    down_both, query_up, latent_up, output_weight = weights[:4]
     cosine, sine = own_tables
     grad_attended = contract_cols(grad_branch, output_weight).astype(bf16)
     grad_query, grad_keyval, grad_shared = attend_back(
         queries, keyval, shared, tables, grad_attended, attended, logs
     )
     grad_in = latent_back(grad_query, grad_keyval, grad_shared, query_up, latent_up)
+    grad_in, wanted = together(grad_in, wanted)
     grad_latent_q, dgain_query = norm_back(latent_q, scale_q, query_gain, grad_in[:, :QRANK])
     grad_latent, dgain_latent = norm_back(
         latent, scale_kv, latent_gain, grad_in[:, QRANK:QRANK + KVRANK]
@@ -857,7 +1005,7 @@
     grad_hidden_norm, dgain_input = norm_back(hidden, scale_in, input_gain, grad_normed)
     grad_hidden = grad_mixed + grad_hidden_norm
     found = (grad_branch, grad_query, grad_keyval, grad_lat)
-    return (grad_hidden, found, (dgain_input, dgain_query, dgain_latent))
+    return (grad_hidden, found, (dgain_input, dgain_query, dgain_latent), wanted)
 
 
 def spread(weight, count):
@@ -907,68 +1055,21 @@
     return count == 4 and lax.axis_size("rep") % 2 == 0
 
 
-def relay_pairs(count):
-    reps = lax.axis_size("rep")
-    places = [(rep, own) for rep in range(reps) for own in range(count)]
-    number = lambda rep, own: rep * count + own
-    same = [(number(r, o), number(r, o ^ 2)) for r, o in places if o % 2 == r % 2]
-    other = [(number(r, o), number(r, o ^ 3)) for r, o in places if o % 2 != r % 2]
-    beside = [(number(r, o), number(r ^ 1, o)) for r, o in places if o % 2 == r % 2]
-    return same, other, beside
-
-
-def relay(value, count):
-    *across, beside = relay_pairs(count)
-    direct = [lax.ppermute(value, ("rep", "shard"), way) for way in across]
-    return [(part, lax.ppermute(part, ("rep", "shard"), beside)) for part in direct]
-
-
-def relay_owner(me):
-    return (me // 2 * 2 + 2) % 4 + lax.axis_index("rep") % 2
-
-
 def spread_hidden(gate, up, count):
     me = lax.axis_index("shard")
     size, width, starts, offsets = hidden_window(count)
     rows = gate.shape[0]
-    whole = jnp.zeros((rows * count, 2 * width), bf16)
-    for step in range(count):
-        owner = me ^ step
-        begin = take_at(starts, owner)
-        part = jnp.concatenate(
-            [lax.dynamic_slice(gate, (0, begin), (rows, width)), lax.dynamic_slice(up, (0, begin), (rows, width))],
-            axis=1,
-        )
-        if step:
-            part = swap(part, step)
-        whole = lax.dynamic_update_slice(whole, part, (owner * rows, 0))
-    return whole
-
-
-def relay_hidden(gate, up, count):
-    me = lax.axis_index("shard")
-    size, width, starts, offsets = hidden_window(count)
-    rows = gate.shape[0]
-    pairs = relay_pairs(count)
-    windows = lambda owner: [
-        lax.dynamic_slice(weight, (0, take_at(starts, owner)), (rows, width)) for weight in (gate, up)
-    ]
-    direct = [
-        [lax.ppermute(part, ("rep", "shard"), way) for way in pairs[:2]] for part in windows(relay_owner(me))
-    ]
-    own = windows(me)
-    beside = [swap(part, 1) for part in windows(me ^ 1)]
-
-    def finish(value):
-        value, *flat = together(value, *direct[0], *direct[1], *beside)
-        whole = jnp.zeros((rows * count, 2 * width), bf16)
-        for which in range(2):
-            far = [part + lax.ppermute(part, ("rep", "shard"), pairs[2]) for part in flat[2 * which:2 * which + 2]]
-            for step, part in enumerate((own[which], flat[4 + which], *far)):
-                whole = lax.dynamic_update_slice(whole, part, ((me ^ step) * rows, which * width))
-        return value, whole
-
-    return finish
+    results = []
+    for weight in (gate, up):
+        whole = jnp.zeros((rows * count, width), bf16)
+        for step in range(count):
+            owner = me ^ step
+            part = lax.dynamic_slice(weight, (0, take_at(starts, owner)), (rows, width))
+            if step:
+                part = swap(part, step)
+            whole = lax.dynamic_update_slice(whole, part, (owner * rows, 0))
+        results.append(whole)
+    return results
 
 
 def window_rows(down, count):
@@ -977,54 +1078,172 @@
     return lax.dynamic_update_slice(whole, down, (take_at(offsets, lax.axis_index("shard")), 0))
 
 
-def window_gradients(two_all, grad_both, count):
+def chip_gradients_kernel(order_ref, two_ref, gate_ref, up_ref, gate_out, up_out, turned):
+    tokens, rows = two_ref.shape
+    piece = 512
+    for start in range(0, tokens, piece):
+        size = min(piece, tokens - start)
+        turned[:, start:start + size] = two_ref[start:start + size, :].T
+    width = gate_ref.shape[1]
+    whole = width // piece
+    for grad, out in ((gate_ref, gate_out), (up_ref, up_out)):
+        def tile(step):
+            lanes = columns(step, piece)
+            out[0, :, lanes] = project(turned[...], grad[:, lanes]).astype(bf16)
+
+        each(whole, False, tile)
+        if whole * piece < width:
+            out[0, :, whole * piece:] = project(turned[...], grad[:, whole * piece:]).astype(bf16)
+
+
+def chip_gradients(two_all, grad_gate, grad_up):
+    me, core, sib, far = partners()
+    tokens, width = grad_gate.shape
+    rows = D // 4
+    held = pl.BlockSpec((tokens, width), lambda i, order: (0, 0), pipeline_mode=pl.Buffered(1))
+    part = pl.BlockSpec((1, rows, width), lambda i, order: (i, 0, 0))
+    gate, up = pl.pallas_call(
+        chip_gradients_kernel,
+        grid_spec=pltpu.PrefetchScalarGridSpec(
+            num_scalar_prefetch=1,
+            grid=(2,),
+            in_specs=[pl.BlockSpec((tokens, rows), lambda i, order: (0, order[i])), held, held],
+            out_specs=[part, part],
+            scratch_shapes=[pltpu.VMEM((rows, tokens), bf16)],
+        ),
+        out_shape=[jax.ShapeDtypeStruct((2, rows, width), bf16)] * 2,
+        compiler_params=pltpu.CompilerParams(vmem_limit_bytes=VMEM_LIMIT),
+        name="chip_gradients",
+    )(jnp.stack([sib, me]).astype(jnp.int32), two_all, grad_gate, grad_up)
+    return [gate[0], up[0], gate[1], up[1]]
+
+
+RECOMPUTE_ROWS = 384
+
+
+def recompute_kernel(from_ref, own_ref, two_ref, down_ref, gate_ref, up_ref, rows_ref, act_own, gate_own, up_own,
+                     act_out, gate_out, up_out):
+    place = pl.program_id(0)
+    width = gate_ref.shape[1]
+    piece = 512
+
+    @pl.when(own_ref[place] == 1)
+    def _():
+        act_out[...] = act_own[...]
+        gate_out[...] = gate_own[...]
+        up_out[...] = up_own[...]
+
+    @pl.when(own_ref[place] == 0)
+    def _():
+        def tile(lanes, some_rows):
+            gate = project(two_ref[...], gate_ref[:, lanes])
+            up = project(two_ref[...], up_ref[:, lanes])
+            grad = contract_cols(down_ref[...], rows_ref[some_rows, :])
+            sigmoid = jax.nn.sigmoid(gate)
+            silu = gate * sigmoid
+            act_out[:, lanes] = (silu * up).astype(bf16)
+            gate_out[:, lanes] = (grad * up * sigmoid * (1.0 + gate * (1.0 - sigmoid))).astype(bf16)
+            up_out[:, lanes] = (grad * silu).astype(bf16)
+
+        each(width // piece, False, lambda step: tile(columns(step, piece), columns(step, piece)))
+        if width % piece:
+            rest = slice(width // piece * piece, width)
+            tile(rest, rest)
+
+
+def recompute(two_all, down_all, gate_columns, up_columns, down_rows, own):
+    tokens, width = two_all.shape[0], gate_columns.shape[1]
+    group = own[0].shape[0]
+    tile = RECOMPUTE_ROWS
+    each_group = group // tile
+    places = jnp.arange(tokens // tile, dtype=jnp.int32)
+    is_own = places // each_group == lax.axis_index("rep")
+    source = jnp.where(is_own, places % each_group, 0).astype(jnp.int32)
+    whole = lambda value: pl.BlockSpec(value.shape, lambda i, a, b: (0, 0), pipeline_mode=pl.Buffered(1))
+    wide = pl.BlockSpec((tile, D), lambda i, a, b: (i, 0))
+    mine = pl.BlockSpec((tile, width), lambda i, a, b: (a[i], 0))
+    part = pl.BlockSpec((tile, width), lambda i, a, b: (i, 0))
+    return pl.pallas_call(
+        recompute_kernel,
+        grid_spec=pltpu.PrefetchScalarGridSpec(
+            num_scalar_prefetch=2,
+            grid=(tokens // tile,),
+            in_specs=[wide, wide, whole(gate_columns), whole(up_columns), whole(down_rows), mine, mine, mine],
+            out_specs=[part] * 3,
+        ),
+        out_shape=[jax.ShapeDtypeStruct((tokens, width), bf16)] * 3,
+        compiler_params=pltpu.CompilerParams(vmem_limit_bytes=VMEM_LIMIT),
+        name="recompute",
+    )(source, is_own.astype(jnp.int32), two_all, down_all, gate_columns, up_columns, down_rows, *own)
+
+
+def down_gradient_kernel(act_ref, down_ref, out_ref, turned):
+    tokens, width = act_ref.shape
+    size = out_ref.shape[0]
+    piece = 512
+
+    @pl.when(pl.program_id(0) == 0)
+    def _():
+        for start in range(0, tokens, piece):
+            turned[:, start:start + piece] = act_ref[start:start + piece, :].T
+
+    offset = lax.axis_index("shard") % 2 * (width - size)
+    half = size // 2
+
+    def tile(step):
+        rows = pl.ds(pl.multiple_of(step * half, 16), half)
+        out_ref[rows, :] = project(turned[pl.ds(pl.multiple_of(step * half + offset, 16), half), :], down_ref[...])
+
+    each(2, False, tile)
+
+
+def down_gradient(activated_all, down_all):
+    tokens, width = activated_all.shape
+    size, piece = FF // 4, 512
+    return pl.pallas_call(
+        down_gradient_kernel,
+        grid=(D // piece,),
+        in_specs=[pl.BlockSpec((tokens, width), lambda i: (0, 0), pipeline_mode=pl.Buffered(1)),
+                  pl.BlockSpec((tokens, piece), lambda i: (0, i))],
+        out_specs=pl.BlockSpec((size, piece), lambda i: (0, i)),
+        out_shape=jax.ShapeDtypeStruct((size, D), f32),
+        scratch_shapes=[pltpu.VMEM((width, tokens), bf16)],
+        compiler_params=pltpu.CompilerParams(vmem_limit_bytes=VMEM_LIMIT),
+        name="down_gradient",
+    )(activated_all, down_all)
+
+
+def owner_gradients(two_all, grad_gate, grad_up, owner, count):
+    rows = D // count
+    left = lax.dynamic_slice(two_all, (0, owner * rows), (two_all.shape[0], rows))
+    return [contract_rows(left, grad).astype(bf16) for grad in (grad_gate, grad_up)]
+
+
+def place_windows(both, count):
+    size, width, starts, offsets = hidden_window(count)
+    rows = both[0][0].shape[0]
+    if count == 4:
+        tile = 64
+        return [
+            pl.pallas_call(
+                place_kernel,
+                grid=(rows // tile,),
+                in_specs=[pl.BlockSpec((tile, width), lambda i: (i, 0))] * 4,
+                out_specs=pl.BlockSpec((tile, FF), lambda i: (i, 0)),
+                out_shape=jax.ShapeDtypeStruct((rows, FF), f32),
+                compiler_params=pltpu.CompilerParams(vmem_limit_bytes=VMEM_LIMIT),
+                cost_estimate=pl.CostEstimate(flops=0, bytes_accessed=rows * FF * 8, transcendentals=0),
+                name="place_windows",
+            )(*some)
+            for some in both
+        ]
     me = lax.axis_index("shard")
-    width = grad_both.shape[1] // 2
-    rows = D // count
-
-    def part(owner, grad):
-        left = lax.dynamic_slice(two_all, (0, owner * rows), (two_all.shape[0], rows))
-        return contract_rows(left, grad).astype(bf16)
-
-    if shared_links(count):
-        owner = relay_owner(me)
-        return [part(owner, grad_both[:, :width]), part(owner, grad_both[:, width:]), part(me ^ 1, grad_both), part(me, grad_both)]
-    return [part(me ^ step, grad_both) for step in reversed(range(count))]
-
-
-def send_windows(parts, count):
-    if shared_links(count):
-        gate, up, beside, own = parts
-        return [own, swap(beside, 1), *(relay(gate, count)), *(relay(up, count))]
-    return [parts[-1]] + [swap(parts[count - 1 - step], step) for step in range(1, count)]
-
-
-def place_windows(parts, count):
-    size, width, starts, offsets = hidden_window(count)
-    rows = parts[0].shape[0]
-    if shared_links(count):
-        own, beside, gate_far, gate_diagonal, up_far, up_diagonal = parts
-        inputs = [own, beside, *gate_far, *gate_diagonal, *up_far, *up_diagonal]
-        tile = 64
-        return pl.pallas_call(
-            functools.partial(place_kernel, width),
-            grid=(rows // tile,),
-            in_specs=[pl.BlockSpec((tile, v.shape[1]), lambda i: (i, 0)) for v in inputs],
-            out_specs=[pl.BlockSpec((tile, FF), lambda i: (i, 0))] * 2,
-            out_shape=[jax.ShapeDtypeStruct((rows, FF), f32)] * 2,
-            compiler_params=pltpu.CompilerParams(vmem_limit_bytes=VMEM_LIMIT),
-            name="place_windows",
-        )(*inputs)
-    me = lax.axis_index("shard")
-    gathered = jnp.zeros((count, rows, 2 * width), bf16)
-    for step, part in enumerate(parts):
-        gathered = lax.dynamic_update_slice(gathered, part[None], (me ^ step, 0, 0))
     totals = []
-    for which in range(2):
-        pieces = []
-        for owner in range(count):
-            offset = which * width + offsets[owner]
-            pieces.append(gathered[owner, :, offset:offset + size])
+    for parts in both:
+        gathered = jnp.zeros((count, rows, width), bf16)
+        for step, part in enumerate(parts):
+            gathered = lax.dynamic_update_slice(gathered, part[None], (me ^ step, 0, 0))
+        pieces = [gathered[owner, :, offset:offset + size] for owner, offset in enumerate(offsets)]
         totals.append(jnp.concatenate(pieces, axis=1).astype(f32))
     return totals
 
@@ -1039,53 +1258,52 @@
     count = lax.axis_size("shard")
     size, width, starts, offsets = hidden_window(count)
     gains = (input_gain[0], query_gain[0], latent_gain[0], post_gain[0])
-    down_q, down_kv, query_up_all, latent_up_all, groups = first_move(
-        query_down[0], latent_down[0], query_up[0], latent_up[0], segment_ids, count
+    down_q, down_kv, query_up_all, latent_up_all, groups, gate_columns, up_columns = first_move(
+        query_down[0], latent_down[0], query_up[0], latent_up[0], segment_ids, gate_weight[0], up_weight[0], count
     )
     down_both = (down_q, down_kv)
-    down_rows = window_rows(down_weight[0], count)
-    weights = (down_both, query_up_all, latent_up_all, output_weight[0], down_rows)
     own_tables = tuple(t.reshape(-1, ROPE // 2) for t in slot_tables(segment_ids))
     tables = head_tables(groups)
 
-    def first_weights(all_in):
-        all_in, gate, up = together(all_in, gate_weight[0], up_weight[0])
-        if shared_links(count):
-            return all_in, relay_hidden(gate, up, count)
-        whole = spread_hidden(gate, up, count)
-        return all_in, lambda value: (value, whole)
-
+    weights = (down_both, query_up_all, latent_up_all, output_weight[0], gate_columns, up_columns, down_weight[0])
     start = tokens.astype(f32)
-    outputs, _, gate_up = layer_forward(start, own_tables, tables, gains, weights, True, first_weights)
-    leaving, low, received = outputs()
-    received, last = together(received, cotangent)
-    last = last.astype(f32)
+    last = cotangent.astype(f32)
+    last_down = (residual_scale * last).astype(bf16)
+    outputs, activated, _, gate_columns, up_columns, all_last = layer_forward(
+        start, own_tables, tables, gains, weights, True, shared_links(count), last_down
+    )
+    leaving, low, received, down_rows = outputs(activated)
+    weights = weights[:4] + (gate_columns, up_columns, down_rows)
     entering = jnp.where(at_start, start, received.astype(f32))
-    outputs, kept, _ = layer_forward(
-        entering, own_tables, tables, gains, weights, False, lambda all_in: (all_in, lambda value: (value, gate_up))
-    )
-    weights = weights[:4] + (gate_up, down_rows)
+    _, kept_activated, kept, _, _, _ = layer_forward(
+        entering, own_tables, tables, gains, weights, False, None, all_last
+    )
 
     (hidden, scale_in, normed, latent_q, scale_q, latent, scale_kv, query_in, kv_in,
      shared, queries, keyval, logs, attended, mixed, normed_two, gate, up) = kept
     rows = hidden.shape[0]
-    _, grad_mixed, _, grad_branch = mlp_backward(last, kept, gains, weights)
     own_two = lax.dynamic_slice_in_dim(normed_two, lax.axis_index("shard") * rows, rows, 0)
+    _, _, _, grad_mixed, _, grad_branch = mlp_backward(last, kept, gains, weights, lambda own: all_last, at_start)
     grad_branch, own_two = together(grad_branch, own_two)
     two_all = lax.all_gather(own_two, ("rep", "shard"), axis=0, tiled=True)
-    grad, _, _ = attention_backward(grad_mixed, grad_branch, kept, own_tables, tables, gains, weights)
-    returned = lax.ppermute(grad.astype(bf16), "section", [(1, 0)])
+    grad, _, _, _ = attention_backward(
+        grad_mixed, grad_branch, kept, own_tables, tables, gains, weights, at_start
+    )
+    grad_low, kept_activated = together(grad.astype(bf16), kept_activated)
+    returned = lax.ppermute(grad_low, "section", [(1, 0)])
+    leaving, boundary = down_project(kept_activated, down_rows, mixed, False)
     incoming = jnp.where(at_start, returned.astype(f32), last)
-
-    own_down, grad_mixed, dgain_post, grad_branch = mlp_backward(incoming, kept, gains, weights)
-    grad_branch, own_down, two_all = together(grad_branch, own_down, two_all)
+    incoming, boundary = together(incoming, boundary)
+
+    own_grads, two_all, own_down, grad_mixed, dgain_post, grad_branch = mlp_backward(
+        incoming, kept, gains, weights, lambda own: gather(own, 1, 512), two_all
+    )
     down_all = lax.all_gather(own_down, ("rep", "shard"), axis=0, tiled=True)
     part_output = contract_rows(attended, grad_branch).astype(bf16)
     grad_branch, part_output = together(grad_branch, part_output)
-    total_output = lax.psum(part_output, "rep")
-
-    grad, found, (dgain_input, dgain_query, dgain_latent) = attention_backward(
-        grad_mixed, grad_branch, kept, own_tables, tables, gains, weights
+
+    grad, found, (dgain_input, dgain_query, dgain_latent), down_all = attention_backward(
+        grad_mixed, grad_branch, kept, own_tables, tables, gains, weights, down_all
     )
     grad_branch, grad_query, grad_keyval, grad_lat = found
     gain_terms = jnp.concatenate([dgain_input, dgain_query, dgain_latent, dgain_post])[None]
@@ -1094,34 +1312,58 @@
     ).reshape(normed.shape[0] * count, -1)
     part_query = contract_rows(query_in, grad_query).astype(bf16)
     part_latent = contract_rows(kv_in, grad_keyval).astype(bf16)
-    lat_all, gains_all, part_query, part_latent = last_move(
-        grad_lat, gain_terms, part_query, part_latent, count
-    )
-    part_down = contract_rows(normed_rows, lat_all[:, :QRANK + KVRANK + ROPE]).astype(bf16)
-    part_gains = jnp.sum(gains_all, axis=0).astype(bf16)
-    part_down, part_query, part_latent, down_all = together(part_down, part_query, part_latent, down_all)
-    part_down, total_output = together(part_down, total_output)
-    side = part_down.shape[1]
-    gain_rows = -(-part_gains.shape[0] // side)
-    part_gains = jnp.pad(part_gains, (0, gain_rows * side - part_gains.shape[0])).reshape(gain_rows, side)
-    part_down = jnp.concatenate([part_down, part_gains], axis=0)
-    total_down_both, total_query, total_latent = (
-        part.astype(f32) for part in lax.psum((part_down, part_query, part_latent), "rep")
-    )
-    gain_totals = total_down_both[-gain_rows:].reshape(-1)
-    total_down_both = total_down_both[:-gain_rows]
-
-    both = project(two_all, gate_up)
-    gate_all, up_all = both[:, :width], both[:, width:]
-    activated_all = (jax.nn.silu(gate_all) * up_all).astype(bf16)
-    grad_both = gate_backward(contract_cols(down_all, down_rows), gate_all, up_all)
-    payloads = window_gradients(two_all, grad_both, count)
-    activated_all, *payloads = together(activated_all, *payloads)
-    hidden_parts = send_windows(payloads, count)
-    total_down = contract_rows(activated_all, down_all)
-    offset = take_at(offsets, lax.axis_index("shard"))
-    total_down = lax.dynamic_slice_in_dim(total_down, offset, size, 0)
-    leaving, boundary = outputs(lambda value: together(value, total_down)[0])
+    exchanged, exchange_end = last_move(grad_lat, gain_terms, part_query, part_latent, count)
+    part_output, down_all, two_all, own_grads, normed_rows = together(
+        part_output, down_all, two_all, own_grads, normed_rows
+    )
+    total_output = lax.psum(part_output, "rep")
+    if count == 4:
+        activated_all, grad_gate, grad_up = recompute(
+            two_all, down_all, gate_columns, up_columns, down_rows, (kept_activated, *own_grads)
+        )
+    else:
+        gate_all = project(two_all, gate_columns)
+        up_all = project(two_all, up_columns)
+        activated_all = (jax.nn.silu(gate_all) * up_all).astype(bf16)
+        grad_gate, grad_up = gate_backward(contract_cols(down_all, down_rows), gate_all, up_all)
+    def attention_shares(exchanged):
+        lat_all, gains_all, part_query, part_latent = exchange_end(exchanged)
+        part_down = contract_rows(normed_rows, lat_all[:, :QRANK + KVRANK + ROPE]).astype(bf16)
+        part_gains = jnp.sum(gains_all, axis=0).astype(bf16)
+        side = part_down.shape[1]
+        gain_rows = -(-part_gains.shape[0] // side)
+        part_gains = jnp.pad(part_gains, (0, gain_rows * side - part_gains.shape[0])).reshape(gain_rows, side)
+        part_down = jnp.concatenate([part_down, part_gains], axis=0)
+        return part_down, part_latent, part_query
+
+    me = lax.axis_index("shard")
+    if count == 4:
+        away = [owner_gradients(two_all, grad_gate, grad_up, me ^ 2, count)]
+        two_all, _, exchanged, total_output = together(two_all, away[0], exchanged, total_output)
+        away.append(owner_gradients(two_all, grad_gate, grad_up, me ^ 3, count))
+        brought = [[swap(away[step][i], 2 + step) for step in range(2)] for i in range(2)]
+        shares = attention_shares(exchanged)
+        two_all, _, *shares = together(two_all, away[1], *shares)
+        total_down_both, total_latent, total_query = lax.psum(tuple(shares), "rep")
+        near = chip_gradients(two_all, grad_gate, grad_up)
+        activated_all, near[0], *brought[0] = together(activated_all, near[0], *brought[0])
+        total_down = down_gradient(activated_all, down_all)
+        hidden_parts = [[near[2 + i], swap(near[i], 1), *brought[i]] for i in range(2)]
+    else:
+        parts = [owner_gradients(two_all, grad_gate, grad_up, me ^ step, count) for step in range(count)]
+        hidden_parts = [
+            [swap(parts[step][i], step) if step else parts[step][i] for step in range(count)] for i in range(2)
+        ]
+        total_down_both, total_latent, total_query = lax.psum(attention_shares(exchanged), "rep")
+        total_down = contract_rows(activated_all, down_all)
+        total_down = lax.dynamic_slice_in_dim(total_down, take_at(offsets, me), size, 0)
+    total_down, total_query, total_latent, hidden_parts[0][0] = together(
+        total_down, total_query, total_latent, hidden_parts[0][0]
+    )
+    gain_rows = total_down_both.shape[0] - D // count
+    gain_totals = total_down_both[-gain_rows:].reshape(-1).astype(f32)
+    total_down_both = total_down_both[:-gain_rows].astype(f32)
+    total_query, total_latent = total_query.astype(f32), total_latent.astype(f32)
     total_gate, total_up = place_windows(hidden_parts, count)
     first, second, third = D, D + QRANK, D + QRANK + KVRANK
     gain_totals = (gain_totals[:first], gain_totals[first:second], gain_totals[second:third], gain_totals[third:third + D])

time: 1460 us -> 1310 us (0.90)
  Pallas kernels: 659 us -> 861 us
  matrix products: 340 us -> 193 us
  waiting for transfers between devices: 192 us -> 106 us
  starting transfers between devices: 59.3 us -> 16.1 us
  local copies, waits for them, and re-layouts: 97.9 us -> 63.2 us
  other arithmetic: 76.6 us -> 52.1 us
    pallas_call x13 -> x16, Pallas kernels: 485 us -> 662 us  [the longest x11 466 us: comm_call(): pl.pallas_call(kernel, in_specs=vmem(len(inputs) - len(aliased)) + any_sp...]
    psum x1, waiting for transfers between devices: 99.3 us -> 0.01 us  [body(): total_down_both, total_latent, total_query = lax.psum(tuple(shares), 'rep')]
    ppermute x17 -> x1, waiting for transfers between devices: 93 us -> 0.01 us  [body(): returned = lax.ppermute(grad_low, 'section', [(1, 0)])]
    ppermute x3 -> x6, waiting for transfers between devices: 0.01 us -> 85.8 us  [swap(): lax.ppermute(value, 'shard', [(source, source ^ step) for source in range...]
    dot_general x11 -> x12, matrix products: 126 us -> 69.8 us  [project(): return jnp.dot(left, weight, preferred_element_type=f32)]
    dot_general x9 -> x8, matrix products: 113 us -> 66.2 us  [contract_rows(): lax.dot_general(left, right, (((0,), (0,)), ((), ())), preferred_element_...]
    dot_general x9 -> x8, matrix products: 100 us -> 57.4 us  [contract_cols(): lax.dot_general(left, right, (((1,), (1,)), ((), ())), preferred_element_...]
    ppermute x17 -> x1, starting transfers between devices: 35.1 us -> 1.28 us  [body(): returned = lax.ppermute(grad_low, 'section', [(1, 0)])]
  transfers between devices with their start and end apart: 25 -> 14, of which waited for: 5 -> 4; matrix products, arithmetic and copies ran while one was open for 28% -> 12% of each run, Pallas kernels for 23% -> 33%
where the time goes in v3:
time: 1310 us
  Pallas kernels  861 us (66%)
  matrix products  193 us (15%)
  waiting for transfers between devices  106 us (8%)
  local copies, waits for them, and re-layouts  63.2 us (5%)
  other arithmetic  52.1 us (4%)
  starting transfers between devices  16.1 us (1%)
  between operations  15.1 us (1%)
    pallas_call x11, Pallas kernels, comm_call(): pl.pallas_call(kernel, in_specs=vmem(len(inputs) - len(aliased)) + any_sp...  466 us
    pallas_call x1, Pallas kernels, move(): pl.pallas_call(functools.partial(move_kernel, len(wholes), [f for _, _, f...  154 us
    pallas_call x1, Pallas kernels, recompute(): pl.pallas_call(recompute_kernel, grid_spec=pltpu.PrefetchScalarGridSpec(n...  91.8 us
    ppermute x6, waiting for transfers between devices, swap(): lax.ppermute(value, 'shard', [(source, source ^ step) for source in range...  85.8 us
    dot_general x12, matrix products, project(): return jnp.dot(left, weight, preferred_element_type=f32)  69.8 us
    dot_general x8, matrix products, contract_rows(): lax.dot_general(left, right, (((0,), (0,)), ((), ())), preferred_element_...  66.2 us
    dot_general x8, matrix products, contract_cols(): lax.dot_general(left, right, (((1,), (1,)), ((), ())), preferred_element_...  57.4 us
    pallas_call x1, Pallas kernels, chip_gradients(): pl.pallas_call(chip_gradients_kernel, grid_spec=pltpu.PrefetchScalarGridS...  43.6 us
  transfers between devices with their start and end apart: 14, of which 4 were waited for; matrix products, arithmetic and copies ran while one was open for 12% of the time, Pallas kernels for 33%

profile of v3, /device:TPU:1, one launch (start us, length us, event | category | flops | bytes accessed | tf_op | source)
XLA Modules:
  0.0 1307.6 jit_solution(1391373766657495793)
XLA Ops:
  12.5 153.7 %first_move.1 = (bf16[4,640,768]{2,1,0:T(8,128)(2,1)}, bf16[4,640,288]{2,1,0:T(8,128)(2,1)}, s32[4,2,96]{2,1,0:T(2,128)}, bf16[4,192,1024]{2,1,0:T(8,128)(2,1)},...) custom-call(bf16[640,768]{1,0:T(8,128)(2,1)} %bitcast.157, ...), custom_call_target="tpu_custom_call" | custom-call | bytes 79465472 | tf_op jit(solution)/shard_map/first_move/pallas_call | solution.py:812
  173.8 16.3 %gather_rows.3 = bf16[768,1152]{1,0:T(8,128)(2,1)} custom-call(bf16[192,1152]{1,0:T(8,128)(2,1)} %fusion.34.own_ref), custom_call_target="tpu_custom_call" | custom-call | tf_op jit(solution)/shard_map/gather_rows/pallas_call | solution.py:397
  226.5 56.8 %output_norm.2 = (f32[192,2560]{1,0:T(8,128)}, bf16[768,2560]{1,0:T(8,128)(2,1)}, bf16[4,640,1664]{2,1,0:T(8,128)(2,1)}) custom-call(bf16[768,640]{1,0:T(8,128)(2,1)} %get-tuple-element.101.att_ref, bf16[640,2560]{1,0:T(8,128)(2,1)} %bitcast.133, f32[192,2560]{1,0:T(8,128)} %convert_element_type.138.hidden_ref, ...), custom_call_target="tpu_custom_call", output_to_operand_aliasing={{2}: (4, {})} | custom-call | tf_op jit(solution)/shard_map/output_norm/pallas_call | solution.py:397
  302.7 45.0 %down_project.2 = (f32[192,2560]{1,0:T(8,128)}, bf16[192,2560]{1,0:T(8,128)(2,1)}, bf16[192,2560]{1,0:T(8,128)(2,1)}, bf16[1664,2560]{1,0:T(8,128)(2,1)}) custom-call(bf16[768,1664]{1,0:T(8,128)(2,1)} %multiply_convert_fusion.5.act_ref, bf16[1600,2560]{1,0:T(8,128)(2,1)} %bitcast.141, f32[192,2560]{1,0:T(8,128)} %get-tuple-element.106.mixed_ref), custom_call_target="tpu_custom_call" | custom-call | tf_op jit(solution)/shard_map/down_project/pallas_call | solution.py:397
  355.9 16.3 %gather_rows.4 = bf16[768,1152]{1,0:T(8,128)(2,1)} custom-call(bf16[192,1152]{1,0:T(8,128)(2,1)} %fusion.35.own_ref), custom_call_target="tpu_custom_call" | custom-call | tf_op jit(solution)/shard_map/gather_rows/pallas_call | solution.py:397
  393.6 56.2 %output_norm.3 = (f32[192,2560]{1,0:T(8,128)}, bf16[768,2560]{1,0:T(8,128)(2,1)}) custom-call(bf16[768,640]{1,0:T(8,128)(2,1)} %get-tuple-element.110.att_ref, bf16[640,2560]{1,0:T(8,128)(2,1)} %bitcast.134, f32[192,2560]{1,0:T(8,128)} %copy-done.1, f32[1,2560]{1,0:T(1,128)} %gain_ref.7), custom_call_target="tpu_custom_call" | custom-call | tf_op jit(solution)/shard_map/output_norm/pallas_call | solution.py:397
  449.8 13.4 %fusion.105 = f32[768,1664]{1,0:T(8,128)} fusion(bf16[768,2560]{1,0:T(8,128)(2,1)} %get-tuple-element.111, bf16[2560,1664]{1,0:T(8,128)(2,1)} %bitcast.117), kind=kOutput, calls=%fused_computation.214 | convolution fusion | flops 6543114240 | bytes 17563648 | tf_op jit(solution)/shard_map/dot_general | solution.py:82
  476.1 14.4 %multiply_convert_fusion.2 = (bf16[768,1664]{1,0:T(8,128)(2,1)}, bf16[768,1664]{1,0:T(8,128)(2,1)}, bf16[768,1664]{1,0:T(8,128)(2,1)}, f32[768,1664]{1,0:T(8,128)}) fusion(f32[768,1664]{1,0:T(8,128)S(1)} %copy-done.53, f32[768,1664]{1,0:T(8,128)S(1)} %fusion.103, bf16[768,2560]{1,0:T(8,128)(2,1)S(1)} %copy-done.26, bf16[2560,1664]{1,0:T(8,128)(2,1)} %bitcast.111), kind=kOutput, calls=%fused_computation.2 | convolution fusion | flops 6563561472 | bytes 35454976 | tf_op jit(solution)/shard_map/dot_general | solution.py:82
  490.5 63.2 %mlp_back.2 = (f32[192,2560]{1,0:T(8,128)}, f32[1,2560]{1,0:T(1,128)}, bf16[768,2560]{1,0:T(8,128)(2,1)}) custom-call(bf16[768,1664]{1,0:T(8,128)(2,1)} %get-tuple-element.280.gate_ref, bf16[768,1664]{1,0:T(8,128)(2,1)} %get-tuple-element.281.up_ref, bf16[2560,1664]{1,0:T(8,128)(2,1)} %bitcast.118, bf16[2560,1664]{1,0:T(8,128)(2,1)} %bitcast.112, ...), custom_call_target="tpu_custom_call" | custom-call | tf_op jit(solution)/shard_map/mlp_back/pallas_call | solution.py:397
  577.2 19.4 %latent_back.2 = f32[192,1280]{1,0:T(8,128)} custom-call(bf16[768,1280]{1,0:T(8,128)(2,1)} %get-tuple-element.119.gq_ref, bf16[768,1280]{1,0:T(8,128)(2,1)} %get-tuple-element.120.gkv_ref, f32[768,128]{1,0:T(8,128)} %get-tuple-element.121.gsh_ref, bf16[768,1280]{1,0:T(8,128)(2,1)} %copy.116.qup_ref, bf16[256,1280]{1,0:T(8,128)(2,1)} %bitcast.135), custom_call_target="tpu_custom_call" | custom-call | tf_op jit(solution)/shard_map/latent_back/pallas_call | solution.py:397
  611.8 53.9 %down_project.3 = (f32[192,2560]{1,0:T(8,128)}, bf16[192,2560]{1,0:T(8,128)(2,1)}) custom-call(bf16[768,1664]{1,0:T(8,128)(2,1)} %get-tuple-element.124.act_ref.act_own, bf16[1664,2560]{1,0:T(8,128)(2,1)} %get-tuple-element.107.given_ref.rows_ref, f32[192,2560]{1,0:T(8,128)} %get-tuple-element.112.mixed_ref), custom_call_target="tpu_custom_call" | custom-call | tf_op jit(solution)/shard_map/down_project/pallas_call | solution.py:397
  669.8 28.7 %gather_rows.5 = bf16[768,2560]{1,0:T(8,128)(2,1)} custom-call(bf16[192,2560]{1,0:T(8,128)(2,1)} %multiply_convert_fusion.6.own_ref), custom_call_target="tpu_custom_call" | custom-call | tf_op jit(solution)/shard_map/gather_rows/pallas_call | solution.py:397
  704.2 16.7 %multiply_convert_fusion = (bf16[768,1664]{1,0:T(8,128)(2,1)}, bf16[768,1664]{1,0:T(8,128)(2,1)}) fusion(f32[768,1664]{1,0:T(8,128)} %fusion.105, f32[768,1664]{1,0:T(8,128)} %get-tuple-element.316, bf16[768,2560]{1,0:T(8,128)(2,1)} %gather_rows.5, bf16[1664,2560]{1,0:T(8,128)(2,1)} %get-tuple-element.107.given_ref.rows_ref), kind=kOutput, calls=%fused_computation | convolution fusion | flops 6559727616 | bytes 27787264 | tf_op jit(solution)/shard_map/dot_general | solution.py:78
  720.9 90.7 %mlp_back.3 = (f32[192,2560]{1,0:T(8,128)}, f32[1,2560]{1,0:T(1,128)}, bf16[768,2560]{1,0:T(8,128)(2,1)}) custom-call(bf16[768,1664]{1,0:T(8,128)(2,1)} %get-tuple-element.143.gate_ref.gate_own, bf16[768,1664]{1,0:T(8,128)(2,1)} %get-tuple-element.144.up_ref.up_own, bf16[2560,1664]{1,0:T(8,128)(2,1)} %bitcast.119, bf16[2560,1664]{1,0:T(8,128)(2,1)} %bitcast.113, ...), custom_call_target="tpu_custom_call" | custom-call | tf_op jit(solution)/shard_map/mlp_back/pallas_call | solution.py:397
  837.6 19.5 %latent_back.3 = f32[192,1280]{1,0:T(8,128)} custom-call(bf16[768,1280]{1,0:T(8,128)(2,1)} %get-tuple-element.133.gq_ref, bf16[768,1280]{1,0:T(8,128)(2,1)} %get-tuple-element.134.gkv_ref, f32[768,128]{1,0:T(8,128)} %get-tuple-element.135.gsh_ref, bf16[768,1280]{1,0:T(8,128)(2,1)} %copy.116.qup_ref, bf16[256,1280]{1,0:T(8,128)(2,1)} %bitcast.136), custom_call_target="tpu_custom_call" | custom-call | tf_op jit(solution)/shard_map/latent_back/pallas_call | solution.py:397
  893.0 91.8 %recompute.1 = (bf16[3072,1664]{1,0:T(8,128)(2,1)}, bf16[3072,1664]{1,0:T(8,128)(2,1)}, bf16[3072,1664]{1,0:T(8,128)(2,1)}) custom-call(s32[8]{0:T(128)} %compare_select_fusion.from_ref, s32[8]{0:T(128)} %compare_convert_fusion.own_ref, bf16[3072,2560]{1,0:T(8,128)(2,1)} %all-gather.6.cloned.1.call-done.two_ref, ...), custom_call_target="tpu_custom_call" | custom-call | tf_op jit(solution)/shard_map/recompute/pallas_call | solution.py:1166
  984.8 12.5 fusion.9
  1008.4 18.2 %all-reduce.12.cloned.1.call-done = bf16[640,2560]{1,0:T(8,128)(2,1)} async-done(((bf16[640,2560]{1,0:T(8,128)(2,1)}), bf16[640,2560]{1,0:T(8,128)(2,1)}) %all-reduce.12.cloned.1.call-update) | async-done | bytes 3276816 | tf_op jit(solution)/shard_map/psum | solution.py:1319
  1038.9 12.6 fusion.18
  1080.8 43.6 %chip_gradients.1 = (bf16[2,640,1664]{2,1,0:T(8,128)(2,1)}, bf16[2,640,1664]{2,1,0:T(8,128)(2,1)}) custom-call(s32[2]{0:T(128)} %pad_add_fusion.order_ref, bf16[3072,2560]{1,0:T(8,128)(2,1)} %all-gather.6.cloned.1.call-done.two_ref, bf16[3072,1664]{1,0:T(8,128)(2,1)} %get-tuple-element.145.gate_ref, bf16[3072,1664]{1,0:T(8,128)(2,1)} %get-tuple-element.146.up_ref), custom_call_target="tpu_custom_call" | custom-call | tf_op jit(solution)/shard_map/chip_gradients/pallas_call | solution.py:1105
  1139.8 78.3 %collective-permute-done.2.refs_3_ = bf16[640,1664]{1,0:T(8,128)(2,1)} collective-permute-done((bf16[640,1664]{1,0:T(8,128)(2,1)}, bf16[640,1664]{1,0:T(8,128)(2,1)}, u32[]{:S(2)}, u32[]{:S(2)}) %collective-permute-start.2) | collective-permute-done | bytes 2129952 | tf_op jit(solution)/shard_map/ppermute | solution.py:1039
  1218.1 36.6 %down_gradient.1 = f32[1600,2560]{1,0:T(8,128)} custom-call(bf16[3072,1664]{1,0:T(8,128)(2,1)} %get-tuple-element.156.act_ref, bf16[3072,2560]{1,0:T(8,128)(2,1)} %all-gather.8.cloned.1.call-done.down_ref), custom_call_target="tpu_custom_call" | custom-call | tf_op jit(solution)/shard_map/down_gradient/pallas_call | solution.py:1203
  1262.3 12.2 place_windows.3
  1287.7 12.2 place_windows.2
  (298 shorter events, 310.2 us)
Async XLA Ops:
  7.2 219.3 %all-gather.4.cloned.1.call-start = ((), (), s32[]{:S(2)}) async-start(), calls=%async_computation.2 | async-start | bytes 4915200 | tf_op jit(solution)/shard_map/all_gather | solution.py:440
  7.2 197.2 %copy-start.42 = (f32[16]{0:T(128)}, f32[16]{0:T(128)S(1)}, u32[]{:S(2)}) copy-start(f32[16]{0:T(128)S(1)} %multiply_exponential_fusion) | copy-start | bytes 196
  11.7 156.9 %copy-start.32 = (f32[192]{0:T(256)}, f32[192]{0:T(256)S(1)}, u32[]{:S(2)}) copy-start(f32[192]{0:T(256)S(1)} %convert_element_type.142) | copy-start | bytes 2308
  12.5 153.7 %copy-start.11 = (bf16[192,2560]{1,0:T(8,128)(2,1)S(1)}, bf16[192,2560]{1,0:T(8,128)(2,1)}, u32[]{:S(2)}) copy-start(bf16[192,2560]{1,0:T(8,128)(2,1)} %param.15) | copy-start | bytes 2949124
  172.6 17.4 %copy-start.12 = (bf16[192,2560]{1,0:T(8,128)(2,1)S(1)}, bf16[192,2560]{1,0:T(8,128)(2,1)}, u32[]{:S(2)}) copy-start(bf16[192,2560]{1,0:T(8,128)(2,1)} %param.29) | copy-start | bytes 2949124
  191.2 507.4 %all-gather.6.cloned.1.call-start = ((), (), s32[]{:S(2)}) async-start(), calls=%async_computation.3 | async-start | bytes 16711680 | tf_op jit(solution)/shard_map/all_gather | solution.py:1288
  351.6 249.6 %copy-start.9 = (f32[192,288]{1,0:T(8,128)}, f32[192,288]{1,0:T(8,128)S(1)}, u32[]{:S(2)}) copy-start(f32[192,288]{1,0:T(8,128)S(1)} %fusion.104) | copy-start | bytes 663556
  354.2 247.0 %copy-start.35 = (f32[192]{0:T(256)}, f32[192]{0:T(256)S(1)}, u32[]{:S(2)}) copy-start(f32[192]{0:T(256)S(1)} %get-tuple-element.308) | copy-start | bytes 2308
  354.2 247.0 %copy-start.46 = (f32[192]{0:T(256)}, f32[192]{0:T(256)S(1)}, u32[]{:S(2)}) copy-start(f32[192]{0:T(256)S(1)} %get-tuple-element.307) | copy-start | bytes 2308
  354.9 22.8 %copy-start.40 = (f32[192]{0:T(256)}, f32[192]{0:T(256)S(1)}, u32[]{:S(2)}) copy-start(f32[192]{0:T(256)S(1)} %get-tuple-element.310) | copy-start | bytes 2308
  553.8 311.4 %all-gather.8.cloned.1.call-start = ((), (), s32[]{:S(2)}) async-start(), calls=%async_computation.4 | async-start | bytes 16711680 | tf_op jit(solution)/shard_map/all_gather | solution.py:1301
  610.5 55.2 %collective-permute-start = (bf16[192,2560]{1,0:T(8,128)(2,1)}, bf16[192,2560]{1,0:T(8,128)(2,1)}, u32[]{:S(2)}, u32[]{:S(2)}) collective-permute-start(bf16[192,2560]{1,0:T(8,128)(2,1)} %add_convert_fusion), channel_id=1, source_target_pairs={{16,0},{17,1},{18,2},{19,3},{20,4},{21,5},{22,6},{23,7},{24,8},{25... | collective-permute-start | bytes 2949128 | tf_op jit(solution)/shard_map/ppermute | solution.py:1293
  699.6 186.3 %all-to-all-start = ((bf16[4,192,640]{2,1,0:T(8,128)(2,1)}), bf16[4,192,640]{2,1,0:T(8,128)(2,1)}, u32[]{:S(2)}, u32[]{:S(2)}) async-start(bf16[4,192,640]{2,1,0:T(8,128)(2,1)} %bitcast.149), calls=%async_computation | async-start | bytes 1966080 | tf_op jit(solution)/shard_map/all_to_all | solution.py:1310
  720.9 90.7 %copy-start.24 = (bf16[768,640]{1,0:T(8,128)(2,1)S(1)}, bf16[768,640]{1,0:T(8,128)(2,1)}, u32[]{:S(2)}) copy-start(bf16[768,640]{1,0:T(8,128)(2,1)} %get-tuple-element.110.att_ref) | copy-start | bytes 2949124
  837.6 19.6 %copy-start.45 = (f32[1,2560]{1,0:T(1,128)S(1)}, f32[1,2560]{1,0:T(1,128)}, u32[]{:S(2)}) copy-start(f32[1,2560]{1,0:T(1,128)} %get-tuple-element.147) | copy-start | bytes 30724
  885.9 140.7 %all-to-all-start.1 = ((bf16[4,464,1280]{2,1,0:T(8,128)(2,1)}), bf16[4,464,1280]{2,1,0:T(8,128)(2,1)}, u32[]{:S(2)}, u32[]{:S(2)}) async-start(bf16[4,464,1280]{2,1,0:T(8,128)(2,1)} %pad_maximum_fusion), calls=%async_computation.1 | async-start | bytes 9502720 | tf_op jit(solution)/shard_map/all_to_all | solution.py:888
  891.4 135.2 %all-reduce.12.cloned.1.call-start = ((), (), s32[]{:S(2)}) async-start(), calls=%async_computation.5 | async-start | bytes 6553600 | tf_op jit(solution)/shard_map/psum | solution.py:1319
  892.0 382.5 %all-reduce.14.cloned.1.call-start = ((), (), s32[]{:S(2)}) async-start(), calls=%async_computation.6 | async-start | bytes 7245824 | tf_op jit(solution)/shard_map/psum | solution.py:1347
  1077.0 62.9 %collective-permute-start.1 = (bf16[640,1664]{1,0:T(8,128)(2,1)}, bf16[640,1664]{1,0:T(8,128)(2,1)}, u32[]{:S(2)}, u32[]{:S(2)}) collective-permute-start(bf16[640,1664]{1,0:T(8,128)(2,1)} %fusion.9), channel_id=1, source_target_pairs={{0,2},{1,3},{2,0},{3,1},{4,6},{5,7},{6,4},{7,5},{8,10},{9,11},{10,... | collective-permute-start | bytes 6389768 | tf_op jit(solution)/shard_map/ppermute | solution.py:1039
  1078.2 176.6 %collective-permute-start.5 = (bf16[640,1664]{1,0:T(8,128)(2,1)}, bf16[640,1664]{1,0:T(8,128)(2,1)}, u32[]{:S(2)}, u32[]{:S(2)}) collective-permute-start(bf16[640,1664]{1,0:T(8,128)(2,1)} %fusion.12), channel_id=1, source_target_pairs={{0,2},{1,3},{2,0},{3,1},{4,6},{5,7},{6,4},{7,5},{8,10},{9,11},{10,... | collective-permute-start | bytes 6389768 | tf_op jit(solution)/shard_map/ppermute | solution.py:1039
  1078.4 139.7 %collective-permute-start.2 = (bf16[640,1664]{1,0:T(8,128)(2,1)}, bf16[640,1664]{1,0:T(8,128)(2,1)}, u32[]{:S(2)}, u32[]{:S(2)}) collective-permute-start(bf16[640,1664]{1,0:T(8,128)(2,1)} %fusion.15), channel_id=1, source_target_pairs={{0,3},{1,2},{2,1},{3,0},{4,7},{5,6},{6,5},{7,4},{8,11},{9,10},{10,... | collective-permute-start | bytes 6389768 | tf_op jit(solution)/shard_map/ppermute | solution.py:1039
  1080.8 181.5 %collective-permute-start.6 = (bf16[640,1664]{1,0:T(8,128)(2,1)}, bf16[640,1664]{1,0:T(8,128)(2,1)}, u32[]{:S(2)}, u32[]{:S(2)}) collective-permute-start(bf16[640,1664]{1,0:T(8,128)(2,1)} %fusion.18), channel_id=1, source_target_pairs={{0,3},{1,2},{2,1},{3,0},{4,7},{5,6},{6,5},{7,4},{8,11},{9,10},{10,... | collective-permute-start | bytes 6389768 | tf_op jit(solution)/shard_map/ppermute | solution.py:1039
  1129.2 125.5 %collective-permute-start.4 = (bf16[640,1664]{1,0:T(8,128)(2,1)}, bf16[640,1664]{1,0:T(8,128)(2,1)}, u32[]{:S(2)}, u32[]{:S(2)}) collective-permute-start(bf16[640,1664]{1,0:T(8,128)(2,1)} %get-tuple-element.284), channel_id=1, source_target_pairs={{0,1},{1,0},{2,3},{3,2},{4,5},{5,4},{6,7},{7,6},{8,9},{9,8},{10,11... | collective-permute-start | bytes 6389768 | tf_op jit(solution)/shard_map/ppermute | solution.py:1039
  1254.7 31.6 %collective-permute-start.3 = (bf16[640,1664]{1,0:T(8,128)(2,1)}, bf16[640,1664]{1,0:T(8,128)(2,1)S(1)}, u32[]{:S(2)}, u32[]{:S(2)}) collective-permute-start(bf16[640,1664]{1,0:T(8,128)(2,1)} %get-tuple-element.163), channel_id=1, source_target_pairs={{0,1},{1,0},{2,3},{3,2},{4,5},{5,4},{6,7},{7,6},{8,9},{9,8},{10,11... | collective-permute-start | bytes 6389768 | tf_op jit(solution)/shard_map/ppermute | solution.py:1039
  (46 other events, 220.0 us)
Sparse Core Ops, SparseCore 0:
  191.3 35.1 all-gather.3
  553.9 140.8 all-gather.5
  698.7 149.4 all-gather.7
  894.3 132.3 all-reduce.11
  1076.5 136.3 all-reduce.13

commit v4 on v3

--- a/solution.py
+++ b/solution.py
@@ -941,15 +941,15 @@
     attended, queries, keyval, logs = attend(
         project(query_in, query_up), project(kv_in, latent_up), shared, tables
     )
-    attended, early = together(attended, early)
     if lacking:
         mixed, normed_two, up_weight = output_norm(attended, output_weight, hidden, post_gain, up_weight)
     else:
         mixed, normed_two = output_norm(attended, output_weight, hidden, post_gain)
+    normed_two, early = together(normed_two, early)
     merge = lambda value: value.reshape(D, -1)
-    gate = project(normed_two, merge(gate_weight))
-    up = project(normed_two, merge(up_weight))
-    activated = (jax.nn.silu(gate) * up).astype(bf16)
+    gate = project(normed_two, merge(gate_weight)).astype(bf16)
+    up = project(normed_two, merge(up_weight)).astype(bf16)
+    activated = (jax.nn.silu(gate.astype(f32)) * up.astype(f32)).astype(bf16)
     def outputs(value):
         return down_project(value, down_weight, mixed, passing)
 
@@ -969,12 +969,12 @@
     mixed, gate, up = kept[14], kept[16], kept[17]
     gate_weight, up_weight, down_weight = weights[4:]
     own_down = (residual_scale * grad_out).astype(bf16)
-    grad_down, own_down, wanted = together(gather_down(own_down), own_down, wanted)
-    grad_gate, grad_up = gate_backward(contract_cols(grad_down, down_weight), gate, up)
+    grad_down, wanted = together(gather_down(own_down), wanted)
+    grad_gate, grad_up = gate_backward(contract_cols(grad_down, down_weight), gate.astype(f32), up.astype(f32))
     grad_mixed, dgain_post, grad_branch = mlp_back(
         grad_gate, grad_up, gate_weight, up_weight, mixed, grad_out, gains[3]
     )
-    return (grad_gate, grad_up), wanted, own_down, grad_mixed, dgain_post[0], grad_branch
+    return (grad_gate, grad_up), wanted, grad_down, grad_mixed, dgain_post[0], grad_branch
 
 
 def attention_backward(grad_mixed, grad_branch, kept, own_tables, tables, gains, weights, wanted):
@@ -1118,11 +1118,8 @@
     return [gate[0], up[0], gate[1], up[1]]
 
 
-RECOMPUTE_ROWS = 384
-
-
-def recompute_kernel(from_ref, own_ref, two_ref, down_ref, gate_ref, up_ref, rows_ref, act_own, gate_own, up_own,
-                     act_out, gate_out, up_out):
+def recompute_kernel(from_ref, own_ref, here_ref, two_ref, near_ref, beside_ref, gate_ref, up_ref, rows_ref,
+                     act_own, gate_own, up_own, act_out, gate_out, up_out, down_ref):
     place = pl.program_id(0)
     width = gate_ref.shape[1]
     piece = 512
@@ -1132,6 +1129,14 @@
         act_out[...] = act_own[...]
         gate_out[...] = gate_own[...]
         up_out[...] = up_own[...]
+
+    @pl.when((own_ref[place] == 0) & (here_ref[place] == 1))
+    def _():
+        down_ref[...] = near_ref[...]
+
+    @pl.when((own_ref[place] == 0) & (here_ref[place] == 0))
+    def _():
+        down_ref[...] = beside_ref[...]
 
     @pl.when(own_ref[place] == 0)
     def _():
@@ -1151,33 +1156,36 @@
             tile(rest, rest)
 
 
-def recompute(two_all, down_all, gate_columns, up_columns, down_rows, own):
+def recompute(two_all, down_halves, gate_columns, up_columns, down_rows, own):
+    reps = lax.axis_size("rep")
     tokens, width = two_all.shape[0], gate_columns.shape[1]
-    group = own[0].shape[0]
-    tile = RECOMPUTE_ROWS
-    each_group = group // tile
+    tile = own[0].shape[0] // 2
     places = jnp.arange(tokens // tile, dtype=jnp.int32)
-    is_own = places // each_group == lax.axis_index("rep")
-    source = jnp.where(is_own, places % each_group, 0).astype(jnp.int32)
-    whole = lambda value: pl.BlockSpec(value.shape, lambda i, a, b: (0, 0), pipeline_mode=pl.Buffered(1))
-    wide = pl.BlockSpec((tile, D), lambda i, a, b: (i, 0))
-    mine = pl.BlockSpec((tile, width), lambda i, a, b: (a[i], 0))
-    part = pl.BlockSpec((tile, width), lambda i, a, b: (i, 0))
+    half = places // reps
+    is_own = places % reps == lax.axis_index("rep")
+    is_here = half == lax.axis_index("shard") % 2
+    whole = lambda value: pl.BlockSpec(value.shape, lambda i, a, b, c: (0, 0), pipeline_mode=pl.Buffered(1))
+    wide = pl.BlockSpec((tile, D), lambda i, a, b, c: (i, 0))
+    again = pl.BlockSpec((tile, D), lambda i, a, b, c: (i % reps, 0))
+    mine = pl.BlockSpec((tile, width), lambda i, a, b, c: (a[i], 0), pipeline_mode=pl.Buffered(1))
+    part = pl.BlockSpec((tile, width), lambda i, a, b, c: (i, 0))
     return pl.pallas_call(
         recompute_kernel,
         grid_spec=pltpu.PrefetchScalarGridSpec(
-            num_scalar_prefetch=2,
+            num_scalar_prefetch=3,
             grid=(tokens // tile,),
-            in_specs=[wide, wide, whole(gate_columns), whole(up_columns), whole(down_rows), mine, mine, mine],
+            in_specs=[wide, again, again, whole(gate_columns), whole(up_columns), whole(down_rows), mine, mine, mine],
             out_specs=[part] * 3,
+            scratch_shapes=[pltpu.VMEM((tile, D), bf16)],
         ),
         out_shape=[jax.ShapeDtypeStruct((tokens, width), bf16)] * 3,
         compiler_params=pltpu.CompilerParams(vmem_limit_bytes=VMEM_LIMIT),
         name="recompute",
-    )(source, is_own.astype(jnp.int32), two_all, down_all, gate_columns, up_columns, down_rows, *own)
-
-
-def down_gradient_kernel(act_ref, down_ref, out_ref, turned):
+    )(half, is_own.astype(jnp.int32), is_here.astype(jnp.int32), two_all, *down_halves,
+      gate_columns, up_columns, down_rows, *own)
+
+
+def down_gradient_kernel(act_ref, near_ref, beside_ref, out_ref, turned):
     tokens, width = act_ref.shape
     size = out_ref.shape[0]
     piece = 512
@@ -1187,65 +1195,78 @@
         for start in range(0, tokens, piece):
             turned[:, start:start + piece] = act_ref[start:start + piece, :].T
 
-    offset = lax.axis_index("shard") % 2 * (width - size)
+    core = lax.axis_index("shard") % 2
+    offset = core * (width - size)
     half = size // 2
+    some = tokens // 2
+    near = pl.ds(pl.multiple_of(core * some, LANES), some)
+    beside = pl.ds(pl.multiple_of((1 - core) * some, LANES), some)
 
     def tile(step):
         rows = pl.ds(pl.multiple_of(step * half, 16), half)
-        out_ref[rows, :] = project(turned[pl.ds(pl.multiple_of(step * half + offset, 16), half), :], down_ref[...])
+        source = pl.ds(pl.multiple_of(step * half + offset, 16), half)
+        out_ref[rows, :] = project(turned[source, near], near_ref[...]) + project(turned[source, beside], beside_ref[...])
 
     each(2, False, tile)
 
 
-def down_gradient(activated_all, down_all):
+def down_gradient(activated_all, down_halves):
     tokens, width = activated_all.shape
     size, piece = FF // 4, 512
     return pl.pallas_call(
         down_gradient_kernel,
         grid=(D // piece,),
         in_specs=[pl.BlockSpec((tokens, width), lambda i: (0, 0), pipeline_mode=pl.Buffered(1)),
-                  pl.BlockSpec((tokens, piece), lambda i: (0, i))],
+                  pl.BlockSpec((tokens // 2, piece), lambda i: (0, i)), pl.BlockSpec((tokens // 2, piece), lambda i: (0, i))],
         out_specs=pl.BlockSpec((size, piece), lambda i: (0, i)),
         out_shape=jax.ShapeDtypeStruct((size, D), f32),
         scratch_shapes=[pltpu.VMEM((width, tokens), bf16)],
         compiler_params=pltpu.CompilerParams(vmem_limit_bytes=VMEM_LIMIT),
         name="down_gradient",
-    )(activated_all, down_all)
-
-
-def owner_gradients(two_all, grad_gate, grad_up, owner, count):
+    )(activated_all, *down_halves)
+
+
+def half_everywhere(group, count):
+    if count != 4:
+        return group
+    rows = group.shape[0] // 2
+    half = lax.dynamic_slice_in_dim(group, lax.axis_index("shard") % 2 * rows, rows, 0)
+    return lax.all_gather(half, "rep", axis=0, tiled=True)
+
+
+def everyone(half, count):
+    if count != 4:
+        return lax.all_gather(half, "rep", axis=0, tiled=True)
+    return lax.all_gather(half, "shard", axis=0, tiled=True, axis_index_groups=[[0, 1], [2, 3]])
+
+
+def owner_gradient(two_all, grad, owner, count):
     rows = D // count
     left = lax.dynamic_slice(two_all, (0, owner * rows), (two_all.shape[0], rows))
-    return [contract_rows(left, grad).astype(bf16) for grad in (grad_gate, grad_up)]
-
-
-def place_windows(both, count):
+    return contract_rows(left, grad).astype(bf16)
+
+
+def place_windows(parts, count):
     size, width, starts, offsets = hidden_window(count)
-    rows = both[0][0].shape[0]
+    rows = parts[0].shape[0]
     if count == 4:
         tile = 64
-        return [
-            pl.pallas_call(
-                place_kernel,
-                grid=(rows // tile,),
-                in_specs=[pl.BlockSpec((tile, width), lambda i: (i, 0))] * 4,
-                out_specs=pl.BlockSpec((tile, FF), lambda i: (i, 0)),
-                out_shape=jax.ShapeDtypeStruct((rows, FF), f32),
-                compiler_params=pltpu.CompilerParams(vmem_limit_bytes=VMEM_LIMIT),
-                cost_estimate=pl.CostEstimate(flops=0, bytes_accessed=rows * FF * 8, transcendentals=0),
-                name="place_windows",
-            )(*some)
-            for some in both
-        ]
+        return pl.pallas_call(
+            place_kernel,
+            grid=(rows // tile,),
+            in_specs=[pl.BlockSpec((tile, width), lambda i: (i, 0))] * 4,
+            out_specs=pl.BlockSpec((tile, FF), lambda i: (i, 0)),
+            out_shape=jax.ShapeDtypeStruct((rows, FF), f32),
+            compiler_params=pltpu.CompilerParams(vmem_limit_bytes=VMEM_LIMIT),
+            cost_estimate=pl.CostEstimate(flops=0, bytes_accessed=rows * FF * 8, transcendentals=0),
+            name="place_windows",
+        )(*parts)
     me = lax.axis_index("shard")
-    totals = []
-    for parts in both:
-        gathered = jnp.zeros((count, rows, width), bf16)
-        for step, part in enumerate(parts):
-            gathered = lax.dynamic_update_slice(gathered, part[None], (me ^ step, 0, 0))
-        pieces = [gathered[owner, :, offset:offset + size] for owner, offset in enumerate(offsets)]
-        totals.append(jnp.concatenate(pieces, axis=1).astype(f32))
-    return totals
+    gathered = jnp.zeros((count, rows, width), bf16)
+    for step, part in enumerate(parts):
+        gathered = lax.dynamic_update_slice(gathered, part[None], (me ^ step, 0, 0))
+    pieces = [gathered[owner, :, offset:offset + size] for owner, offset in enumerate(offsets)]
+    return jnp.concatenate(pieces, axis=1).astype(f32)
 
 
 def together(*values):
@@ -1281,29 +1302,27 @@
 
     (hidden, scale_in, normed, latent_q, scale_q, latent, scale_kv, query_in, kv_in,
      shared, queries, keyval, logs, attended, mixed, normed_two, gate, up) = kept
-    rows = hidden.shape[0]
-    own_two = lax.dynamic_slice_in_dim(normed_two, lax.axis_index("shard") * rows, rows, 0)
+    half_two = half_everywhere(normed_two, count)
     _, _, _, grad_mixed, _, grad_branch = mlp_backward(last, kept, gains, weights, lambda own: all_last, at_start)
-    grad_branch, own_two = together(grad_branch, own_two)
-    two_all = lax.all_gather(own_two, ("rep", "shard"), axis=0, tiled=True)
-    grad, _, _, _ = attention_backward(
-        grad_mixed, grad_branch, kept, own_tables, tables, gains, weights, at_start
-    )
+    grad, _, _, half_two = attention_backward(
+        grad_mixed, grad_branch, kept, own_tables, tables, gains, weights, half_two
+    )
+    two_all = everyone(half_two, count)
     grad_low, kept_activated = together(grad.astype(bf16), kept_activated)
     returned = lax.ppermute(grad_low, "section", [(1, 0)])
     leaving, boundary = down_project(kept_activated, down_rows, mixed, False)
     incoming = jnp.where(at_start, returned.astype(f32), last)
     incoming, boundary = together(incoming, boundary)
 
-    own_grads, two_all, own_down, grad_mixed, dgain_post, grad_branch = mlp_backward(
+    own_grads, two_all, grad_down, grad_mixed, dgain_post, grad_branch = mlp_backward(
         incoming, kept, gains, weights, lambda own: gather(own, 1, 512), two_all
     )
-    down_all = lax.all_gather(own_down, ("rep", "shard"), axis=0, tiled=True)
+    half_down = half_everywhere(grad_down, count)
     part_output = contract_rows(attended, grad_branch).astype(bf16)
     grad_branch, part_output = together(grad_branch, part_output)
 
-    grad, found, (dgain_input, dgain_query, dgain_latent), down_all = attention_backward(
-        grad_mixed, grad_branch, kept, own_tables, tables, gains, weights, down_all
+    grad, found, (dgain_input, dgain_query, dgain_latent), _ = attention_backward(
+        grad_mixed, grad_branch, kept, own_tables, tables, gains, weights, at_start
     )
     grad_branch, grad_query, grad_keyval, grad_lat = found
     gain_terms = jnp.concatenate([dgain_input, dgain_query, dgain_latent, dgain_post])[None]
@@ -1312,11 +1331,12 @@
     ).reshape(normed.shape[0] * count, -1)
     part_query = contract_rows(query_in, grad_query).astype(bf16)
     part_latent = contract_rows(kv_in, grad_keyval).astype(bf16)
+    gain_terms, half_down = together(gain_terms, half_down)
     exchanged, exchange_end = last_move(grad_lat, gain_terms, part_query, part_latent, count)
-    part_output, down_all, two_all, own_grads, normed_rows = together(
-        part_output, down_all, two_all, own_grads, normed_rows
-    )
+    part_output, half_down = together(part_output, half_down)
+    down_all = [half_down, swap(half_down, 1)] if count == 4 else everyone(half_down, count)
     total_output = lax.psum(part_output, "rep")
+    down_all, two_all, own_grads, normed_rows = together(down_all, two_all, own_grads, normed_rows)
     if count == 4:
         activated_all, grad_gate, grad_up = recompute(
             two_all, down_all, gate_columns, up_columns, down_rows, (kept_activated, *own_grads)
@@ -1338,33 +1358,38 @@
 
     me = lax.axis_index("shard")
     if count == 4:
-        away = [owner_gradients(two_all, grad_gate, grad_up, me ^ 2, count)]
-        two_all, _, exchanged, total_output = together(two_all, away[0], exchanged, total_output)
-        away.append(owner_gradients(two_all, grad_gate, grad_up, me ^ 3, count))
-        brought = [[swap(away[step][i], 2 + step) for step in range(2)] for i in range(2)]
+        grad_gate, grad_up, total_output = together(grad_gate, grad_up, total_output)
+        away = [owner_gradient(two_all, grad_gate, me ^ step, count) for step in (2, 3)]
+        brought = [[swap(part, 2 + i) for i, part in enumerate(away)]]
+        two_all, _, exchanged, total_output = together(two_all, away, exchanged, total_output)
         shares = attention_shares(exchanged)
-        two_all, _, *shares = together(two_all, away[1], *shares)
+        two_all, *shares = together(two_all, *shares)
         total_down_both, total_latent, total_query = lax.psum(tuple(shares), "rep")
+        away = [owner_gradient(two_all, grad_up, me ^ step, count) for step in (2, 3)]
+        brought.append([swap(part, 2 + i) for i, part in enumerate(away)])
+        two_all, _ = together(two_all, away)
         near = chip_gradients(two_all, grad_gate, grad_up)
-        activated_all, near[0], *brought[0] = together(activated_all, near[0], *brought[0])
+        activated_all, near[0], brought[0] = together(activated_all, near[0], brought[0])
         total_down = down_gradient(activated_all, down_all)
         hidden_parts = [[near[2 + i], swap(near[i], 1), *brought[i]] for i in range(2)]
+        total_down, hidden_parts[0] = together(total_down, hidden_parts[0])
     else:
-        parts = [owner_gradients(two_all, grad_gate, grad_up, me ^ step, count) for step in range(count)]
+        parts = [
+            [owner_gradient(two_all, grad, me ^ step, count) for grad in (grad_gate, grad_up)] for step in range(count)
+        ]
         hidden_parts = [
             [swap(parts[step][i], step) if step else parts[step][i] for step in range(count)] for i in range(2)
         ]
         total_down_both, total_latent, total_query = lax.psum(attention_shares(exchanged), "rep")
         total_down = contract_rows(activated_all, down_all)
         total_down = lax.dynamic_slice_in_dim(total_down, take_at(offsets, me), size, 0)
-    total_down, total_query, total_latent, hidden_parts[0][0] = together(
-        total_down, total_query, total_latent, hidden_parts[0][0]
-    )
+    total_gate = place_windows(hidden_parts[0], count)
+    total_gate, hidden_parts[1][0] = together(total_gate, hidden_parts[1][0])
+    total_up = place_windows(hidden_parts[1], count)
     gain_rows = total_down_both.shape[0] - D // count
     gain_totals = total_down_both[-gain_rows:].reshape(-1).astype(f32)
     total_down_both = total_down_both[:-gain_rows].astype(f32)
     total_query, total_latent = total_query.astype(f32), total_latent.astype(f32)
-    total_gate, total_up = place_windows(hidden_parts, count)
     first, second, third = D, D + QRANK, D + QRANK + KVRANK
     gain_totals = (gain_totals[:first], gain_totals[first:second], gain_totals[second:third], gain_totals[third:third + D])
     return (

time: 1310 us -> 1210 us (0.924)
  waiting for transfers between devices: 106 us -> 46.8 us
  Pallas kernels: 861 us -> 818 us
    ppermute x6 -> x7, waiting for transfers between devices: 85.8 us -> 1.03 us  [swap(): lax.ppermute(value, 'shard', [(source, source ^ step) for source in range...]
    pallas_call x11, Pallas kernels: 466 us -> 422 us  [comm_call(): pl.pallas_call(kernel, in_specs=vmem(len(inputs) - len(aliased)) + any_sp...]
    psum x1, waiting for transfers between devices: 0.01 us -> 35.4 us  [body(): total_down_both, total_latent, total_query = lax.psum(tuple(shares), 'rep')]
    psum x1, waiting for transfers between devices: 18.2 us -> 2.13 us  [body(): total_output = lax.psum(part_output, 'rep')]
  transfers between devices with their start and end apart: 14 -> 16, of which waited for: 4 -> 5; matrix products, arithmetic and copies ran while one was open for 12% -> 19% of each run, Pallas kernels for 33% -> 42%
where the time goes in v4:
time: 1210 us; the launch traced here: 1200 us
  Pallas kernels  818 us (68%)
  matrix products  187 us (15%)
  local copies, waits for them, and re-layouts  65.4 us (5%)
  other arithmetic  51.5 us (4%)
  waiting for transfers between devices  46.8 us (4%)
  starting transfers between devices  16.3 us (1%)
  between operations  15.8 us (1%)
    pallas_call x11, Pallas kernels, comm_call(): pl.pallas_call(kernel, in_specs=vmem(len(inputs) - len(aliased)) + any_sp...  422 us
    pallas_call x1, Pallas kernels, move(): pl.pallas_call(functools.partial(move_kernel, len(wholes), [f for _, _, f...  154 us
    pallas_call x1, Pallas kernels, recompute(): pl.pallas_call(recompute_kernel, grid_spec=pltpu.PrefetchScalarGridSpec(n...  93.2 us
    dot_general x12, matrix products, project(): return jnp.dot(left, weight, preferred_element_type=f32)  65.3 us
    dot_general x8, matrix products, contract_rows(): lax.dot_general(left, right, (((0,), (0,)), ((), ())), preferred_element_...  65.1 us
    dot_general x8, matrix products, contract_cols(): lax.dot_general(left, right, (((1,), (1,)), ((), ())), preferred_element_...  57 us
    pallas_call x1, Pallas kernels, chip_gradients(): pl.pallas_call(chip_gradients_kernel, grid_spec=pltpu.PrefetchScalarGridS...  43.7 us
    pallas_call x1, Pallas kernels, down_gradient(): pl.pallas_call(down_gradient_kernel, grid=(D // piece,), in_specs=[pl.Blo...  36.7 us
  transfers between devices with their start and end apart: 16, of which 5 were waited for; matrix products, arithmetic and copies ran while one was open for 19% of the time, Pallas kernels for 42%

profile of v4, /device:TPU:1, one launch (start us, length us, event | category | flops | bytes accessed | tf_op | source)
XLA Modules:
  0.0 1201.7 jit_solution(14771766174883882817)
XLA Ops:
  14.3 153.6 %first_move.1 = (bf16[4,640,768]{2,1,0:T(8,128)(2,1)}, bf16[4,640,288]{2,1,0:T(8,128)(2,1)}, s32[4,2,96]{2,1,0:T(2,128)}, bf16[4,192,1024]{2,1,0:T(8,128)(2,1)},...) custom-call(bf16[640,768]{1,0:T(8,128)(2,1)} %bitcast.157, ...), custom_call_target="tpu_custom_call" | custom-call | bytes 79465472 | tf_op jit(solution)/shard_map/first_move/pallas_call | solution.py:812
  175.5 16.2 %gather_rows.3 = bf16[768,1152]{1,0:T(8,128)(2,1)} custom-call(bf16[192,1152]{1,0:T(8,128)(2,1)} %fusion.54.own_ref), custom_call_target="tpu_custom_call" | custom-call | tf_op jit(solution)/shard_map/gather_rows/pallas_call | solution.py:397
  225.1 57.7 %output_norm.2 = (f32[192,2560]{1,0:T(8,128)}, bf16[768,2560]{1,0:T(8,128)(2,1)}, bf16[4,640,1664]{2,1,0:T(8,128)(2,1)}) custom-call(bf16[768,640]{1,0:T(8,128)(2,1)} %get-tuple-element.105.att_ref, bf16[640,2560]{1,0:T(8,128)(2,1)} %bitcast.132, f32[192,2560]{1,0:T(8,128)} %convert_element_type.173.hidden_ref, ...), custom_call_target="tpu_custom_call", output_to_operand_aliasing={{2}: (4, {})} | custom-call | tf_op jit(solution)/shard_map/output_norm/pallas_call | solution.py:397
  303.1 45.8 %down_project.2 = (f32[192,2560]{1,0:T(8,128)}, bf16[192,2560]{1,0:T(8,128)(2,1)}, bf16[192,2560]{1,0:T(8,128)(2,1)}, bf16[1664,2560]{1,0:T(8,128)(2,1)}) custom-call(bf16[768,1664]{1,0:T(8,128)(2,1)} %fusion.19.act_ref, bf16[1600,2560]{1,0:T(8,128)(2,1)} %bitcast.140, f32[192,2560]{1,0:T(8,128)} %get-tuple-element.114.mixed_ref), custom_call_target="tpu_custom_call" | custom-call | tf_op jit(solution)/shard_map/down_project/pallas_call | solution.py:397
  358.4 15.8 %gather_rows.4 = bf16[768,1152]{1,0:T(8,128)(2,1)} custom-call(bf16[192,1152]{1,0:T(8,128)(2,1)} %fusion.55.own_ref), custom_call_target="tpu_custom_call" | custom-call | tf_op jit(solution)/shard_map/gather_rows/pallas_call | solution.py:397
  395.7 56.1 %output_norm.3 = (f32[192,2560]{1,0:T(8,128)}, bf16[768,2560]{1,0:T(8,128)(2,1)}) custom-call(bf16[768,640]{1,0:T(8,128)(2,1)} %get-tuple-element.118.att_ref, bf16[640,2560]{1,0:T(8,128)(2,1)} %bitcast.133, f32[192,2560]{1,0:T(8,128)} %copy-done.1, f32[1,2560]{1,0:T(1,128)} %gain_ref.7), custom_call_target="tpu_custom_call" | custom-call | tf_op jit(solution)/shard_map/output_norm/pallas_call | solution.py:397
  460.5 13.9 %convolution_convert_fusion.1 = bf16[768,1664]{1,0:T(8,128)(2,1)} fusion(bf16[768,2560]{1,0:T(8,128)(2,1)} %get-tuple-element.119, bf16[2560,1664]{1,0:T(8,128)(2,1)} %bitcast.116), kind=kOutput, calls=%fused_computation.43 | convolution fusion | flops 6544392192 | bytes 15007744 | tf_op jit(solution)/shard_map/dot_general | solution.py:82
  483.0 16.1 %fusion.16 = (bf16[768,1664]{1,0:T(8,128)(2,1)}, bf16[768,1664]{1,0:T(8,128)(2,1)}, bf16[768,1664]{1,0:T(8,128)(2,1)}) fusion(bf16[768,1664]{1,0:T(8,128)(2,1)} %convolution_convert_fusion.1, bf16[768,1664]{1,0:T(8,128)(2,1)} %convolution_convert_fusion.2, bf16[768,2560]{1,0:T(8,128)(2,1)} %all-gather.5.cloned.1.call-done, ...), kind=kOutput, calls=%fused_computation.26 | convolution fusion | flops 6566117376 | bytes 25231360 | tf_op jit(solution)/shard_map/dot_general | solution.py:78
  499.1 63.6 %mlp_back.2 = (f32[192,2560]{1,0:T(8,128)}, f32[1,2560]{1,0:T(1,128)}, bf16[768,2560]{1,0:T(8,128)(2,1)}) custom-call(bf16[768,1664]{1,0:T(8,128)(2,1)} %get-tuple-element.296.gate_ref, bf16[768,1664]{1,0:T(8,128)(2,1)} %get-tuple-element.295.up_ref, bf16[2560,1664]{1,0:T(8,128)(2,1)} %bitcast.117, bf16[2560,1664]{1,0:T(8,128)(2,1)} %bitcast.108, ...), custom_call_target="tpu_custom_call" | custom-call | tf_op jit(solution)/shard_map/mlp_back/pallas_call | solution.py:397
  581.6 19.2 %latent_back.2 = f32[192,1280]{1,0:T(8,128)} custom-call(bf16[768,1280]{1,0:T(8,128)(2,1)} %get-tuple-element.126.gq_ref, bf16[768,1280]{1,0:T(8,128)(2,1)} %get-tuple-element.127.gkv_ref, f32[768,128]{1,0:T(8,128)} %get-tuple-element.128.gsh_ref, bf16[768,1280]{1,0:T(8,128)(2,1)} %copy.116.qup_ref, bf16[256,1280]{1,0:T(8,128)(2,1)} %bitcast.134), custom_call_target="tpu_custom_call" | custom-call | tf_op jit(solution)/shard_map/latent_back/pallas_call | solution.py:397
  612.0 35.9 %down_project.3 = (f32[192,2560]{1,0:T(8,128)}, bf16[192,2560]{1,0:T(8,128)(2,1)}) custom-call(bf16[768,1664]{1,0:T(8,128)(2,1)} %get-tuple-element.131.act_ref.act_own, bf16[1664,2560]{1,0:T(8,128)(2,1)} %get-tuple-element.115.given_ref.rows_ref, f32[192,2560]{1,0:T(8,128)} %get-tuple-element.120.mixed_ref), custom_call_target="tpu_custom_call" | custom-call | tf_op jit(solution)/shard_map/down_project/pallas_call | solution.py:397
  652.1 28.4 %gather_rows.5 = bf16[768,2560]{1,0:T(8,128)(2,1)} custom-call(bf16[192,2560]{1,0:T(8,128)(2,1)} %multiply_convert_fusion.own_ref), custom_call_target="tpu_custom_call" | custom-call | tf_op jit(solution)/shard_map/gather_rows/pallas_call | solution.py:397
  683.7 15.4 %fusion.18 = (bf16[768,1664]{1,0:T(8,128)(2,1)}, bf16[768,1664]{1,0:T(8,128)(2,1)}) fusion(bf16[768,1664]{1,0:T(8,128)(2,1)} %convolution_convert_fusion.1, bf16[768,1664]{1,0:T(8,128)(2,1)} %convolution_convert_fusion.2, bf16[768,2560]{1,0:T(8,128)(2,1)} %gather_rows.5, bf16[1664,2560]{1,0:T(8,128)(2,1)} %get-tuple-element.115.given_ref.rows_ref), kind=kOutput, calls=%fused_computation.28 | convolution fusion | flops 6562283520 | bytes 22675456 | tf_op jit(solution)/shard_map/dot_general | solution.py:78
  699.0 63.6 %mlp_back.3 = (f32[192,2560]{1,0:T(8,128)}, f32[1,2560]{1,0:T(1,128)}, bf16[768,2560]{1,0:T(8,128)(2,1)}) custom-call(bf16[768,1664]{1,0:T(8,128)(2,1)} %get-tuple-element.152.gate_ref.gate_own, bf16[768,1664]{1,0:T(8,128)(2,1)} %get-tuple-element.153.up_ref.up_own, bf16[2560,1664]{1,0:T(8,128)(2,1)} %bitcast.118, bf16[2560,1664]{1,0:T(8,128)(2,1)} %bitcast.109, ...), custom_call_target="tpu_custom_call" | custom-call | tf_op jit(solution)/shard_map/mlp_back/pallas_call | solution.py:397
  790.1 19.4 %latent_back.3 = f32[192,1280]{1,0:T(8,128)} custom-call(bf16[768,1280]{1,0:T(8,128)(2,1)} %get-tuple-element.140.gq_ref, bf16[768,1280]{1,0:T(8,128)(2,1)} %get-tuple-element.141.gkv_ref, f32[768,128]{1,0:T(8,128)} %get-tuple-element.142.gsh_ref, bf16[768,1280]{1,0:T(8,128)(2,1)} %copy.116.qup_ref, bf16[256,1280]{1,0:T(8,128)(2,1)} %bitcast.135), custom_call_target="tpu_custom_call" | custom-call | tf_op jit(solution)/shard_map/latent_back/pallas_call | solution.py:397
  857.2 93.2 %recompute.1 = (bf16[3072,1664]{1,0:T(8,128)(2,1)}, bf16[3072,1664]{1,0:T(8,128)(2,1)}, bf16[3072,1664]{1,0:T(8,128)(2,1)}) custom-call(s32[8]{0:T(128)} %and_select_fusion.3.from_ref, s32[8]{0:T(128)} %get-tuple-element.336.own_ref, s32[8]{0:T(128)} %get-tuple-element.335.here_ref, bf16[3072,2560]{1,0:T(8,128)(2,1)} %all-gather.9.cloned.1.call-done.two_ref, ...), custom_call_target="tpu_custom_call" | custom-call | tf_op jit(solution)/shard_map/recompute/pallas_call | solution.py:1172
  952.5 14.1 %fusion.32 = bf16[640,1664]{1,0:T(8,128)(2,1)} fusion(bf16[3072,1664]{1,0:T(8,128)(2,1)} %get-tuple-element.157.gate_ref, bf16[3072,2560]{1,0:T(8,128)(2,1)} %all-gather.9.cloned.1.call-done.two_ref, s32[]{:T(128)S(6)} %select_n.72), kind=kOutput, calls=%fused_computation.50 | convolution fusion | flops 6544179200 | bytes 16285700 | tf_op jit(solution)/shard_map/dot_general | solution.py:74
  1001.0 12.4 %fusion.35 = bf16[640,1664]{1,0:T(8,128)(2,1)} fusion(bf16[3072,1664]{1,0:T(8,128)(2,1)} %get-tuple-element.169.up_ref, bf16[3072,2560]{1,0:T(8,128)(2,1)} %all-gather.9.cloned.1.call-done.two_ref, s32[]{:T(128)S(6)} %select_n.69), kind=kOutput, calls=%fused_computation.51 | convolution fusion | flops 6544179200 | bytes 16285700 | tf_op jit(solution)/shard_map/dot_general | solution.py:74
  1014.6 12.2 %fusion.38 = bf16[640,1664]{1,0:T(8,128)(2,1)} fusion(bf16[3072,1664]{1,0:T(8,128)(2,1)} %get-tuple-element.169.up_ref, bf16[3072,2560]{1,0:T(8,128)(2,1)} %all-gather.9.cloned.1.call-done.two_ref, s32[]{:T(128)S(6)} %select_n.72), kind=kOutput, calls=%fused_computation.52 | convolution fusion | flops 6544179200 | bytes 16285700 | tf_op jit(solution)/shard_map/dot_general | solution.py:74
  1027.2 43.7 %chip_gradients.1 = (bf16[2,640,1664]{2,1,0:T(8,128)(2,1)}, bf16[2,640,1664]{2,1,0:T(8,128)(2,1)}) custom-call(s32[2]{0:T(128)} %pad_add_fusion.order_ref, bf16[3072,2560]{1,0:T(8,128)(2,1)} %all-gather.9.cloned.1.call-done.two_ref, bf16[3072,1664]{1,0:T(8,128)(2,1)} %get-tuple-element.157.gate_ref, bf16[3072,1664]{1,0:T(8,128)(2,1)} %get-tuple-element.169.up_ref), custom_call_target="tpu_custom_call" | custom-call | tf_op jit(solution)/shard_map/chip_gradients/pallas_call | solution.py:1105
  1083.2 36.7 %down_gradient.1 = f32[1600,2560]{1,0:T(8,128)} custom-call(bf16[3072,1664]{1,0:T(8,128)(2,1)} %get-tuple-element.172.act_ref, bf16[1536,2560]{1,0:T(8,128)(2,1)} %all-gather.11.cloned.1.call-done.near_ref, bf16[1536,2560]{1,0:T(8,128)(2,1)} %collective-permute-done.1.beside_ref), custom_call_target="tpu_custom_call" | custom-call | tf_op jit(solution)/shard_map/down_gradient/pallas_call | solution.py:1216
  1119.9 35.4 %all-reduce.14.cloned.1.call-done = (bf16[646,1056]{1,0:T(8,128)(2,1)}, bf16[1,192,3840]{2,1,0:T(8,128)(2,1)}, bf16[1,64,5120]{2,1,0:T(8,128)(2,1)}) async-done(((bf16[646,1056]{1,0:T(8,128)(2,1)}, bf16[1,192,3840]{2,1,0:T(8,128)(2,1)}, bf16[1,64,5120]{2,1,0:T(8,128)(2,1)}), (bf16[646,1056]{1,0:T(8,128)(2,1)}, bf16[1,192,3840]{2,1,0:T(8,128)(2,1)}, ...) | async-done | bytes 3494288 | tf_op jit(solution)/shard_map/psum | solution.py:1367
  1168.9 12.2 %place_windows.2 = f32[640,6400]{1,0:T(8,128)} custom-call(bf16[640,1664]{1,0:T(8,128)(2,1)} %get-tuple-element.176.refs_0_, bf16[640,1664]{1,0:T(8,128)(2,1)} %collective-permute-done.4.refs_1_, bf16[640,1664]{1,0:T(8,128)(2,1)} %collective-permute-done.2.refs_2_, bf16[640,1664]{1,0:T(8,128)(2,1)} %collective-permute-done.3.refs_3_), custom_call_target="tpu_custom_call" | custom-call | bytes 32768000 | tf_op jit(solution)/shard_map/place_windows/pallas_call | solution.py:1254
  1181.2 12.3 %place_windows.3 = f32[640,6400]{1,0:T(8,128)} custom-call(bf16[640,1664]{1,0:T(8,128)(2,1)} %get-tuple-element.182.refs_0_, bf16[640,1664]{1,0:T(8,128)(2,1)} %collective-permute-done.5.refs_1_, bf16[640,1664]{1,0:T(8,128)(2,1)} %collective-permute-done.6.refs_2_, bf16[640,1664]{1,0:T(8,128)(2,1)} %collective-permute-done.7.refs_3_), custom_call_target="tpu_custom_call" | custom-call | bytes 32768000 | tf_op jit(solution)/shard_map/place_windows/pallas_call | solution.py:1254
  (327 shorter events, 293.0 us)
Async XLA Ops:
  7.2 275.6 %all-gather.5.cloned.1.call-start = ((), (), s32[]{:S(2)}) async-start(), calls=%async_computation.2 | async-start | bytes 4915200 | tf_op jit(solution)/shard_map/all_gather | solution.py:440
  7.2 163.2 %copy-start.50 = (f32[16]{0:T(128)}, f32[16]{0:T(128)S(1)}, u32[]{:S(2)}) copy-start(f32[16]{0:T(128)S(1)} %multiply_exponential_fusion) | copy-start | bytes 196
  8.3 162.1 %copy-start.40 = (f32[192]{0:T(256)}, f32[192]{0:T(256)S(1)}, u32[]{:S(2)}) copy-start(f32[192]{0:T(256)S(1)} %convert_element_type.177) | copy-start | bytes 2308
  10.5 592.8 %copy-start.32 = (f32[768]{0:T(1024)}, f32[768]{0:T(1024)S(1)}, u32[]{:S(2)}) copy-start(f32[768]{0:T(1024)S(1)} %reduce.2) | copy-start | bytes 9220
  11.3 596.0 %copy-start.30 = (f32[2560]{0:T(1024)}, f32[2560]{0:T(1024)S(1)}, u32[]{:S(2)}) copy-start(f32[2560]{0:T(1024)S(1)} %reduce.1) | copy-start | bytes 30724
  14.3 153.7 %copy-start.12 = (bf16[192,2560]{1,0:T(8,128)(2,1)S(1)}, bf16[192,2560]{1,0:T(8,128)(2,1)}, u32[]{:S(2)}) copy-start(bf16[192,2560]{1,0:T(8,128)(2,1)} %param.15) | copy-start | bytes 2949124
  191.7 409.2 %all-gather.7.cloned.1.call-start = ((), (), s32[]{:S(2)}) async-start(), calls=%async_computation.3 | async-start | bytes 9830400 | tf_op jit(solution)/shard_map/all_gather | solution.py:1234
  357.4 24.0 %copy-start.44 = (f32[192]{0:T(256)}, f32[192]{0:T(256)S(1)}, u32[]{:S(2)}) copy-start(f32[192]{0:T(256)S(1)} %get-tuple-element.326) | copy-start | bytes 2308
  454.8 225.9 %all-gather.9.cloned.1.call-start = ((), (), s32[]{:S(2)}) async-start(), calls=%async_computation.4 | async-start | bytes 23592960 | tf_op jit(solution)/shard_map/all_gather | solution.py:1240
  601.0 225.9 %all-gather.11.cloned.1.call-start = ((), (), s32[]{:S(2)}) async-start(), calls=%async_computation.5 | async-start | bytes 9830400 | tf_op jit(solution)/shard_map/all_gather | solution.py:1234
  610.8 37.2 %collective-permute-start = (bf16[192,2560]{1,0:T(8,128)(2,1)}, bf16[192,2560]{1,0:T(8,128)(2,1)}, u32[]{:S(2)}, u32[]{:S(2)}) collective-permute-start(bf16[192,2560]{1,0:T(8,128)(2,1)} %add_convert_fusion), channel_id=1, source_target_pairs={{16,0},{17,1},{18,2},{19,3},{20,4},{21,5},{22,6},{23,7},{24,8},{25... | collective-permute-start | bytes 2949128 | tf_op jit(solution)/shard_map/ppermute | solution.py:1312
  683.6 268.9 %all-reduce.12.cloned.1.call-start = ((), (), s32[]{:S(2)}) async-start(), calls=%async_computation.6 | async-start | bytes 6553600 | tf_op jit(solution)/shard_map/psum | solution.py:1338
  790.0 21.2 %copy-start.39 = (f32[1,256]{1,0:T(1,128)S(1)}, f32[1,256]{1,0:T(1,128)}, u32[]{:S(2)}) copy-start(f32[1,256]{1,0:T(1,128)} %param.19) | copy-start | bytes 3076
  790.1 22.3 %copy-start.33 = (f32[768]{0:T(1024)S(1)}, f32[768]{0:T(1024)}, u32[]{:S(2)}) copy-start(f32[768]{0:T(1024)} %copy-done.32) | copy-start | bytes 9220
  826.9 30.3 %collective-permute-start.1 = (bf16[1536,2560]{1,0:T(8,128)(2,1)}, bf16[1536,2560]{1,0:T(8,128)(2,1)}, u32[]{:S(2)}, u32[]{:S(2)}) collective-permute-start(bf16[1536,2560]{1,0:T(8,128)(2,1)} %all-gather.11.cloned.1.call-done.near_ref), channel_id=1, source_target_pairs={{0,1},{1,0},{2,3},{3,2},{4,5},{5,4},{6,7},{7,6},{8,9},{9,8},{10,11... | collective-permute-start | bytes 23592968 | tf_op jit(solution)/shard_map/ppermute | solution.py:1039
  830.1 17.2 %all-to-all-start = ((bf16[4,192,640]{2,1,0:T(8,128)(2,1)}), bf16[4,192,640]{2,1,0:T(8,128)(2,1)}, u32[]{:S(2)}, u32[]{:S(2)}) async-start(bf16[4,192,640]{2,1,0:T(8,128)(2,1)} %bitcast.149), calls=%async_computation | async-start | bytes 1966080 | tf_op jit(solution)/shard_map/all_to_all | solution.py:1329
  847.4 130.3 %all-to-all-start.1 = ((bf16[4,464,1280]{2,1,0:T(8,128)(2,1)}), bf16[4,464,1280]{2,1,0:T(8,128)(2,1)}, u32[]{:S(2)}, u32[]{:S(2)}) async-start(bf16[4,464,1280]{2,1,0:T(8,128)(2,1)} %pad_maximum_fusion), calls=%async_computation.1 | async-start | bytes 9502720 | tf_op jit(solution)/shard_map/all_to_all | solution.py:888
  853.2 302.1 %all-reduce.14.cloned.1.call-start = ((), (), s32[]{:S(2)}) async-start(), calls=%async_computation.7 | async-start | bytes 7245824 | tf_op jit(solution)/shard_map/psum | solution.py:1367
  984.0 94.5 %collective-permute-start.2 = (bf16[640,1664]{1,0:T(8,128)(2,1)}, bf16[640,1664]{1,0:T(8,128)(2,1)}, u32[]{:S(2)}, u32[]{:S(2)}) collective-permute-start(bf16[640,1664]{1,0:T(8,128)(2,1)} %fusion.29), channel_id=1, source_target_pairs={{0,2},{1,3},{2,0},{3,1},{4,6},{5,7},{6,4},{7,5},{8,10},{9,11},{10,... | collective-permute-start | bytes 6389768 | tf_op jit(solution)/shard_map/ppermute | solution.py:1039
  985.3 94.2 %collective-permute-start.3 = (bf16[640,1664]{1,0:T(8,128)(2,1)}, bf16[640,1664]{1,0:T(8,128)(2,1)}, u32[]{:S(2)}, u32[]{:S(2)}) collective-permute-start(bf16[640,1664]{1,0:T(8,128)(2,1)} %fusion.32), channel_id=1, source_target_pairs={{0,3},{1,2},{2,1},{3,0},{4,7},{5,6},{6,5},{7,4},{8,11},{9,10},{10,... | collective-permute-start | bytes 6389768 | tf_op jit(solution)/shard_map/ppermute | solution.py:1039
  1013.4 167.7 %collective-permute-start.6 = (bf16[640,1664]{1,0:T(8,128)(2,1)}, bf16[640,1664]{1,0:T(8,128)(2,1)}, u32[]{:S(2)}, u32[]{:S(2)}) collective-permute-start(bf16[640,1664]{1,0:T(8,128)(2,1)} %fusion.35), channel_id=1, source_target_pairs={{0,2},{1,3},{2,0},{3,1},{4,6},{5,7},{6,4},{7,5},{8,10},{9,11},{10,... | collective-permute-start | bytes 6389768 | tf_op jit(solution)/shard_map/ppermute | solution.py:1039
  1026.8 154.3 %collective-permute-start.7 = (bf16[640,1664]{1,0:T(8,128)(2,1)}, bf16[640,1664]{1,0:T(8,128)(2,1)}, u32[]{:S(2)}, u32[]{:S(2)}) collective-permute-start(bf16[640,1664]{1,0:T(8,128)(2,1)} %fusion.38), channel_id=1, source_target_pairs={{0,3},{1,2},{2,1},{3,0},{4,7},{5,6},{6,5},{7,4},{8,11},{9,10},{10,... | collective-permute-start | bytes 6389768 | tf_op jit(solution)/shard_map/ppermute | solution.py:1039
  1075.6 105.5 %collective-permute-start.5 = (bf16[640,1664]{1,0:T(8,128)(2,1)}, bf16[640,1664]{1,0:T(8,128)(2,1)}, u32[]{:S(2)}, u32[]{:S(2)}) collective-permute-start(bf16[640,1664]{1,0:T(8,128)(2,1)} %get-tuple-element.300), channel_id=1, source_target_pairs={{0,1},{1,0},{2,3},{3,2},{4,5},{5,4},{6,7},{7,6},{8,9},{9,8},{10,11... | collective-permute-start | bytes 6389768 | tf_op jit(solution)/shard_map/ppermute | solution.py:1039
  1079.5 89.4 %collective-permute-start.4 = (bf16[640,1664]{1,0:T(8,128)(2,1)}, bf16[640,1664]{1,0:T(8,128)(2,1)}, u32[]{:S(2)}, u32[]{:S(2)}) collective-permute-start(bf16[640,1664]{1,0:T(8,128)(2,1)} %get-tuple-element.173), channel_id=1, source_target_pairs={{0,1},{1,0},{2,3},{3,2},{4,5},{5,4},{6,7},{7,6},{8,9},{9,8},{10,11... | collective-permute-start | bytes 6389768 | tf_op jit(solution)/shard_map/ppermute | solution.py:1039
  (58 other events, 300.9 us)
Sparse Core Ops, SparseCore 0:
  191.8 35.1 all-gather.4
  454.9 140.6 all-gather.6
  601.1 30.6 all-gather.8
  683.7 143.1 all-gather.10
  829.2 123.2 all-reduce.11
  1014.8 140.4 all-reduce.13

commit v5 on v4

--- a/solution.py
+++ b/solution.py
@@ -706,7 +706,7 @@
     )
 
 
-def move_kernel(whole, split, relayed, *refs):
+def move_kernel(whole, alike, split, relayed, *refs):
     amount = whole + len(split) + len(relayed)
     inputs, outputs, held = refs[:amount], refs[amount:2 * amount], refs[2 * amount:3 * amount]
     sems, local, *relays = refs[3 * amount:]
@@ -724,9 +724,14 @@
             to_far = send_to(source, target.at[me], sems, number, far)
             to_sib = send_to(source, target.at[me], sems, number + 1, sib)
             onward = send_to(target.at[far], target.at[far], sems, number + 2, sib)
-            to_far.start()
+            if i < alike:
+                @pl.when(away == 0)
+                def _():
+                    to_far.start()
+            else:
+                to_far.start()
             to_sib.start()
-            forwards.append((to_far, onward))
+            forwards.append((target, to_far, onward))
             waits.append(to_sib)
             kept = source
         elif i < whole + len(split):
@@ -739,20 +744,21 @@
         else:
             begin, arrive, passed = relays
             place = i - whole - len(split)
+            part = relayed[place][0]
             taker = far // 2 * 2 + lax.axis_index("rep") % 2
 
-            def across(owner, slot):
+            def across(owner, slot, source=source, target=target, part=part, place=place):
                 return pltpu.make_async_remote_copy(
-                    src_ref=hidden_columns(source, taker), dst_ref=target.at[owner], send_sem=begin.at[place],
+                    src_ref=part(source, taker), dst_ref=target.at[owner], send_sem=begin.at[place],
                     recv_sem=arrive.at[place, slot], device_id={"shard": taker}, device_id_type=MESH,
                 )
 
             across(me, away).start()
-            beside = send_to(hidden_columns(source, sib), target.at[me], sems, number, sib)
+            beside = send_to(part(source, sib), target.at[me], sems, number, sib)
             beside.start()
             waits.append(beside)
             bulk.append((place, target, across))
-            kept = hidden_columns(source, me)
+            kept = part(source, me)
         number += 3
         keep = pltpu.make_async_copy(kept, held[i], local.at[0, i])
         keep.start()
@@ -760,18 +766,38 @@
     for keep, store in keeps:
         keep.wait()
         store.start()
-    for to_far, onward in forwards:
-        to_far.wait_recv()
+    for step, (target, to_far, onward) in enumerate(forwards):
+        if step < alike:
+            hop = pass_on(target, relays[2], 2 * len(relayed) + step, far)
+
+            @pl.when(away == 0)
+            def _():
+                to_far.wait_recv()
+                hop.start()
+
+            @pl.when(away == 1)
+            def _():
+                hop.wait_recv()
+        else:
+            to_far.wait_recv()
         onward.start()
-    for to_far, onward in forwards:
-        to_far.wait_send()
+    for step, (target, to_far, onward) in enumerate(forwards):
+        if step < alike:
+            hop = pass_on(target, relays[2], 2 * len(relayed) + step, far)
+
+            @pl.when(away == 0)
+            def _():
+                to_far.wait_send()
+                hop.wait_send()
+        else:
+            to_far.wait_send()
         onward.wait()
     for copy in waits:
         copy.wait()
     for keep, store in keeps:
         store.wait()
     for place, target, across in bulk:
-        passing = relayed[place]
+        passing = relayed[place][1]
         passed = relays[2]
 
         @pl.when(away == 0)
@@ -782,7 +808,7 @@
                     pass_on(target, passed, 2 * place + slot, owner).start()
 
     for place, target, across in bulk:
-        passing = relayed[place]
+        passing = relayed[place][1]
         passed = relays[2]
         across(me, away).wait_send()
         if passing:
@@ -797,9 +823,9 @@
                     pass_on(target, passed, 2 * place + slot, owner).wait_recv()
 
 
-def move(name, number, wholes, splits, relayed=()):
-    inputs = list(wholes) + [array for array, _, _ in (*splits, *relayed)]
-    shapes = [w.shape for w in wholes] + [part for _, part, _ in (*splits, *relayed)]
+def move(name, number, wholes, splits, relayed=(), alike=0):
+    inputs = list(wholes) + [entry[0] for entry in (*splits, *relayed)]
+    shapes = [w.shape for w in wholes] + [entry[1] for entry in (*splits, *relayed)]
     out_shape = [jax.ShapeDtypeStruct((4,) + tuple(sh), v.dtype) for sh, v in zip(shapes, inputs)]
     scratch = [pltpu.VMEM(sh, v.dtype) for sh, v in zip(shapes, inputs)]
     scratch += [pltpu.SemaphoreType.DMA((2, 3 * len(inputs))), pltpu.SemaphoreType.DMA((2, len(inputs)))]
@@ -807,10 +833,10 @@
         amount = len(relayed)
         scratch += [
             pltpu.SemaphoreType.DMA((amount,)), pltpu.SemaphoreType.DMA((amount, 2)),
-            pltpu.SemaphoreType.DMA((2, 2 * amount)),
+            pltpu.SemaphoreType.DMA((2, 2 * amount + len(wholes))),
         ]
     return pl.pallas_call(
-        functools.partial(move_kernel, len(wholes), [f for _, _, f in splits], [p for _, _, p in relayed]),
+        functools.partial(move_kernel, len(wholes), alike, [f for _, _, f in splits], [entry[2:] for entry in relayed]),
         in_specs=any_space(len(inputs)),
         out_specs=any_space(len(inputs)),
         out_shape=out_shape,
@@ -851,12 +877,15 @@
             spread(latent_up, count), plain_gather(segments), gate, up,
         )
     part = (gate.shape[0], HIDDEN_WINDOW)
-    relayed = [(gate, part, True), (up, part, False)] if shared_links(count) else []
+    heads = [(query_up, (query_up.shape[0], QUERY_WINDOW), query_window),
+             (latent_up, (latent_up.shape[0], 1280), latent_window)]
+    relayed = []
+    if shared_links(count):
+        relayed = [entry + (True,) for entry in heads]
+        relayed += [(gate, part, hidden_columns, True), (up, part, hidden_columns, False)]
+        heads = []
     down_q, down_kv, groups, up_q, up_kv, *hidden = move(
-        "first_move", 7, [query_down, latent_down, segments],
-        [(query_up, (query_up.shape[0], QUERY_WINDOW), query_window),
-         (latent_up, (latent_up.shape[0], 1280), latent_window)],
-        relayed,
+        "first_move", 7, [query_down, latent_down, segments], heads, relayed, 2 if relayed else 0
     )
     merge = lambda value: value.reshape((-1,) + value.shape[2:])
     up_q = lax.dynamic_slice_in_dim(merge(up_q), lax.axis_index("shard") % 2 * 64, 960, 1)
@@ -1386,6 +1415,9 @@
     total_gate = place_windows(hidden_parts[0], count)
     total_gate, hidden_parts[1][0] = together(total_gate, hidden_parts[1][0])
     total_up = place_windows(hidden_parts[1], count)
+    total_up, total_down_both, total_latent, total_query = together(
+        total_up, total_down_both, total_latent, total_query
+    )
     gain_rows = total_down_both.shape[0] - D // count
     gain_totals = total_down_both[-gain_rows:].reshape(-1).astype(f32)
     total_down_both = total_down_both[:-gain_rows].astype(f32)

time: 1210 us -> 1200 us (level)
    psum x1, waiting for transfers between devices: 35.4 us -> 0.01 us  [body(): total_down_both, total_latent, total_query = lax.psum(tuple(shares), 'rep')]
    ppermute x7, waiting for transfers between devices: 1.03 us -> 29.8 us  [swap(): lax.ppermute(value, 'shard', [(source, source ^ step) for source in range...]
  transfers between devices with their start and end apart: 16 -> 16, of which waited for: 5 -> 4; matrix products, arithmetic and copies ran while one was open for 19% -> 19% of each run, Pallas kernels for 42% -> 44%
where the time goes in v5:
time: 1200 us; the launch traced here: 1190 us
  Pallas kernels  808 us (67%)
  matrix products  188 us (16%)
  local copies, waits for them, and re-layouts  68.5 us (6%)
  other arithmetic  48.4 us (4%)
  waiting for transfers between devices  44 us (4%)
  starting transfers between devices  16.4 us (1%)
  between operations  15.8 us (1%)
    pallas_call x11, Pallas kernels, comm_call(): pl.pallas_call(kernel, in_specs=vmem(len(inputs) - len(aliased)) + any_sp...  422 us
    pallas_call x1, Pallas kernels, move(): pl.pallas_call(functools.partial(move_kernel, len(wholes), alike, [f for...  142 us
    pallas_call x1, Pallas kernels, recompute(): pl.pallas_call(recompute_kernel, grid_spec=pltpu.PrefetchScalarGridSpec(n...  93.2 us
    dot_general x8, matrix products, contract_rows(): lax.dot_general(left, right, (((0,), (0,)), ((), ())), preferred_element_...  65.9 us
    dot_general x12, matrix products, project(): return jnp.dot(left, weight, preferred_element_type=f32)  65.3 us
    dot_general x8, matrix products, contract_cols(): lax.dot_general(left, right, (((1,), (1,)), ((), ())), preferred_element_...  57 us
    pallas_call x1, Pallas kernels, chip_gradients(): pl.pallas_call(chip_gradients_kernel, grid_spec=pltpu.PrefetchScalarGridS...  43.7 us
    pallas_call x1, Pallas kernels, down_gradient(): pl.pallas_call(down_gradient_kernel, grid=(D // piece,), in_specs=[pl.Blo...  37.5 us
  transfers between devices with their start and end apart: 16, of which 4 were waited for; matrix products, arithmetic and copies ran while one was open for 19% of the time, Pallas kernels for 44%

profile of v5, /device:TPU:1, one launch (start us, length us, event | category | flops | bytes accessed | tf_op | source)
XLA Modules:
  0.0 1188.7 jit_solution(11296132917087807404)
XLA Ops:
  14.3 141.9 %first_move.1 = (bf16[4,640,768]{2,1,0:T(8,128)(2,1)}, bf16[4,640,288]{2,1,0:T(8,128)(2,1)}, s32[4,2,96]{2,1,0:T(2,128)}, bf16[4,192,1024]{2,1,0:T(8,128)(2,1)},...) custom-call(bf16[640,768]{1,0:T(8,128)(2,1)} %bitcast.160, ...), custom_call_target="tpu_custom_call" | custom-call | bytes 79465472 | tf_op jit(solution)/shard_map/first_move/pallas_call | solution.py:838
  163.7 16.2 %gather_rows.3 = bf16[768,1152]{1,0:T(8,128)(2,1)} custom-call(bf16[192,1152]{1,0:T(8,128)(2,1)} %fusion.54.own_ref), custom_call_target="tpu_custom_call" | custom-call | tf_op jit(solution)/shard_map/gather_rows/pallas_call | solution.py:397
  213.3 57.7 %output_norm.2 = (f32[192,2560]{1,0:T(8,128)}, bf16[768,2560]{1,0:T(8,128)(2,1)}, bf16[4,640,1664]{2,1,0:T(8,128)(2,1)}) custom-call(bf16[768,640]{1,0:T(8,128)(2,1)} %get-tuple-element.109.att_ref, bf16[640,2560]{1,0:T(8,128)(2,1)} %bitcast.136, f32[192,2560]{1,0:T(8,128)} %convert_element_type.173.hidden_ref, ...), custom_call_target="tpu_custom_call", output_to_operand_aliasing={{2}: (4, {})} | custom-call | tf_op jit(solution)/shard_map/output_norm/pallas_call | solution.py:397
  291.4 45.8 %down_project.2 = (f32[192,2560]{1,0:T(8,128)}, bf16[192,2560]{1,0:T(8,128)(2,1)}, bf16[192,2560]{1,0:T(8,128)(2,1)}, bf16[1664,2560]{1,0:T(8,128)(2,1)}) custom-call(bf16[768,1664]{1,0:T(8,128)(2,1)} %fusion.19.act_ref, bf16[1600,2560]{1,0:T(8,128)(2,1)} %bitcast.144, f32[192,2560]{1,0:T(8,128)} %get-tuple-element.118.mixed_ref), custom_call_target="tpu_custom_call" | custom-call | tf_op jit(solution)/shard_map/down_project/pallas_call | solution.py:397
  346.7 15.8 %gather_rows.4 = bf16[768,1152]{1,0:T(8,128)(2,1)} custom-call(bf16[192,1152]{1,0:T(8,128)(2,1)} %fusion.55.own_ref), custom_call_target="tpu_custom_call" | custom-call | tf_op jit(solution)/shard_map/gather_rows/pallas_call | solution.py:397
  384.0 56.1 %output_norm.3 = (f32[192,2560]{1,0:T(8,128)}, bf16[768,2560]{1,0:T(8,128)(2,1)}) custom-call(bf16[768,640]{1,0:T(8,128)(2,1)} %get-tuple-element.122.att_ref, bf16[640,2560]{1,0:T(8,128)(2,1)} %bitcast.137, f32[192,2560]{1,0:T(8,128)} %copy-done.1, f32[1,2560]{1,0:T(1,128)} %gain_ref.7), custom_call_target="tpu_custom_call" | custom-call | tf_op jit(solution)/shard_map/output_norm/pallas_call | solution.py:397
  448.9 13.9 %convolution_convert_fusion.1 = bf16[768,1664]{1,0:T(8,128)(2,1)} fusion(bf16[768,2560]{1,0:T(8,128)(2,1)} %get-tuple-element.123, bf16[2560,1664]{1,0:T(8,128)(2,1)} %bitcast.120), kind=kOutput, calls=%fused_computation.43 | convolution fusion | flops 6544392192 | bytes 15007744 | tf_op jit(solution)/shard_map/dot_general | solution.py:82
  471.4 16.1 %fusion.16 = (bf16[768,1664]{1,0:T(8,128)(2,1)}, bf16[768,1664]{1,0:T(8,128)(2,1)}, bf16[768,1664]{1,0:T(8,128)(2,1)}) fusion(bf16[768,1664]{1,0:T(8,128)(2,1)} %convolution_convert_fusion.1, bf16[768,1664]{1,0:T(8,128)(2,1)} %convolution_convert_fusion.2, bf16[768,2560]{1,0:T(8,128)(2,1)} %all-gather.5.cloned.1.call-done, ...), kind=kOutput, calls=%fused_computation.26 | convolution fusion | flops 6566117376 | bytes 25231360 | tf_op jit(solution)/shard_map/dot_general | solution.py:78
  487.4 63.7 %mlp_back.2 = (f32[192,2560]{1,0:T(8,128)}, f32[1,2560]{1,0:T(1,128)}, bf16[768,2560]{1,0:T(8,128)(2,1)}) custom-call(bf16[768,1664]{1,0:T(8,128)(2,1)} %get-tuple-element.304.gate_ref, bf16[768,1664]{1,0:T(8,128)(2,1)} %get-tuple-element.303.up_ref, bf16[2560,1664]{1,0:T(8,128)(2,1)} %bitcast.121, bf16[2560,1664]{1,0:T(8,128)(2,1)} %bitcast.112, ...), custom_call_target="tpu_custom_call" | custom-call | tf_op jit(solution)/shard_map/mlp_back/pallas_call | solution.py:397
  570.1 19.2 %latent_back.2 = f32[192,1280]{1,0:T(8,128)} custom-call(bf16[768,1280]{1,0:T(8,128)(2,1)} %get-tuple-element.130.gq_ref, bf16[768,1280]{1,0:T(8,128)(2,1)} %get-tuple-element.131.gkv_ref, f32[768,128]{1,0:T(8,128)} %get-tuple-element.132.gsh_ref, bf16[768,1280]{1,0:T(8,128)(2,1)} %copy.116.qup_ref, bf16[256,1280]{1,0:T(8,128)(2,1)} %bitcast.138), custom_call_target="tpu_custom_call" | custom-call | tf_op jit(solution)/shard_map/latent_back/pallas_call | solution.py:397
  600.5 35.9 %down_project.3 = (f32[192,2560]{1,0:T(8,128)}, bf16[192,2560]{1,0:T(8,128)(2,1)}) custom-call(bf16[768,1664]{1,0:T(8,128)(2,1)} %get-tuple-element.135.act_ref.act_own, bf16[1664,2560]{1,0:T(8,128)(2,1)} %get-tuple-element.119.given_ref.rows_ref, f32[192,2560]{1,0:T(8,128)} %get-tuple-element.124.mixed_ref), custom_call_target="tpu_custom_call" | custom-call | tf_op jit(solution)/shard_map/down_project/pallas_call | solution.py:397
  640.6 28.5 %gather_rows.5 = bf16[768,2560]{1,0:T(8,128)(2,1)} custom-call(bf16[192,2560]{1,0:T(8,128)(2,1)} %multiply_convert_fusion.own_ref), custom_call_target="tpu_custom_call" | custom-call | tf_op jit(solution)/shard_map/gather_rows/pallas_call | solution.py:397
  672.1 15.3 %fusion.18 = (bf16[768,1664]{1,0:T(8,128)(2,1)}, bf16[768,1664]{1,0:T(8,128)(2,1)}) fusion(bf16[768,1664]{1,0:T(8,128)(2,1)} %convolution_convert_fusion.1, bf16[768,1664]{1,0:T(8,128)(2,1)} %convolution_convert_fusion.2, bf16[768,2560]{1,0:T(8,128)(2,1)} %gather_rows.5, bf16[1664,2560]{1,0:T(8,128)(2,1)} %get-tuple-element.119.given_ref.rows_ref), kind=kOutput, calls=%fused_computation.28 | convolution fusion | flops 6562283520 | bytes 22675456 | tf_op jit(solution)/shard_map/dot_general | solution.py:78
  687.4 63.5 %mlp_back.3 = (f32[192,2560]{1,0:T(8,128)}, f32[1,2560]{1,0:T(1,128)}, bf16[768,2560]{1,0:T(8,128)(2,1)}) custom-call(bf16[768,1664]{1,0:T(8,128)(2,1)} %get-tuple-element.156.gate_ref.gate_own, bf16[768,1664]{1,0:T(8,128)(2,1)} %get-tuple-element.157.up_ref.up_own, bf16[2560,1664]{1,0:T(8,128)(2,1)} %bitcast.122, bf16[2560,1664]{1,0:T(8,128)(2,1)} %bitcast.113, ...), custom_call_target="tpu_custom_call" | custom-call | tf_op jit(solution)/shard_map/mlp_back/pallas_call | solution.py:397
  778.4 19.4 %latent_back.3 = f32[192,1280]{1,0:T(8,128)} custom-call(bf16[768,1280]{1,0:T(8,128)(2,1)} %get-tuple-element.144.gq_ref, bf16[768,1280]{1,0:T(8,128)(2,1)} %get-tuple-element.145.gkv_ref, f32[768,128]{1,0:T(8,128)} %get-tuple-element.146.gsh_ref, bf16[768,1280]{1,0:T(8,128)(2,1)} %copy.116.qup_ref, bf16[256,1280]{1,0:T(8,128)(2,1)} %bitcast.139), custom_call_target="tpu_custom_call" | custom-call | tf_op jit(solution)/shard_map/latent_back/pallas_call | solution.py:397
  841.5 93.2 %recompute.1 = (bf16[3072,1664]{1,0:T(8,128)(2,1)}, bf16[3072,1664]{1,0:T(8,128)(2,1)}, bf16[3072,1664]{1,0:T(8,128)(2,1)}) custom-call(s32[8]{0:T(128)} %and_select_fusion.3.from_ref, s32[8]{0:T(128)} %get-tuple-element.344.own_ref, s32[8]{0:T(128)} %get-tuple-element.343.here_ref, bf16[3072,2560]{1,0:T(8,128)(2,1)} %all-gather.9.cloned.1.call-done.two_ref, ...), custom_call_target="tpu_custom_call" | custom-call | tf_op jit(solution)/shard_map/recompute/pallas_call | solution.py:1201
  940.8 14.2 %fusion.32 = bf16[640,1664]{1,0:T(8,128)(2,1)} fusion(bf16[3072,1664]{1,0:T(8,128)(2,1)} %get-tuple-element.162.gate_ref, bf16[3072,2560]{1,0:T(8,128)(2,1)} %all-gather.9.cloned.1.call-done.two_ref, s32[]{:T(128)S(6)} %select_n.72), kind=kOutput, calls=%fused_computation.50 | convolution fusion | flops 6544179200 | bytes 16285700 | tf_op jit(solution)/shard_map/dot_general | solution.py:74
  993.5 12.2 %fusion.38 = bf16[640,1664]{1,0:T(8,128)(2,1)} fusion(bf16[3072,1664]{1,0:T(8,128)(2,1)} %get-tuple-element.169.up_ref, bf16[3072,2560]{1,0:T(8,128)(2,1)} %all-gather.9.cloned.1.call-done.two_ref, s32[]{:T(128)S(6)} %select_n.72), kind=kOutput, calls=%fused_computation.52 | convolution fusion | flops 6544179200 | bytes 16285700 | tf_op jit(solution)/shard_map/dot_general | solution.py:74
  1005.7 12.2 %fusion.35 = bf16[640,1664]{1,0:T(8,128)(2,1)} fusion(bf16[3072,1664]{1,0:T(8,128)(2,1)} %get-tuple-element.169.up_ref, bf16[3072,2560]{1,0:T(8,128)(2,1)} %all-gather.9.cloned.1.call-done.two_ref, s32[]{:T(128)S(6)} %select_n.71), kind=kOutput, calls=%fused_computation.51 | convolution fusion | flops 6544179200 | bytes 16285700 | tf_op jit(solution)/shard_map/dot_general | solution.py:74
  1019.4 43.7 %chip_gradients.1 = (bf16[2,640,1664]{2,1,0:T(8,128)(2,1)}, bf16[2,640,1664]{2,1,0:T(8,128)(2,1)}) custom-call(s32[2]{0:T(128)} %pad_add_fusion.order_ref, bf16[3072,2560]{1,0:T(8,128)(2,1)} %all-gather.9.cloned.1.call-done.two_ref, bf16[3072,1664]{1,0:T(8,128)(2,1)} %get-tuple-element.162.gate_ref, bf16[3072,1664]{1,0:T(8,128)(2,1)} %get-tuple-element.169.up_ref), custom_call_target="tpu_custom_call" | custom-call | tf_op jit(solution)/shard_map/chip_gradients/pallas_call | solution.py:1134
  1078.3 37.5 %down_gradient.1 = f32[1600,2560]{1,0:T(8,128)} custom-call(bf16[3072,1664]{1,0:T(8,128)(2,1)} %get-tuple-element.172.act_ref, bf16[1536,2560]{1,0:T(8,128)(2,1)} %all-gather.11.cloned.1.call-done.near_ref, bf16[1536,2560]{1,0:T(8,128)(2,1)} %collective-permute-done.1.beside_ref), custom_call_target="tpu_custom_call" | custom-call | tf_op jit(solution)/shard_map/down_gradient/pallas_call | solution.py:1245
  1115.8 12.3 %place_windows.2 = f32[640,6400]{1,0:T(8,128)} custom-call(bf16[640,1664]{1,0:T(8,128)(2,1)} %get-tuple-element.176.refs_0_, bf16[640,1664]{1,0:T(8,128)(2,1)} %collective-permute-done.4.refs_1_, bf16[640,1664]{1,0:T(8,128)(2,1)} %collective-permute-done.2.refs_2_, bf16[640,1664]{1,0:T(8,128)(2,1)} %collective-permute-done.3.refs_3_), custom_call_target="tpu_custom_call" | custom-call | bytes 32768000 | tf_op jit(solution)/shard_map/place_windows/pallas_call | solution.py:1283
  1128.1 29.7 %collective-permute-done.7.refs_3_ = bf16[640,1664]{1,0:T(8,128)(2,1)} collective-permute-done((bf16[640,1664]{1,0:T(8,128)(2,1)}, bf16[640,1664]{1,0:T(8,128)(2,1)}, u32[]{:S(2)}, u32[]{:S(2)}) %collective-permute-start.7) | collective-permute-done | bytes 2129952 | tf_op jit(solution)/shard_map/ppermute | solution.py:1068
  1157.8 12.2 %place_windows.3 = f32[640,6400]{1,0:T(8,128)} custom-call(bf16[640,1664]{1,0:T(8,128)(2,1)} %get-tuple-element.181.refs_0_, bf16[640,1664]{1,0:T(8,128)(2,1)} %collective-permute-done.5.refs_1_, bf16[640,1664]{1,0:T(8,128)(2,1)} %collective-permute-done.6.refs_2_, bf16[640,1664]{1,0:T(8,128)(2,1)} %collective-permute-done.7.refs_3_), custom_call_target="tpu_custom_call" | custom-call | bytes 32768000 | tf_op jit(solution)/shard_map/place_windows/pallas_call | solution.py:1283
  (331 shorter events, 296.7 us)
Async XLA Ops:
  7.2 263.8 %all-gather.5.cloned.1.call-start = ((), (), s32[]{:S(2)}) async-start(), calls=%async_computation.2 | async-start | bytes 4915200 | tf_op jit(solution)/shard_map/all_gather | solution.py:440
  7.2 151.4 %copy-start.52 = (f32[16]{0:T(128)}, f32[16]{0:T(128)S(1)}, u32[]{:S(2)}) copy-start(f32[16]{0:T(128)S(1)} %multiply_exponential_fusion) | copy-start | bytes 196
  8.3 150.4 %copy-start.42 = (f32[192]{0:T(256)}, f32[192]{0:T(256)S(1)}, u32[]{:S(2)}) copy-start(f32[192]{0:T(256)S(1)} %convert_element_type.177) | copy-start | bytes 2308
  10.5 581.3 %copy-start.34 = (f32[768]{0:T(1024)}, f32[768]{0:T(1024)S(1)}, u32[]{:S(2)}) copy-start(f32[768]{0:T(1024)S(1)} %reduce.2) | copy-start | bytes 9220
  11.3 584.5 %copy-start.32 = (f32[2560]{0:T(1024)}, f32[2560]{0:T(1024)S(1)}, u32[]{:S(2)}) copy-start(f32[2560]{0:T(1024)S(1)} %reduce.1) | copy-start | bytes 30724
  14.3 141.9 %copy-start.12 = (bf16[192,2560]{1,0:T(8,128)(2,1)S(1)}, bf16[192,2560]{1,0:T(8,128)(2,1)}, u32[]{:S(2)}) copy-start(bf16[192,2560]{1,0:T(8,128)(2,1)} %param.15) | copy-start | bytes 2949124
  179.9 409.4 %all-gather.7.cloned.1.call-start = ((), (), s32[]{:S(2)}) async-start(), calls=%async_computation.3 | async-start | bytes 9830400 | tf_op jit(solution)/shard_map/all_gather | solution.py:1263
  345.8 24.0 %copy-start.46 = (f32[192]{0:T(256)}, f32[192]{0:T(256)S(1)}, u32[]{:S(2)}) copy-start(f32[192]{0:T(256)S(1)} %get-tuple-element.334) | copy-start | bytes 2308
  443.1 225.9 %all-gather.9.cloned.1.call-start = ((), (), s32[]{:S(2)}) async-start(), calls=%async_computation.4 | async-start | bytes 23592960 | tf_op jit(solution)/shard_map/all_gather | solution.py:1269
  589.4 225.8 %all-gather.11.cloned.1.call-start = ((), (), s32[]{:S(2)}) async-start(), calls=%async_computation.5 | async-start | bytes 9830400 | tf_op jit(solution)/shard_map/all_gather | solution.py:1263
  599.2 37.2 %collective-permute-start = (bf16[192,2560]{1,0:T(8,128)(2,1)}, bf16[192,2560]{1,0:T(8,128)(2,1)}, u32[]{:S(2)}, u32[]{:S(2)}) collective-permute-start(bf16[192,2560]{1,0:T(8,128)(2,1)} %add_convert_fusion), channel_id=1, source_target_pairs={{16,0},{17,1},{18,2},{19,3},{20,4},{21,5},{22,6},{23,7},{24,8},{25... | collective-permute-start | bytes 2949128 | tf_op jit(solution)/shard_map/ppermute | solution.py:1341
  672.0 268.8 %all-reduce.12.cloned.1.call-start = ((), (), s32[]{:S(2)}) async-start(), calls=%async_computation.6 | async-start | bytes 6553600 | tf_op jit(solution)/shard_map/psum | solution.py:1367
  778.4 21.1 %copy-start.41 = (f32[1,256]{1,0:T(1,128)S(1)}, f32[1,256]{1,0:T(1,128)}, u32[]{:S(2)}) copy-start(f32[1,256]{1,0:T(1,128)} %param.19) | copy-start | bytes 3076
  778.4 22.3 %copy-start.35 = (f32[768]{0:T(1024)S(1)}, f32[768]{0:T(1024)}, u32[]{:S(2)}) copy-start(f32[768]{0:T(1024)} %copy-done.34) | copy-start | bytes 9220
  815.3 26.2 %collective-permute-start.1 = (bf16[1536,2560]{1,0:T(8,128)(2,1)}, bf16[1536,2560]{1,0:T(8,128)(2,1)}, u32[]{:S(2)}, u32[]{:S(2)}) collective-permute-start(bf16[1536,2560]{1,0:T(8,128)(2,1)} %all-gather.11.cloned.1.call-done.near_ref), channel_id=1, source_target_pairs={{0,1},{1,0},{2,3},{3,2},{4,5},{5,4},{6,7},{7,6},{8,9},{9,8},{10,11... | collective-permute-start | bytes 23592968 | tf_op jit(solution)/shard_map/ppermute | solution.py:1068
  816.8 17.2 %all-to-all-start = ((bf16[4,192,640]{2,1,0:T(8,128)(2,1)}), bf16[4,192,640]{2,1,0:T(8,128)(2,1)}, u32[]{:S(2)}, u32[]{:S(2)}) async-start(bf16[4,192,640]{2,1,0:T(8,128)(2,1)} %bitcast.152), calls=%async_computation | async-start | bytes 1966080 | tf_op jit(solution)/shard_map/all_to_all | solution.py:1358
  834.0 132.1 %all-to-all-start.1 = ((bf16[4,464,1280]{2,1,0:T(8,128)(2,1)}), bf16[4,464,1280]{2,1,0:T(8,128)(2,1)}, u32[]{:S(2)}, u32[]{:S(2)}) async-start(bf16[4,464,1280]{2,1,0:T(8,128)(2,1)} %pad_maximum_fusion), calls=%async_computation.1 | async-start | bytes 9502720 | tf_op jit(solution)/shard_map/all_to_all | solution.py:917
  839.9 330.2 %all-reduce.14.cloned.1.call-start = ((), (), s32[]{:S(2)}) async-start(), calls=%async_computation.7 | async-start | bytes 7245824 | tf_op jit(solution)/shard_map/psum | solution.py:1396
  972.5 95.4 %collective-permute-start.2 = (bf16[640,1664]{1,0:T(8,128)(2,1)}, bf16[640,1664]{1,0:T(8,128)(2,1)}, u32[]{:S(2)}, u32[]{:S(2)}) collective-permute-start(bf16[640,1664]{1,0:T(8,128)(2,1)} %fusion.29), channel_id=1, source_target_pairs={{0,2},{1,3},{2,0},{3,1},{4,6},{5,7},{6,4},{7,5},{8,10},{9,11},{10,... | collective-permute-start | bytes 6389768 | tf_op jit(solution)/shard_map/ppermute | solution.py:1068
  973.6 94.4 %collective-permute-start.3 = (bf16[640,1664]{1,0:T(8,128)(2,1)}, bf16[640,1664]{1,0:T(8,128)(2,1)}, u32[]{:S(2)}, u32[]{:S(2)}) collective-permute-start(bf16[640,1664]{1,0:T(8,128)(2,1)} %fusion.32), channel_id=1, source_target_pairs={{0,3},{1,2},{2,1},{3,0},{4,7},{5,6},{6,5},{7,4},{8,11},{9,10},{10,... | collective-permute-start | bytes 6389768 | tf_op jit(solution)/shard_map/ppermute | solution.py:1068
  1017.9 110.2 %collective-permute-start.6 = (bf16[640,1664]{1,0:T(8,128)(2,1)}, bf16[640,1664]{1,0:T(8,128)(2,1)}, u32[]{:S(2)}, u32[]{:S(2)}) collective-permute-start(bf16[640,1664]{1,0:T(8,128)(2,1)} %fusion.35), channel_id=1, source_target_pairs={{0,2},{1,3},{2,0},{3,1},{4,6},{5,7},{6,4},{7,5},{8,10},{9,11},{10,... | collective-permute-start | bytes 6389768 | tf_op jit(solution)/shard_map/ppermute | solution.py:1068
  1019.1 138.7 %collective-permute-start.7 = (bf16[640,1664]{1,0:T(8,128)(2,1)}, bf16[640,1664]{1,0:T(8,128)(2,1)}, u32[]{:S(2)}, u32[]{:S(2)}) collective-permute-start(bf16[640,1664]{1,0:T(8,128)(2,1)} %fusion.38), channel_id=1, source_target_pairs={{0,3},{1,2},{2,1},{3,0},{4,7},{5,6},{6,5},{7,4},{8,11},{9,10},{10,... | collective-permute-start | bytes 6389768 | tf_op jit(solution)/shard_map/ppermute | solution.py:1068
  1067.9 47.9 %collective-permute-start.4 = (bf16[640,1664]{1,0:T(8,128)(2,1)}, bf16[640,1664]{1,0:T(8,128)(2,1)}, u32[]{:S(2)}, u32[]{:S(2)}) collective-permute-start(bf16[640,1664]{1,0:T(8,128)(2,1)} %get-tuple-element.173), channel_id=1, source_target_pairs={{0,1},{1,0},{2,3},{3,2},{4,5},{5,4},{6,7},{7,6},{8,9},{9,8},{10,11... | collective-permute-start | bytes 6389768 | tf_op jit(solution)/shard_map/ppermute | solution.py:1068
  1070.8 87.0 %collective-permute-start.5 = (bf16[640,1664]{1,0:T(8,128)(2,1)}, bf16[640,1664]{1,0:T(8,128)(2,1)}, u32[]{:S(2)}, u32[]{:S(2)}) collective-permute-start(bf16[640,1664]{1,0:T(8,128)(2,1)} %get-tuple-element.308), channel_id=1, source_target_pairs={{0,1},{1,0},{2,3},{3,2},{4,5},{5,4},{6,7},{7,6},{8,9},{9,8},{10,11... | collective-permute-start | bytes 6389768 | tf_op jit(solution)/shard_map/ppermute | solution.py:1068
  (60 other events, 282.4 us)
Sparse Core Ops, SparseCore 0:
  180.1 35.1 all-gather.4
  443.2 140.6 all-gather.6
  589.5 30.5 all-gather.8
  672.2 143.0 all-gather.10
  817.5 123.2 all-reduce.11
  1005.8 137.0 all-reduce.13

commit v6 on v5

--- a/solution.py
+++ b/solution.py
@@ -1413,17 +1413,20 @@
         total_down = contract_rows(activated_all, down_all)
         total_down = lax.dynamic_slice_in_dim(total_down, take_at(offsets, me), size, 0)
     total_gate = place_windows(hidden_parts[0], count)
-    total_gate, hidden_parts[1][0] = together(total_gate, hidden_parts[1][0])
-    total_up = place_windows(hidden_parts[1], count)
-    total_up, total_down_both, total_latent, total_query = together(
-        total_up, total_down_both, total_latent, total_query
+    total_gate, total_down_both, total_latent, total_query = together(
+        total_gate, total_down_both, total_latent, total_query
     )
     gain_rows = total_down_both.shape[0] - D // count
     gain_totals = total_down_both[-gain_rows:].reshape(-1).astype(f32)
     total_down_both = total_down_both[:-gain_rows].astype(f32)
-    total_query, total_latent = total_query.astype(f32), total_latent.astype(f32)
     first, second, third = D, D + QRANK, D + QRANK + KVRANK
-    gain_totals = (gain_totals[:first], gain_totals[first:second], gain_totals[second:third], gain_totals[third:third + D])
+    hidden_parts[1][0], total_gate, *finished = together(
+        hidden_parts[1][0], total_gate, total_down_both[:, :QRANK], total_down_both[:, QRANK:],
+        total_query.astype(f32), total_latent.astype(f32), gain_totals[:first], gain_totals[first:second],
+        gain_totals[second:third], gain_totals[third:third + D],
+    )
+    total_down_q, total_down_kv, total_query, total_latent, *gain_totals = finished
+    total_up = place_windows(hidden_parts[1], count)
     return (
         boundary[None],
         grad[None],
@@ -1431,9 +1434,9 @@
         gain_totals[1][None],
         gain_totals[2][None],
         gain_totals[3][None],
-        total_down_both[None, :, :QRANK],
+        total_down_q[None],
         total_query[None],
-        total_down_both[None, :, QRANK:],
+        total_down_kv[None],
         total_latent[None],
         total_output.astype(f32)[None],
         total_gate[None],

time: 1200 us -> 1190 us (level)
    ppermute x7, waiting for transfers between devices: 29.8 us -> 8.96 us  [swap(): lax.ppermute(value, 'shard', [(source, source ^ step) for source in range...]
    psum x1, waiting for transfers between devices: 0.01 us -> 15.1 us  [body(): total_down_both, total_latent, total_query = lax.psum(tuple(shares), 'rep')]
  transfers between devices with their start and end apart: 16 -> 16, of which waited for: 4 -> 6; matrix products, arithmetic and copies ran while one was open for 19% -> 19% of each run, Pallas kernels for 44% -> 43%
where the time goes in v6:
time: 1190 us; the launch traced here: 1180 us
  Pallas kernels  808 us (68%)
  matrix products  188 us (16%)
  local copies, waits for them, and re-layouts  68.5 us (6%)
  other arithmetic  48.4 us (4%)
  waiting for transfers between devices  38.3 us (3%)
  starting transfers between devices  16.5 us (1%)
  between operations  15.8 us (1%)
    pallas_call x11, Pallas kernels, comm_call(): pl.pallas_call(kernel, in_specs=vmem(len(inputs) - len(aliased)) + any_sp...  422 us
    pallas_call x1, Pallas kernels, move(): pl.pallas_call(functools.partial(move_kernel, len(wholes), alike, [f for...  142 us
    pallas_call x1, Pallas kernels, recompute(): pl.pallas_call(recompute_kernel, grid_spec=pltpu.PrefetchScalarGridSpec(n...  93.2 us
    dot_general x8, matrix products, contract_rows(): lax.dot_general(left, right, (((0,), (0,)), ((), ())), preferred_element_...  65.9 us
    dot_general x12, matrix products, project(): return jnp.dot(left, weight, preferred_element_type=f32)  65.3 us
    dot_general x8, matrix products, contract_cols(): lax.dot_general(left, right, (((1,), (1,)), ((), ())), preferred_element_...  57 us
    pallas_call x1, Pallas kernels, chip_gradients(): pl.pallas_call(chip_gradients_kernel, grid_spec=pltpu.PrefetchScalarGridS...  43.8 us
    pallas_call x1, Pallas kernels, down_gradient(): pl.pallas_call(down_gradient_kernel, grid=(D // piece,), in_specs=[pl.Blo...  37.5 us
  transfers between devices with their start and end apart: 16, of which 6 were waited for; matrix products, arithmetic and copies ran while one was open for 19% of the time, Pallas kernels for 43%

profile of v6, /device:TPU:1, one launch (start us, length us, event | category | flops | bytes accessed | tf_op | source)
XLA Modules:
  0.0 1183.2 jit_solution(5463584666076262391)
XLA Ops:
  14.3 141.9 %first_move.1 = (bf16[4,640,768]{2,1,0:T(8,128)(2,1)}, bf16[4,640,288]{2,1,0:T(8,128)(2,1)}, s32[4,2,96]{2,1,0:T(2,128)}, bf16[4,192,1024]{2,1,0:T(8,128)(2,1)},...) custom-call(bf16[640,768]{1,0:T(8,128)(2,1)} %bitcast.158, ...), custom_call_target="tpu_custom_call" | custom-call | bytes 79465472 | tf_op jit(solution)/shard_map/first_move/pallas_call | solution.py:838
  163.7 16.2 %gather_rows.3 = bf16[768,1152]{1,0:T(8,128)(2,1)} custom-call(bf16[192,1152]{1,0:T(8,128)(2,1)} %fusion.54.own_ref), custom_call_target="tpu_custom_call" | custom-call | tf_op jit(solution)/shard_map/gather_rows/pallas_call | solution.py:397
  213.3 57.7 %output_norm.2 = (f32[192,2560]{1,0:T(8,128)}, bf16[768,2560]{1,0:T(8,128)(2,1)}, bf16[4,640,1664]{2,1,0:T(8,128)(2,1)}) custom-call(bf16[768,640]{1,0:T(8,128)(2,1)} %get-tuple-element.117.att_ref, bf16[640,2560]{1,0:T(8,128)(2,1)} %bitcast.130, f32[192,2560]{1,0:T(8,128)} %convert_element_type.177.hidden_ref, ...), custom_call_target="tpu_custom_call", output_to_operand_aliasing={{2}: (4, {})} | custom-call | tf_op jit(solution)/shard_map/output_norm/pallas_call | solution.py:397
  291.4 45.8 %down_project.2 = (f32[192,2560]{1,0:T(8,128)}, bf16[192,2560]{1,0:T(8,128)(2,1)}, bf16[192,2560]{1,0:T(8,128)(2,1)}, bf16[1664,2560]{1,0:T(8,128)(2,1)}) custom-call(bf16[768,1664]{1,0:T(8,128)(2,1)} %fusion.19.act_ref, bf16[1600,2560]{1,0:T(8,128)(2,1)} %bitcast.139, f32[192,2560]{1,0:T(8,128)} %get-tuple-element.126.mixed_ref), custom_call_target="tpu_custom_call" | custom-call | tf_op jit(solution)/shard_map/down_project/pallas_call | solution.py:397
  346.6 15.9 %gather_rows.4 = bf16[768,1152]{1,0:T(8,128)(2,1)} custom-call(bf16[192,1152]{1,0:T(8,128)(2,1)} %fusion.55.own_ref), custom_call_target="tpu_custom_call" | custom-call | tf_op jit(solution)/shard_map/gather_rows/pallas_call | solution.py:397
  383.9 56.1 %output_norm.3 = (f32[192,2560]{1,0:T(8,128)}, bf16[768,2560]{1,0:T(8,128)(2,1)}) custom-call(bf16[768,640]{1,0:T(8,128)(2,1)} %get-tuple-element.130.att_ref, bf16[640,2560]{1,0:T(8,128)(2,1)} %bitcast.131, f32[192,2560]{1,0:T(8,128)} %copy-done.1, f32[1,2560]{1,0:T(1,128)} %gain_ref.7), custom_call_target="tpu_custom_call" | custom-call | tf_op jit(solution)/shard_map/output_norm/pallas_call | solution.py:397
  448.7 13.9 %convolution_convert_fusion.1 = bf16[768,1664]{1,0:T(8,128)(2,1)} fusion(bf16[768,2560]{1,0:T(8,128)(2,1)} %get-tuple-element.131, bf16[2560,1664]{1,0:T(8,128)(2,1)} %bitcast.114), kind=kOutput, calls=%fused_computation.43 | convolution fusion | flops 6544392192 | bytes 15007744 | tf_op jit(solution)/shard_map/dot_general | solution.py:82
  471.2 16.1 %fusion.16 = (bf16[768,1664]{1,0:T(8,128)(2,1)}, bf16[768,1664]{1,0:T(8,128)(2,1)}, bf16[768,1664]{1,0:T(8,128)(2,1)}) fusion(bf16[768,1664]{1,0:T(8,128)(2,1)} %convolution_convert_fusion.1, bf16[768,1664]{1,0:T(8,128)(2,1)} %convolution_convert_fusion.2, bf16[768,2560]{1,0:T(8,128)(2,1)} %all-gather.5.cloned.1.call-done, ...), kind=kOutput, calls=%fused_computation.26 | convolution fusion | flops 6566117376 | bytes 25231360 | tf_op jit(solution)/shard_map/dot_general | solution.py:78
  487.3 63.6 %mlp_back.2 = (f32[192,2560]{1,0:T(8,128)}, f32[1,2560]{1,0:T(1,128)}, bf16[768,2560]{1,0:T(8,128)(2,1)}) custom-call(bf16[768,1664]{1,0:T(8,128)(2,1)} %get-tuple-element.320.gate_ref, bf16[768,1664]{1,0:T(8,128)(2,1)} %get-tuple-element.319.up_ref, bf16[2560,1664]{1,0:T(8,128)(2,1)} %bitcast.115, bf16[2560,1664]{1,0:T(8,128)(2,1)} %bitcast.106, ...), custom_call_target="tpu_custom_call" | custom-call | tf_op jit(solution)/shard_map/mlp_back/pallas_call | solution.py:397
  569.9 19.3 %latent_back.2 = f32[192,1280]{1,0:T(8,128)} custom-call(bf16[768,1280]{1,0:T(8,128)(2,1)} %get-tuple-element.138.gq_ref, bf16[768,1280]{1,0:T(8,128)(2,1)} %get-tuple-element.139.gkv_ref, f32[768,128]{1,0:T(8,128)} %get-tuple-element.140.gsh_ref, bf16[768,1280]{1,0:T(8,128)(2,1)} %copy.116.qup_ref, bf16[256,1280]{1,0:T(8,128)(2,1)} %bitcast.133), custom_call_target="tpu_custom_call" | custom-call | tf_op jit(solution)/shard_map/latent_back/pallas_call | solution.py:397
  600.4 36.0 %down_project.3 = (f32[192,2560]{1,0:T(8,128)}, bf16[192,2560]{1,0:T(8,128)(2,1)}) custom-call(bf16[768,1664]{1,0:T(8,128)(2,1)} %get-tuple-element.143.act_ref.act_own, bf16[1664,2560]{1,0:T(8,128)(2,1)} %get-tuple-element.127.given_ref.rows_ref, f32[192,2560]{1,0:T(8,128)} %get-tuple-element.132.mixed_ref), custom_call_target="tpu_custom_call" | custom-call | tf_op jit(solution)/shard_map/down_project/pallas_call | solution.py:397
  640.5 28.4 %gather_rows.5 = bf16[768,2560]{1,0:T(8,128)(2,1)} custom-call(bf16[192,2560]{1,0:T(8,128)(2,1)} %multiply_convert_fusion.own_ref), custom_call_target="tpu_custom_call" | custom-call | tf_op jit(solution)/shard_map/gather_rows/pallas_call | solution.py:397
  672.0 15.3 %fusion.18 = (bf16[768,1664]{1,0:T(8,128)(2,1)}, bf16[768,1664]{1,0:T(8,128)(2,1)}) fusion(bf16[768,1664]{1,0:T(8,128)(2,1)} %convolution_convert_fusion.1, bf16[768,1664]{1,0:T(8,128)(2,1)} %convolution_convert_fusion.2, bf16[768,2560]{1,0:T(8,128)(2,1)} %gather_rows.5, bf16[1664,2560]{1,0:T(8,128)(2,1)} %get-tuple-element.127.given_ref.rows_ref), kind=kOutput, calls=%fused_computation.28 | convolution fusion | flops 6562283520 | bytes 22675456 | tf_op jit(solution)/shard_map/dot_general | solution.py:78
  687.3 63.5 %mlp_back.3 = (f32[192,2560]{1,0:T(8,128)}, f32[1,2560]{1,0:T(1,128)}, bf16[768,2560]{1,0:T(8,128)(2,1)}) custom-call(bf16[768,1664]{1,0:T(8,128)(2,1)} %get-tuple-element.164.gate_ref.gate_own, bf16[768,1664]{1,0:T(8,128)(2,1)} %get-tuple-element.165.up_ref.up_own, bf16[2560,1664]{1,0:T(8,128)(2,1)} %bitcast.116, bf16[2560,1664]{1,0:T(8,128)(2,1)} %bitcast.107, ...), custom_call_target="tpu_custom_call" | custom-call | tf_op jit(solution)/shard_map/mlp_back/pallas_call | solution.py:397
  778.4 19.4 %latent_back.3 = f32[192,1280]{1,0:T(8,128)} custom-call(bf16[768,1280]{1,0:T(8,128)(2,1)} %get-tuple-element.152.gq_ref, bf16[768,1280]{1,0:T(8,128)(2,1)} %get-tuple-element.153.gkv_ref, f32[768,128]{1,0:T(8,128)} %get-tuple-element.154.gsh_ref, bf16[768,1280]{1,0:T(8,128)(2,1)} %copy.116.qup_ref, bf16[256,1280]{1,0:T(8,128)(2,1)} %bitcast.134), custom_call_target="tpu_custom_call" | custom-call | tf_op jit(solution)/shard_map/latent_back/pallas_call | solution.py:397
  841.5 93.2 %recompute.1 = (bf16[3072,1664]{1,0:T(8,128)(2,1)}, bf16[3072,1664]{1,0:T(8,128)(2,1)}, bf16[3072,1664]{1,0:T(8,128)(2,1)}) custom-call(s32[8]{0:T(128)} %and_select_fusion.3.from_ref, s32[8]{0:T(128)} %get-tuple-element.360.own_ref, s32[8]{0:T(128)} %get-tuple-element.359.here_ref, bf16[3072,2560]{1,0:T(8,128)(2,1)} %all-gather.9.cloned.1.call-done.two_ref, ...), custom_call_target="tpu_custom_call" | custom-call | tf_op jit(solution)/shard_map/recompute/pallas_call | solution.py:1201
  940.8 14.2 %fusion.32 = bf16[640,1664]{1,0:T(8,128)(2,1)} fusion(bf16[3072,1664]{1,0:T(8,128)(2,1)} %get-tuple-element.169.gate_ref, bf16[3072,2560]{1,0:T(8,128)(2,1)} %all-gather.9.cloned.1.call-done.two_ref, s32[]{:T(128)S(6)} %select_n.72), kind=kOutput, calls=%fused_computation.50 | convolution fusion | flops 6544179200 | bytes 16285700 | tf_op jit(solution)/shard_map/dot_general | solution.py:74
  993.4 12.2 %fusion.38 = bf16[640,1664]{1,0:T(8,128)(2,1)} fusion(bf16[3072,1664]{1,0:T(8,128)(2,1)} %get-tuple-element.176.up_ref, bf16[3072,2560]{1,0:T(8,128)(2,1)} %all-gather.9.cloned.1.call-done.two_ref, s32[]{:T(128)S(6)} %select_n.72), kind=kOutput, calls=%fused_computation.52 | convolution fusion | flops 6544179200 | bytes 16285700 | tf_op jit(solution)/shard_map/dot_general | solution.py:74
  1005.6 12.2 %fusion.35 = bf16[640,1664]{1,0:T(8,128)(2,1)} fusion(bf16[3072,1664]{1,0:T(8,128)(2,1)} %get-tuple-element.176.up_ref, bf16[3072,2560]{1,0:T(8,128)(2,1)} %all-gather.9.cloned.1.call-done.two_ref, s32[]{:T(128)S(6)} %select_n.69), kind=kOutput, calls=%fused_computation.51 | convolution fusion | flops 6544179200 | bytes 16285700 | tf_op jit(solution)/shard_map/dot_general | solution.py:74
  1017.9 43.8 %chip_gradients.1 = (bf16[2,640,1664]{2,1,0:T(8,128)(2,1)}, bf16[2,640,1664]{2,1,0:T(8,128)(2,1)}) custom-call(s32[2]{0:T(128)} %pad_add_fusion.order_ref, bf16[3072,2560]{1,0:T(8,128)(2,1)} %all-gather.9.cloned.1.call-done.two_ref, bf16[3072,1664]{1,0:T(8,128)(2,1)} %get-tuple-element.169.gate_ref, bf16[3072,1664]{1,0:T(8,128)(2,1)} %get-tuple-element.176.up_ref), custom_call_target="tpu_custom_call" | custom-call | tf_op jit(solution)/shard_map/chip_gradients/pallas_call | solution.py:1134
  1078.0 37.5 %down_gradient.1 = f32[1600,2560]{1,0:T(8,128)} custom-call(bf16[3072,1664]{1,0:T(8,128)(2,1)} %get-tuple-element.181.act_ref, bf16[1536,2560]{1,0:T(8,128)(2,1)} %all-gather.11.cloned.1.call-done.near_ref, bf16[1536,2560]{1,0:T(8,128)(2,1)} %collective-permute-done.1.beside_ref), custom_call_target="tpu_custom_call" | custom-call | tf_op jit(solution)/shard_map/down_gradient/pallas_call | solution.py:1245
  1115.5 12.3 %place_windows.2 = f32[640,6400]{1,0:T(8,128)} custom-call(bf16[640,1664]{1,0:T(8,128)(2,1)} %get-tuple-element.185.refs_0_, bf16[640,1664]{1,0:T(8,128)(2,1)} %collective-permute-done.4.refs_1_, bf16[640,1664]{1,0:T(8,128)(2,1)} %collective-permute-done.2.refs_2_, bf16[640,1664]{1,0:T(8,128)(2,1)} %collective-permute-done.3.refs_3_), custom_call_target="tpu_custom_call" | custom-call | bytes 32768000 | tf_op jit(solution)/shard_map/place_windows/pallas_call | solution.py:1283
  1127.7 15.1 %all-reduce.14.cloned.1.call-done = (bf16[646,1056]{1,0:T(8,128)(2,1)}, bf16[64,5120]{1,0:T(8,128)(2,1)}, bf16[192,3840]{1,0:T(8,128)(2,1)}) async-done(((bf16[646,1056]{1,0:T(8,128)(2,1)}, bf16[64,5120]{1,0:T(8,128)(2,1)}, bf16[192,3840]{1,0:T(8,128)(2,1)}), (bf16[646,1056]{1,0:T(8,128)(2,1)}, bf16[64,5120]{1,0:T(8,128)(2,1)}, bf16[192,3840]{1,0:T(8,128)(2,1)})) %all-reduce.14.cloned.1.call-update) | async-done | bytes 3494288 | tf_op jit(solution)/shard_map/psum | solution.py:1396
  1162.7 12.2 %place_windows.3 = f32[640,6400]{1,0:T(8,128)} custom-call(bf16[640,1664]{1,0:T(8,128)(2,1)} %get-tuple-element.206.refs_0_, bf16[640,1664]{1,0:T(8,128)(2,1)} %collective-permute-done.5.refs_1_, bf16[640,1664]{1,0:T(8,128)(2,1)} %collective-permute-done.6.refs_2_, bf16[640,1664]{1,0:T(8,128)(2,1)} %collective-permute-done.7.refs_3_), custom_call_target="tpu_custom_call" | custom-call | bytes 32768000 | tf_op jit(solution)/shard_map/place_windows/pallas_call | solution.py:1283
  (334 shorter events, 305.8 us)
Async XLA Ops:
  7.2 263.9 %all-gather.5.cloned.1.call-start = ((), (), s32[]{:S(2)}) async-start(), calls=%async_computation.2 | async-start | bytes 4915200 | tf_op jit(solution)/shard_map/all_gather | solution.py:440
  7.2 151.4 %copy-start.53 = (f32[16]{0:T(128)}, f32[16]{0:T(128)S(1)}, u32[]{:S(2)}) copy-start(f32[16]{0:T(128)S(1)} %multiply_exponential_fusion) | copy-start | bytes 196
  8.3 150.4 %copy-start.43 = (f32[192]{0:T(256)}, f32[192]{0:T(256)S(1)}, u32[]{:S(2)}) copy-start(f32[192]{0:T(256)S(1)} %convert_element_type.181) | copy-start | bytes 2308
  10.5 581.1 %copy-start.35 = (f32[768]{0:T(1024)}, f32[768]{0:T(1024)S(1)}, u32[]{:S(2)}) copy-start(f32[768]{0:T(1024)S(1)} %reduce.2) | copy-start | bytes 9220
  11.3 584.3 %copy-start.33 = (f32[2560]{0:T(1024)}, f32[2560]{0:T(1024)S(1)}, u32[]{:S(2)}) copy-start(f32[2560]{0:T(1024)S(1)} %reduce.1) | copy-start | bytes 30724
  14.3 141.9 %copy-start.13 = (bf16[192,2560]{1,0:T(8,128)(2,1)S(1)}, bf16[192,2560]{1,0:T(8,128)(2,1)}, u32[]{:S(2)}) copy-start(bf16[192,2560]{1,0:T(8,128)(2,1)} %param.15) | copy-start | bytes 2949124
  179.9 409.3 %all-gather.7.cloned.1.call-start = ((), (), s32[]{:S(2)}) async-start(), calls=%async_computation.3 | async-start | bytes 9830400 | tf_op jit(solution)/shard_map/all_gather | solution.py:1263
  345.6 24.0 %copy-start.47 = (f32[192]{0:T(256)}, f32[192]{0:T(256)S(1)}, u32[]{:S(2)}) copy-start(f32[192]{0:T(256)S(1)} %get-tuple-element.350) | copy-start | bytes 2308
  443.0 226.0 %all-gather.9.cloned.1.call-start = ((), (), s32[]{:S(2)}) async-start(), calls=%async_computation.4 | async-start | bytes 23592960 | tf_op jit(solution)/shard_map/all_gather | solution.py:1269
  589.3 225.9 %all-gather.11.cloned.1.call-start = ((), (), s32[]{:S(2)}) async-start(), calls=%async_computation.5 | async-start | bytes 9830400 | tf_op jit(solution)/shard_map/all_gather | solution.py:1263
  599.1 37.3 %collective-permute-start = (bf16[192,2560]{1,0:T(8,128)(2,1)}, bf16[192,2560]{1,0:T(8,128)(2,1)}, u32[]{:S(2)}, u32[]{:S(2)}) collective-permute-start(bf16[192,2560]{1,0:T(8,128)(2,1)} %add_convert_fusion), channel_id=1, source_target_pairs={{16,0},{17,1},{18,2},{19,3},{20,4},{21,5},{22,6},{23,7},{24,8},{25... | collective-permute-start | bytes 2949128 | tf_op jit(solution)/shard_map/ppermute | solution.py:1341
  672.0 268.9 %all-reduce.12.cloned.1.call-start = ((), (), s32[]{:S(2)}) async-start(), calls=%async_computation.6 | async-start | bytes 6553600 | tf_op jit(solution)/shard_map/psum | solution.py:1367
  778.3 21.1 %copy-start.42 = (f32[1,256]{1,0:T(1,128)S(1)}, f32[1,256]{1,0:T(1,128)}, u32[]{:S(2)}) copy-start(f32[1,256]{1,0:T(1,128)} %param.19) | copy-start | bytes 3076
  778.4 22.3 %copy-start.36 = (f32[768]{0:T(1024)S(1)}, f32[768]{0:T(1024)}, u32[]{:S(2)}) copy-start(f32[768]{0:T(1024)} %copy-done.35) | copy-start | bytes 9220
  815.3 26.2 %collective-permute-start.1 = (bf16[1536,2560]{1,0:T(8,128)(2,1)}, bf16[1536,2560]{1,0:T(8,128)(2,1)}, u32[]{:S(2)}, u32[]{:S(2)}) collective-permute-start(bf16[1536,2560]{1,0:T(8,128)(2,1)} %all-gather.11.cloned.1.call-done.near_ref), channel_id=1, source_target_pairs={{0,1},{1,0},{2,3},{3,2},{4,5},{5,4},{6,7},{7,6},{8,9},{9,8},{10,11... | collective-permute-start | bytes 23592968 | tf_op jit(solution)/shard_map/ppermute | solution.py:1068
  816.8 17.2 %all-to-all-start = ((bf16[4,192,640]{2,1,0:T(8,128)(2,1)}), bf16[4,192,640]{2,1,0:T(8,128)(2,1)}, u32[]{:S(2)}, u32[]{:S(2)}) async-start(bf16[4,192,640]{2,1,0:T(8,128)(2,1)} %bitcast.147), calls=%async_computation | async-start | bytes 1966080 | tf_op jit(solution)/shard_map/all_to_all | solution.py:1358
  834.0 132.0 %all-to-all-start.1 = ((bf16[4,464,1280]{2,1,0:T(8,128)(2,1)}), bf16[4,464,1280]{2,1,0:T(8,128)(2,1)}, u32[]{:S(2)}, u32[]{:S(2)}) async-start(bf16[4,464,1280]{2,1,0:T(8,128)(2,1)} %pad_maximum_fusion), calls=%async_computation.1 | async-start | bytes 9502720 | tf_op jit(solution)/shard_map/all_to_all | solution.py:917
  839.9 302.9 %all-reduce.14.cloned.1.call-start = ((), (), s32[]{:S(2)}) async-start(), calls=%async_computation.7 | async-start | bytes 7245824 | tf_op jit(solution)/shard_map/psum | solution.py:1396
  972.4 94.0 %collective-permute-start.2 = (bf16[640,1664]{1,0:T(8,128)(2,1)}, bf16[640,1664]{1,0:T(8,128)(2,1)}, u32[]{:S(2)}, u32[]{:S(2)}) collective-permute-start(bf16[640,1664]{1,0:T(8,128)(2,1)} %fusion.29), channel_id=1, source_target_pairs={{0,2},{1,3},{2,0},{3,1},{4,6},{5,7},{6,4},{7,5},{8,10},{9,11},{10,... | collective-permute-start | bytes 6389768 | tf_op jit(solution)/shard_map/ppermute | solution.py:1068
  973.7 93.0 %collective-permute-start.3 = (bf16[640,1664]{1,0:T(8,128)(2,1)}, bf16[640,1664]{1,0:T(8,128)(2,1)}, u32[]{:S(2)}, u32[]{:S(2)}) collective-permute-start(bf16[640,1664]{1,0:T(8,128)(2,1)} %fusion.32), channel_id=1, source_target_pairs={{0,3},{1,2},{2,1},{3,0},{4,7},{5,6},{6,5},{7,4},{8,11},{9,10},{10,... | collective-permute-start | bytes 6389768 | tf_op jit(solution)/shard_map/ppermute | solution.py:1068
  1066.7 48.7 %collective-permute-start.4 = (bf16[640,1664]{1,0:T(8,128)(2,1)}, bf16[640,1664]{1,0:T(8,128)(2,1)}, u32[]{:S(2)}, u32[]{:S(2)}) collective-permute-start(bf16[640,1664]{1,0:T(8,128)(2,1)} %get-tuple-element.182), channel_id=1, source_target_pairs={{0,1},{1,0},{2,3},{3,2},{4,5},{5,4},{6,7},{7,6},{8,9},{9,8},{10,11... | collective-permute-start | bytes 6389768 | tf_op jit(solution)/shard_map/ppermute | solution.py:1068
  1068.7 85.4 %collective-permute-start.6 = (bf16[640,1664]{1,0:T(8,128)(2,1)}, bf16[640,1664]{1,0:T(8,128)(2,1)}, u32[]{:S(2)}, u32[]{:S(2)}) collective-permute-start(bf16[640,1664]{1,0:T(8,128)(2,1)} %fusion.35), channel_id=1, source_target_pairs={{0,2},{1,3},{2,0},{3,1},{4,6},{5,7},{6,4},{7,5},{8,10},{9,11},{10,... | collective-permute-start | bytes 6389768 | tf_op jit(solution)/shard_map/ppermute | solution.py:1068
  1070.0 92.7 %collective-permute-start.7 = (bf16[640,1664]{1,0:T(8,128)(2,1)}, bf16[640,1664]{1,0:T(8,128)(2,1)}, u32[]{:S(2)}, u32[]{:S(2)}) collective-permute-start(bf16[640,1664]{1,0:T(8,128)(2,1)} %fusion.38), channel_id=1, source_target_pairs={{0,3},{1,2},{2,1},{3,0},{4,7},{5,6},{6,5},{7,4},{8,11},{9,10},{10,... | collective-permute-start | bytes 6389768 | tf_op jit(solution)/shard_map/ppermute | solution.py:1068
  1073.3 80.8 %collective-permute-start.5 = (bf16[640,1664]{1,0:T(8,128)(2,1)}, bf16[640,1664]{1,0:T(8,128)(2,1)}, u32[]{:S(2)}, u32[]{:S(2)}) collective-permute-start(bf16[640,1664]{1,0:T(8,128)(2,1)} %get-tuple-element.324), channel_id=1, source_target_pairs={{0,1},{1,0},{2,3},{3,2},{4,5},{5,4},{6,7},{7,6},{8,9},{9,8},{10,11... | collective-permute-start | bytes 6389768 | tf_op jit(solution)/shard_map/ppermute | solution.py:1068
  (62 other events, 310.9 us)
Sparse Core Ops, SparseCore 0:
  180.1 35.1 all-gather.4
  443.1 140.6 all-gather.6
  589.4 30.6 all-gather.8
  672.1 143.1 all-gather.10
  817.5 123.2 all-reduce.11
  1005.8 137.0 all-reduce.13

commit v7 on v6

--- a/solution.py
+++ b/solution.py
@@ -444,7 +444,7 @@
     return lax.psum_scatter(value.astype(bf16), "shard", scatter_dimension=0, tiled=True).astype(f32)
 
 
-MODEL_STEP = 512
+MODEL_STEP = 256
 
 
 def output_kernel(relaying, att_ref, weight_ref, hidden_ref, gain_ref, *refs):
@@ -1344,7 +1344,7 @@
     incoming, boundary = together(incoming, boundary)
 
     own_grads, two_all, grad_down, grad_mixed, dgain_post, grad_branch = mlp_backward(
-        incoming, kept, gains, weights, lambda own: gather(own, 1, 512), two_all
+        incoming, kept, gains, weights, lambda own: gather(own, 1, 256), two_all
     )
     half_down = half_everywhere(grad_down, count)
     part_output = contract_rows(attended, grad_branch).astype(bf16)

time: 1190 us -> 1190 us (level)
  no operation moved by 1% of the time
where the time goes in v7:
time: 1190 us
  Pallas kernels  810 us (68%)
  matrix products  188 us (16%)
  local copies, waits for them, and re-layouts  68.5 us (6%)
  other arithmetic  48.4 us (4%)
  waiting for transfers between devices  38.7 us (3%)
  starting transfers between devices  16.5 us (1%)
  between operations  15.8 us (1%)
    pallas_call x11, Pallas kernels, comm_call(): pl.pallas_call(kernel, in_specs=vmem(len(inputs) - len(aliased)) + any_sp...  424 us
    pallas_call x1, Pallas kernels, move(): pl.pallas_call(functools.partial(move_kernel, len(wholes), alike, [f for...  142 us
    pallas_call x1, Pallas kernels, recompute(): pl.pallas_call(recompute_kernel, grid_spec=pltpu.PrefetchScalarGridSpec(n...  93.2 us
    dot_general x8, matrix products, contract_rows(): lax.dot_general(left, right, (((0,), (0,)), ((), ())), preferred_element_...  65.9 us
    dot_general x12, matrix products, project(): return jnp.dot(left, weight, preferred_element_type=f32)  65.3 us
    dot_general x8, matrix products, contract_cols(): lax.dot_general(left, right, (((1,), (1,)), ((), ())), preferred_element_...  57 us
    pallas_call x1, Pallas kernels, chip_gradients(): pl.pallas_call(chip_gradients_kernel, grid_spec=pltpu.PrefetchScalarGridS...  43.8 us
    pallas_call x1, Pallas kernels, down_gradient(): pl.pallas_call(down_gradient_kernel, grid=(D // piece,), in_specs=[pl.Blo...  37.5 us
  transfers between devices with their start and end apart: 16, of which 6 were waited for; matrix products, arithmetic and copies ran while one was open for 19% of the time, Pallas kernels for 43%

profile of v7, /device:TPU:1, one launch (start us, length us, event | category | flops | bytes accessed | tf_op | source)
XLA Modules:
  0.0 1185.9 jit_solution(12679644288676726247)
XLA Ops:
  14.3 141.9 %first_move.1 = (bf16[4,640,768]{2,1,0:T(8,128)(2,1)}, bf16[4,640,288]{2,1,0:T(8,128)(2,1)}, s32[4,2,96]{2,1,0:T(2,128)}, bf16[4,192,1024]{2,1,0:T(8,128)(2,1)},...) custom-call(bf16[640,768]{1,0:T(8,128)(2,1)} %bitcast.158, ...), custom_call_target="tpu_custom_call" | custom-call | bytes 79465472 | tf_op jit(solution)/shard_map/first_move/pallas_call | solution.py:838
  163.7 16.2 %gather_rows.3 = bf16[768,1152]{1,0:T(8,128)(2,1)} custom-call(bf16[192,1152]{1,0:T(8,128)(2,1)} %fusion.54.own_ref), custom_call_target="tpu_custom_call" | custom-call | tf_op jit(solution)/shard_map/gather_rows/pallas_call | solution.py:397
  213.3 57.8 %output_norm.2 = (f32[192,2560]{1,0:T(8,128)}, bf16[768,2560]{1,0:T(8,128)(2,1)}, bf16[4,640,1664]{2,1,0:T(8,128)(2,1)}) custom-call(bf16[768,640]{1,0:T(8,128)(2,1)} %get-tuple-element.117.att_ref, bf16[640,2560]{1,0:T(8,128)(2,1)} %bitcast.130, f32[192,2560]{1,0:T(8,128)} %convert_element_type.177.hidden_ref, ...), custom_call_target="tpu_custom_call", output_to_operand_aliasing={{2}: (4, {})} | custom-call | tf_op jit(solution)/shard_map/output_norm/pallas_call | solution.py:397
  291.5 49.6 %down_project.2 = (f32[192,2560]{1,0:T(8,128)}, bf16[192,2560]{1,0:T(8,128)(2,1)}, bf16[192,2560]{1,0:T(8,128)(2,1)}, bf16[1664,2560]{1,0:T(8,128)(2,1)}) custom-call(bf16[768,1664]{1,0:T(8,128)(2,1)} %fusion.19.act_ref, bf16[1600,2560]{1,0:T(8,128)(2,1)} %bitcast.139, f32[192,2560]{1,0:T(8,128)} %get-tuple-element.126.mixed_ref), custom_call_target="tpu_custom_call" | custom-call | tf_op jit(solution)/shard_map/down_project/pallas_call | solution.py:397
  350.5 15.9 %gather_rows.4 = bf16[768,1152]{1,0:T(8,128)(2,1)} custom-call(bf16[192,1152]{1,0:T(8,128)(2,1)} %fusion.55.own_ref), custom_call_target="tpu_custom_call" | custom-call | tf_op jit(solution)/shard_map/gather_rows/pallas_call | solution.py:397
  387.8 56.3 %output_norm.3 = (f32[192,2560]{1,0:T(8,128)}, bf16[768,2560]{1,0:T(8,128)(2,1)}) custom-call(bf16[768,640]{1,0:T(8,128)(2,1)} %get-tuple-element.130.att_ref, bf16[640,2560]{1,0:T(8,128)(2,1)} %bitcast.131, f32[192,2560]{1,0:T(8,128)} %copy-done.1, f32[1,2560]{1,0:T(1,128)} %gain_ref.7), custom_call_target="tpu_custom_call" | custom-call | tf_op jit(solution)/shard_map/output_norm/pallas_call | solution.py:397
  452.8 13.8 %convolution_convert_fusion.1 = bf16[768,1664]{1,0:T(8,128)(2,1)} fusion(bf16[768,2560]{1,0:T(8,128)(2,1)} %get-tuple-element.131, bf16[2560,1664]{1,0:T(8,128)(2,1)} %bitcast.114), kind=kOutput, calls=%fused_computation.43 | convolution fusion | flops 6544392192 | bytes 15007744 | tf_op jit(solution)/shard_map/dot_general | solution.py:82
  475.2 16.1 %fusion.16 = (bf16[768,1664]{1,0:T(8,128)(2,1)}, bf16[768,1664]{1,0:T(8,128)(2,1)}, bf16[768,1664]{1,0:T(8,128)(2,1)}) fusion(bf16[768,1664]{1,0:T(8,128)(2,1)} %convolution_convert_fusion.1, bf16[768,1664]{1,0:T(8,128)(2,1)} %convolution_convert_fusion.2, bf16[768,2560]{1,0:T(8,128)(2,1)} %all-gather.5.cloned.1.call-done, ...), kind=kOutput, calls=%fused_computation.26 | convolution fusion | flops 6566117376 | bytes 25231360 | tf_op jit(solution)/shard_map/dot_general | solution.py:78
  491.3 62.7 %mlp_back.2 = (f32[192,2560]{1,0:T(8,128)}, f32[1,2560]{1,0:T(1,128)}, bf16[768,2560]{1,0:T(8,128)(2,1)}) custom-call(bf16[768,1664]{1,0:T(8,128)(2,1)} %get-tuple-element.320.gate_ref, bf16[768,1664]{1,0:T(8,128)(2,1)} %get-tuple-element.319.up_ref, bf16[2560,1664]{1,0:T(8,128)(2,1)} %bitcast.115, bf16[2560,1664]{1,0:T(8,128)(2,1)} %bitcast.106, ...), custom_call_target="tpu_custom_call" | custom-call | tf_op jit(solution)/shard_map/mlp_back/pallas_call | solution.py:397
  573.0 19.3 %latent_back.2 = f32[192,1280]{1,0:T(8,128)} custom-call(bf16[768,1280]{1,0:T(8,128)(2,1)} %get-tuple-element.138.gq_ref, bf16[768,1280]{1,0:T(8,128)(2,1)} %get-tuple-element.139.gkv_ref, f32[768,128]{1,0:T(8,128)} %get-tuple-element.140.gsh_ref, bf16[768,1280]{1,0:T(8,128)(2,1)} %copy.116.qup_ref, bf16[256,1280]{1,0:T(8,128)(2,1)} %bitcast.133), custom_call_target="tpu_custom_call" | custom-call | tf_op jit(solution)/shard_map/latent_back/pallas_call | solution.py:397
  603.5 35.7 %down_project.3 = (f32[192,2560]{1,0:T(8,128)}, bf16[192,2560]{1,0:T(8,128)(2,1)}) custom-call(bf16[768,1664]{1,0:T(8,128)(2,1)} %get-tuple-element.143.act_ref.act_own, bf16[1664,2560]{1,0:T(8,128)(2,1)} %get-tuple-element.127.given_ref.rows_ref, f32[192,2560]{1,0:T(8,128)} %get-tuple-element.132.mixed_ref), custom_call_target="tpu_custom_call" | custom-call | tf_op jit(solution)/shard_map/down_project/pallas_call | solution.py:397
  643.4 28.6 %gather_rows.5 = bf16[768,2560]{1,0:T(8,128)(2,1)} custom-call(bf16[192,2560]{1,0:T(8,128)(2,1)} %multiply_convert_fusion.own_ref), custom_call_target="tpu_custom_call" | custom-call | tf_op jit(solution)/shard_map/gather_rows/pallas_call | solution.py:397
  675.0 15.3 %fusion.18 = (bf16[768,1664]{1,0:T(8,128)(2,1)}, bf16[768,1664]{1,0:T(8,128)(2,1)}) fusion(bf16[768,1664]{1,0:T(8,128)(2,1)} %convolution_convert_fusion.1, bf16[768,1664]{1,0:T(8,128)(2,1)} %convolution_convert_fusion.2, bf16[768,2560]{1,0:T(8,128)(2,1)} %gather_rows.5, bf16[1664,2560]{1,0:T(8,128)(2,1)} %get-tuple-element.127.given_ref.rows_ref), kind=kOutput, calls=%fused_computation.28 | convolution fusion | flops 6562283520 | bytes 22675456 | tf_op jit(solution)/shard_map/dot_general | solution.py:78
  690.3 62.8 %mlp_back.3 = (f32[192,2560]{1,0:T(8,128)}, f32[1,2560]{1,0:T(1,128)}, bf16[768,2560]{1,0:T(8,128)(2,1)}) custom-call(bf16[768,1664]{1,0:T(8,128)(2,1)} %get-tuple-element.164.gate_ref.gate_own, bf16[768,1664]{1,0:T(8,128)(2,1)} %get-tuple-element.165.up_ref.up_own, bf16[2560,1664]{1,0:T(8,128)(2,1)} %bitcast.116, bf16[2560,1664]{1,0:T(8,128)(2,1)} %bitcast.107, ...), custom_call_target="tpu_custom_call" | custom-call | tf_op jit(solution)/shard_map/mlp_back/pallas_call | solution.py:397
  780.7 19.4 %latent_back.3 = f32[192,1280]{1,0:T(8,128)} custom-call(bf16[768,1280]{1,0:T(8,128)(2,1)} %get-tuple-element.152.gq_ref, bf16[768,1280]{1,0:T(8,128)(2,1)} %get-tuple-element.153.gkv_ref, f32[768,128]{1,0:T(8,128)} %get-tuple-element.154.gsh_ref, bf16[768,1280]{1,0:T(8,128)(2,1)} %copy.116.qup_ref, bf16[256,1280]{1,0:T(8,128)(2,1)} %bitcast.134), custom_call_target="tpu_custom_call" | custom-call | tf_op jit(solution)/shard_map/latent_back/pallas_call | solution.py:397
  844.2 93.2 %recompute.1 = (bf16[3072,1664]{1,0:T(8,128)(2,1)}, bf16[3072,1664]{1,0:T(8,128)(2,1)}, bf16[3072,1664]{1,0:T(8,128)(2,1)}) custom-call(s32[8]{0:T(128)} %and_select_fusion.3.from_ref, s32[8]{0:T(128)} %get-tuple-element.360.own_ref, s32[8]{0:T(128)} %get-tuple-element.359.here_ref, bf16[3072,2560]{1,0:T(8,128)(2,1)} %all-gather.9.cloned.1.call-done.two_ref, ...), custom_call_target="tpu_custom_call" | custom-call | tf_op jit(solution)/shard_map/recompute/pallas_call | solution.py:1201
  943.5 14.2 %fusion.32 = bf16[640,1664]{1,0:T(8,128)(2,1)} fusion(bf16[3072,1664]{1,0:T(8,128)(2,1)} %get-tuple-element.169.gate_ref, bf16[3072,2560]{1,0:T(8,128)(2,1)} %all-gather.9.cloned.1.call-done.two_ref, s32[]{:T(128)S(6)} %select_n.72), kind=kOutput, calls=%fused_computation.50 | convolution fusion | flops 6544179200 | bytes 16285700 | tf_op jit(solution)/shard_map/dot_general | solution.py:74
  996.1 12.2 %fusion.38 = bf16[640,1664]{1,0:T(8,128)(2,1)} fusion(bf16[3072,1664]{1,0:T(8,128)(2,1)} %get-tuple-element.176.up_ref, bf16[3072,2560]{1,0:T(8,128)(2,1)} %all-gather.9.cloned.1.call-done.two_ref, s32[]{:T(128)S(6)} %select_n.72), kind=kOutput, calls=%fused_computation.52 | convolution fusion | flops 6544179200 | bytes 16285700 | tf_op jit(solution)/shard_map/dot_general | solution.py:74
  1008.3 12.2 %fusion.35 = bf16[640,1664]{1,0:T(8,128)(2,1)} fusion(bf16[3072,1664]{1,0:T(8,128)(2,1)} %get-tuple-element.176.up_ref, bf16[3072,2560]{1,0:T(8,128)(2,1)} %all-gather.9.cloned.1.call-done.two_ref, s32[]{:T(128)S(6)} %select_n.69), kind=kOutput, calls=%fused_computation.51 | convolution fusion | flops 6544179200 | bytes 16285700 | tf_op jit(solution)/shard_map/dot_general | solution.py:74
  1020.6 43.8 %chip_gradients.1 = (bf16[2,640,1664]{2,1,0:T(8,128)(2,1)}, bf16[2,640,1664]{2,1,0:T(8,128)(2,1)}) custom-call(s32[2]{0:T(128)} %pad_add_fusion.order_ref, bf16[3072,2560]{1,0:T(8,128)(2,1)} %all-gather.9.cloned.1.call-done.two_ref, bf16[3072,1664]{1,0:T(8,128)(2,1)} %get-tuple-element.169.gate_ref, bf16[3072,1664]{1,0:T(8,128)(2,1)} %get-tuple-element.176.up_ref), custom_call_target="tpu_custom_call" | custom-call | tf_op jit(solution)/shard_map/chip_gradients/pallas_call | solution.py:1134
  1080.7 37.5 %down_gradient.1 = f32[1600,2560]{1,0:T(8,128)} custom-call(bf16[3072,1664]{1,0:T(8,128)(2,1)} %get-tuple-element.181.act_ref, bf16[1536,2560]{1,0:T(8,128)(2,1)} %all-gather.11.cloned.1.call-done.near_ref, bf16[1536,2560]{1,0:T(8,128)(2,1)} %collective-permute-done.1.beside_ref), custom_call_target="tpu_custom_call" | custom-call | tf_op jit(solution)/shard_map/down_gradient/pallas_call | solution.py:1245
  1118.2 12.3 %place_windows.2 = f32[640,6400]{1,0:T(8,128)} custom-call(bf16[640,1664]{1,0:T(8,128)(2,1)} %get-tuple-element.185.refs_0_, bf16[640,1664]{1,0:T(8,128)(2,1)} %collective-permute-done.4.refs_1_, bf16[640,1664]{1,0:T(8,128)(2,1)} %collective-permute-done.2.refs_2_, bf16[640,1664]{1,0:T(8,128)(2,1)} %collective-permute-done.3.refs_3_), custom_call_target="tpu_custom_call" | custom-call | bytes 32768000 | tf_op jit(solution)/shard_map/place_windows/pallas_call | solution.py:1283
  1130.4 15.1 %all-reduce.14.cloned.1.call-done = (bf16[646,1056]{1,0:T(8,128)(2,1)}, bf16[64,5120]{1,0:T(8,128)(2,1)}, bf16[192,3840]{1,0:T(8,128)(2,1)}) async-done(((bf16[646,1056]{1,0:T(8,128)(2,1)}, bf16[64,5120]{1,0:T(8,128)(2,1)}, bf16[192,3840]{1,0:T(8,128)(2,1)}), (bf16[646,1056]{1,0:T(8,128)(2,1)}, bf16[64,5120]{1,0:T(8,128)(2,1)}, bf16[192,3840]{1,0:T(8,128)(2,1)})) %all-reduce.14.cloned.1.call-update) | async-done | bytes 3494288 | tf_op jit(solution)/shard_map/psum | solution.py:1396
  1165.4 12.2 %place_windows.3 = f32[640,6400]{1,0:T(8,128)} custom-call(bf16[640,1664]{1,0:T(8,128)(2,1)} %get-tuple-element.206.refs_0_, bf16[640,1664]{1,0:T(8,128)(2,1)} %collective-permute-done.5.refs_1_, bf16[640,1664]{1,0:T(8,128)(2,1)} %collective-permute-done.6.refs_2_, bf16[640,1664]{1,0:T(8,128)(2,1)} %collective-permute-done.7.refs_3_), custom_call_target="tpu_custom_call" | custom-call | bytes 32768000 | tf_op jit(solution)/shard_map/place_windows/pallas_call | solution.py:1283
  (334 shorter events, 306.2 us)
Async XLA Ops:
  7.2 263.9 %all-gather.5.cloned.1.call-start = ((), (), s32[]{:S(2)}) async-start(), calls=%async_computation.2 | async-start | bytes 4915200 | tf_op jit(solution)/shard_map/all_gather | solution.py:440
  7.2 151.4 %copy-start.53 = (f32[16]{0:T(128)}, f32[16]{0:T(128)S(1)}, u32[]{:S(2)}) copy-start(f32[16]{0:T(128)S(1)} %multiply_exponential_fusion) | copy-start | bytes 196
  8.3 150.4 %copy-start.43 = (f32[192]{0:T(256)}, f32[192]{0:T(256)S(1)}, u32[]{:S(2)}) copy-start(f32[192]{0:T(256)S(1)} %convert_element_type.181) | copy-start | bytes 2308
  10.5 584.3 %copy-start.35 = (f32[768]{0:T(1024)}, f32[768]{0:T(1024)S(1)}, u32[]{:S(2)}) copy-start(f32[768]{0:T(1024)S(1)} %reduce.2) | copy-start | bytes 9220
  11.3 587.5 %copy-start.33 = (f32[2560]{0:T(1024)}, f32[2560]{0:T(1024)S(1)}, u32[]{:S(2)}) copy-start(f32[2560]{0:T(1024)S(1)} %reduce.1) | copy-start | bytes 30724
  14.3 141.9 %copy-start.13 = (bf16[192,2560]{1,0:T(8,128)(2,1)S(1)}, bf16[192,2560]{1,0:T(8,128)(2,1)}, u32[]{:S(2)}) copy-start(bf16[192,2560]{1,0:T(8,128)(2,1)} %param.15) | copy-start | bytes 2949124
  179.9 412.4 %all-gather.7.cloned.1.call-start = ((), (), s32[]{:S(2)}) async-start(), calls=%async_computation.3 | async-start | bytes 9830400 | tf_op jit(solution)/shard_map/all_gather | solution.py:1263
  349.5 24.0 %copy-start.47 = (f32[192]{0:T(256)}, f32[192]{0:T(256)S(1)}, u32[]{:S(2)}) copy-start(f32[192]{0:T(256)S(1)} %get-tuple-element.350) | copy-start | bytes 2308
  447.0 224.9 %all-gather.9.cloned.1.call-start = ((), (), s32[]{:S(2)}) async-start(), calls=%async_computation.4 | async-start | bytes 23592960 | tf_op jit(solution)/shard_map/all_gather | solution.py:1269
  592.5 225.5 %all-gather.11.cloned.1.call-start = ((), (), s32[]{:S(2)}) async-start(), calls=%async_computation.5 | async-start | bytes 9830400 | tf_op jit(solution)/shard_map/all_gather | solution.py:1263
  602.2 37.0 %collective-permute-start = (bf16[192,2560]{1,0:T(8,128)(2,1)}, bf16[192,2560]{1,0:T(8,128)(2,1)}, u32[]{:S(2)}, u32[]{:S(2)}) collective-permute-start(bf16[192,2560]{1,0:T(8,128)(2,1)} %add_convert_fusion), channel_id=1, source_target_pairs={{16,0},{17,1},{18,2},{19,3},{20,4},{21,5},{22,6},{23,7},{24,8},{25... | collective-permute-start | bytes 2949128 | tf_op jit(solution)/shard_map/ppermute | solution.py:1341
  674.9 268.6 %all-reduce.12.cloned.1.call-start = ((), (), s32[]{:S(2)}) async-start(), calls=%async_computation.6 | async-start | bytes 6553600 | tf_op jit(solution)/shard_map/psum | solution.py:1367
  780.6 21.2 %copy-start.42 = (f32[1,256]{1,0:T(1,128)S(1)}, f32[1,256]{1,0:T(1,128)}, u32[]{:S(2)}) copy-start(f32[1,256]{1,0:T(1,128)} %param.19) | copy-start | bytes 3076
  780.6 22.3 %copy-start.36 = (f32[768]{0:T(1024)S(1)}, f32[768]{0:T(1024)}, u32[]{:S(2)}) copy-start(f32[768]{0:T(1024)} %copy-done.35) | copy-start | bytes 9220
  817.9 26.2 %collective-permute-start.1 = (bf16[1536,2560]{1,0:T(8,128)(2,1)}, bf16[1536,2560]{1,0:T(8,128)(2,1)}, u32[]{:S(2)}, u32[]{:S(2)}) collective-permute-start(bf16[1536,2560]{1,0:T(8,128)(2,1)} %all-gather.11.cloned.1.call-done.near_ref), channel_id=1, source_target_pairs={{0,1},{1,0},{2,3},{3,2},{4,5},{5,4},{6,7},{7,6},{8,9},{9,8},{10,11... | collective-permute-start | bytes 23592968 | tf_op jit(solution)/shard_map/ppermute | solution.py:1068
  819.5 17.2 %all-to-all-start = ((bf16[4,192,640]{2,1,0:T(8,128)(2,1)}), bf16[4,192,640]{2,1,0:T(8,128)(2,1)}, u32[]{:S(2)}, u32[]{:S(2)}) async-start(bf16[4,192,640]{2,1,0:T(8,128)(2,1)} %bitcast.147), calls=%async_computation | async-start | bytes 1966080 | tf_op jit(solution)/shard_map/all_to_all | solution.py:1358
  836.7 132.0 %all-to-all-start.1 = ((bf16[4,464,1280]{2,1,0:T(8,128)(2,1)}), bf16[4,464,1280]{2,1,0:T(8,128)(2,1)}, u32[]{:S(2)}, u32[]{:S(2)}) async-start(bf16[4,464,1280]{2,1,0:T(8,128)(2,1)} %pad_maximum_fusion), calls=%async_computation.1 | async-start | bytes 9502720 | tf_op jit(solution)/shard_map/all_to_all | solution.py:917
  842.6 302.9 %all-reduce.14.cloned.1.call-start = ((), (), s32[]{:S(2)}) async-start(), calls=%async_computation.7 | async-start | bytes 7245824 | tf_op jit(solution)/shard_map/psum | solution.py:1396
  975.1 94.0 %collective-permute-start.2 = (bf16[640,1664]{1,0:T(8,128)(2,1)}, bf16[640,1664]{1,0:T(8,128)(2,1)}, u32[]{:S(2)}, u32[]{:S(2)}) collective-permute-start(bf16[640,1664]{1,0:T(8,128)(2,1)} %fusion.29), channel_id=1, source_target_pairs={{0,2},{1,3},{2,0},{3,1},{4,6},{5,7},{6,4},{7,5},{8,10},{9,11},{10,... | collective-permute-start | bytes 6389768 | tf_op jit(solution)/shard_map/ppermute | solution.py:1068
  976.4 93.0 %collective-permute-start.3 = (bf16[640,1664]{1,0:T(8,128)(2,1)}, bf16[640,1664]{1,0:T(8,128)(2,1)}, u32[]{:S(2)}, u32[]{:S(2)}) collective-permute-start(bf16[640,1664]{1,0:T(8,128)(2,1)} %fusion.32), channel_id=1, source_target_pairs={{0,3},{1,2},{2,1},{3,0},{4,7},{5,6},{6,5},{7,4},{8,11},{9,10},{10,... | collective-permute-start | bytes 6389768 | tf_op jit(solution)/shard_map/ppermute | solution.py:1068
  1069.4 48.7 %collective-permute-start.4 = (bf16[640,1664]{1,0:T(8,128)(2,1)}, bf16[640,1664]{1,0:T(8,128)(2,1)}, u32[]{:S(2)}, u32[]{:S(2)}) collective-permute-start(bf16[640,1664]{1,0:T(8,128)(2,1)} %get-tuple-element.182), channel_id=1, source_target_pairs={{0,1},{1,0},{2,3},{3,2},{4,5},{5,4},{6,7},{7,6},{8,9},{9,8},{10,11... | collective-permute-start | bytes 6389768 | tf_op jit(solution)/shard_map/ppermute | solution.py:1068
  1071.4 85.4 %collective-permute-start.6 = (bf16[640,1664]{1,0:T(8,128)(2,1)}, bf16[640,1664]{1,0:T(8,128)(2,1)}, u32[]{:S(2)}, u32[]{:S(2)}) collective-permute-start(bf16[640,1664]{1,0:T(8,128)(2,1)} %fusion.35), channel_id=1, source_target_pairs={{0,2},{1,3},{2,0},{3,1},{4,6},{5,7},{6,4},{7,5},{8,10},{9,11},{10,... | collective-permute-start | bytes 6389768 | tf_op jit(solution)/shard_map/ppermute | solution.py:1068
  1072.7 92.7 %collective-permute-start.7 = (bf16[640,1664]{1,0:T(8,128)(2,1)}, bf16[640,1664]{1,0:T(8,128)(2,1)}, u32[]{:S(2)}, u32[]{:S(2)}) collective-permute-start(bf16[640,1664]{1,0:T(8,128)(2,1)} %fusion.38), channel_id=1, source_target_pairs={{0,3},{1,2},{2,1},{3,0},{4,7},{5,6},{6,5},{7,4},{8,11},{9,10},{10,... | collective-permute-start | bytes 6389768 | tf_op jit(solution)/shard_map/ppermute | solution.py:1068
  1076.0 80.8 %collective-permute-start.5 = (bf16[640,1664]{1,0:T(8,128)(2,1)}, bf16[640,1664]{1,0:T(8,128)(2,1)}, u32[]{:S(2)}, u32[]{:S(2)}) collective-permute-start(bf16[640,1664]{1,0:T(8,128)(2,1)} %get-tuple-element.324), channel_id=1, source_target_pairs={{0,1},{1,0},{2,3},{3,2},{4,5},{5,4},{6,7},{7,6},{8,9},{9,8},{10,11... | collective-permute-start | bytes 6389768 | tf_op jit(solution)/shard_map/ppermute | solution.py:1068
  (62 other events, 311.1 us)
Sparse Core Ops, SparseCore 0:
  180.1 35.1 all-gather.4
  447.2 140.4 all-gather.6
  592.6 30.0 all-gather.8
  675.1 142.8 all-gather.10
  820.2 123.2 all-reduce.11
  1008.5 137.0 all-reduce.13
